TPU v7x, 32 devices: a whole 2x2x4 slice. The times are simulated.
32 devices in a mesh: dp: 8 (over z, x), tensor: 4 (over y, core).
Axes of the slice: x: 2, y: 2, z: 4, core: 2. Of those that a mesh axis runs over, the one named last changes fastest.
Arguments:
- rollout_states: bfloat16 [8192, 8192], P('dp', 'tensor'), may hold values from -6 to 6
- norm_gain: float32 [8192], replicated, may hold values from 0.1 to 1.9
- w_query: bfloat16 [8192, 4096], P('dp', 'tensor'), as said below
- w_key: bfloat16 [8192, 512], P('dp', 'tensor'), as said below
- w_value: bfloat16 [8192, 512], P('dp', 'tensor'), may hold values from -0.0625 to 0.0625
- b_query: float32 [4096], P('tensor'), may hold values from -3 to 3
- b_key: float32 [512], P('tensor'), may hold values from -3 to 3
- b_value: float32 [512], P('tensor'), may hold values from -3 to 3
- seq_lengths: int32 [64], replicated, may hold values from 1 to 255, as said below
- seq_dest: int32 [64], replicated, may hold values from 0 to 7, as said below
- seq_offset: int32 [64], replicated, may hold values from 0 to 1023, as said below
Outputs:
- context: bfloat16 [8192, 4096], P('dp', 'tensor')
Inputs may be any that keep to these rules, and one draw needn't show every extreme that they name: `seq_lengths`: the 8 responses r * 8 to r * 8 + 7 lie in this order in rollout device r's 1024 rows and fill them; some response has exactly 255 tokens. `seq_dest`: the responses of one rollout device go to 8 different learners, so every learner receives exactly one response from every rollout device. `seq_offset`: the responses of one learner occupy disjoint runs of rows that together cover its 1024 rows. `w_query`: A weight matrix. `w_key`: A weight matrix.
All inputs are finite; a program needn't handle non-finite values.
Results may differ from a plain program's by a relative error of at most 0.012.
The roundings to bfloat16 on the way count: a program that leaves them out, or rounds other values in their place, can miss the bound.
Values may be sent and summed in bfloat16 or wider, within the bound.
No kernel may reach another device: no remote copies, remote signals or barrier semaphores. Data moves between devices by JAX's collectives and lax.ppermute only.
A program may use at most 128 MiB of HBM per device.

v0:
```python
import jax
import jax.numpy as jnp
from jax import lax
from jax.sharding import PartitionSpec as P

HD = 128


rope_base = 1000000.0
norm_eps = 1e-06


def rope_tables(positions):
    half_dim = HD // 2
    frequency = rope_base ** (-(jnp.arange(half_dim).astype(jnp.float32) * 2.0 / HD))
    angles = positions.astype(jnp.float32)[:, None] * frequency[None, :]
    return (jnp.cos(angles), jnp.sin(angles))


def rotate(states, cosine, sine):
    half_dim = states.shape[-1] // 2
    first_half = states[..., :half_dim]
    second_half = states[..., half_dim:]
    cos_wide = cosine[:, None, :]
    sin_wide = sine[:, None, :]
    return jnp.concatenate(
        [
            first_half * cos_wide - second_half * sin_wide,
            second_half * cos_wide + first_half * sin_wide,
        ],
        axis=-1,
    )


def local(
    rollout_states,
    norm_gain,
    w_query,
    w_key,
    w_value,
    b_query,
    b_key,
    b_value,
    seq_lengths,
    seq_dest,
    seq_offset,
):
    learners = lax.axis_size("dp")
    own_index = lax.axis_index("dp")
    row_count, feature_count = rollout_states.shape
    capacity = 2 * row_count // learners - 1
    lengths = seq_lengths.reshape(learners, learners)
    dests = seq_dest.reshape(learners, learners)
    offsets = seq_offset.reshape(learners, learners)
    starts = jnp.cumsum(lengths, axis=1) - lengths
    peer_ids = jnp.arange(learners, dtype=jnp.int32)
    own_length = lax.dynamic_index_in_dim(lengths, own_index, 0, keepdims=False)
    own_start = lax.dynamic_index_in_dim(starts, own_index, 0, keepdims=False)
    own_dest = lax.dynamic_index_in_dim(dests, own_index, 0, keepdims=False)
    match_send = (own_dest[None, :] == peer_ids[:, None]).astype(jnp.int32)
    send_start = jnp.sum(match_send * own_start[None, :], axis=1)
    send_length = jnp.sum(match_send * own_length[None, :], axis=1)
    slot_index = jnp.arange(capacity, dtype=jnp.int32)
    pick_rows = send_start[:, None] + slot_index[None, :]
    padded = jnp.concatenate(
        [rollout_states, jnp.zeros((capacity, feature_count), rollout_states.dtype)], axis=0
    )
    live_slots = (slot_index[None, :] < send_length[:, None])[..., None]
    outgoing = jnp.where(
        live_slots, jnp.take(padded, pick_rows, axis=0), jnp.zeros((), rollout_states.dtype)
    )
    incoming = lax.all_to_all(outgoing, "dp", split_axis=0, concat_axis=0, tiled=True)
    matched = (dests == own_index).astype(jnp.int32)
    run_start = jnp.sum(matched * offsets, axis=1)
    run_length = jnp.sum(matched * lengths, axis=1)
    rows = jnp.arange(row_count, dtype=jnp.int32)
    inside = (
        (rows[:, None] >= run_start[None, :]) & (rows[:, None] < (run_start + run_length)[None, :])
    ).astype(jnp.int32)
    source_ids = jnp.sum(inside * peer_ids[None, :], axis=1)
    within_seq = rows - jnp.sum(inside * run_start[None, :], axis=1)
    arrived = jnp.take(
        incoming.reshape(learners * capacity, feature_count),
        source_ids * capacity + within_seq,
        axis=0,
    )
    gathered = lax.all_gather(arrived, "tensor", axis=1, tiled=True)
    widened = gathered.astype(jnp.float32)
    statistic = jnp.mean(widened * widened, axis=-1, keepdims=True)
    normed = (widened * lax.rsqrt(statistic + norm_eps) * norm_gain[None, :]).astype(jnp.bfloat16)
    full_query, full_key, full_value = (
        lax.all_gather(w_query, "dp", axis=0, tiled=True),
        lax.all_gather(w_key, "dp", axis=0, tiled=True),
        lax.all_gather(w_value, "dp", axis=0, tiled=True),
    )
    query = jnp.dot(normed, full_query, preferred_element_type=jnp.float32)
    key = jnp.dot(normed, full_key, preferred_element_type=jnp.float32)
    value = jnp.dot(normed, full_value, preferred_element_type=jnp.float32)
    query = query + b_query[None, :]
    key = key + b_key[None, :]
    value = value + b_value[None, :]
    heads_here = query.shape[1] // HD
    kv_here = key.shape[1] // HD
    group = heads_here // kv_here
    cosine, sine = rope_tables(within_seq)
    rot_query = rotate(query.reshape(row_count, heads_here, HD), cosine, sine).astype(jnp.bfloat16)
    rot_query = rot_query.reshape(row_count, kv_here, group, HD)
    rot_key = rotate(key.reshape(row_count, kv_here, HD), cosine, sine).astype(jnp.bfloat16)
    value_bf = value.reshape(row_count, kv_here, HD).astype(jnp.bfloat16)
    block_rows = min(512, row_count)

    def one_block(block_number):
        first_row = block_number * block_rows
        query_block = lax.dynamic_slice_in_dim(rot_query, first_row, block_rows, 0)
        query_source = lax.dynamic_slice_in_dim(source_ids, first_row, block_rows, 0)
        query_rows = first_row + jnp.arange(block_rows, dtype=jnp.int32)
        scores = jnp.einsum(
            "bcgd,kcd->cgbk", query_block, rot_key, preferred_element_type=jnp.float32
        )
        scores = scores * HD ** (-0.5)
        allowed = (source_ids[None, :] == query_source[:, None]) & (
            rows[None, :] <= query_rows[:, None]
        )
        scores = jnp.where(allowed[None, None], scores, -1e30)
        peak = jnp.max(scores, axis=-1, keepdims=True)
        raised = jnp.exp(scores - peak)
        weights = (raised / jnp.sum(raised, axis=-1, keepdims=True)).astype(jnp.bfloat16)
        context = jnp.einsum(
            "cgbk,kcd->bcgd", weights, value_bf, preferred_element_type=jnp.float32
        )
        return context.astype(jnp.bfloat16).reshape(block_rows, heads_here * HD)

    outputs = lax.map(one_block, jnp.arange(row_count // block_rows, dtype=jnp.int32))
    return outputs.reshape(row_count, heads_here * HD)


def solution(mesh):
    placed = (
        P("dp", "tensor"),
        P(),
        P("dp", "tensor"),
        P("dp", "tensor"),
        P("dp", "tensor"),
        P("tensor"),
        P("tensor"),
        P("tensor"),
        P(),
        P(),
        P(),
    )
    return jax.shard_map(
        local, mesh=mesh, in_specs=placed, out_specs=P("dp", "tensor"), check_vma=False
    )
```

profile of v0, /device:TPU:0, one launch (start us, length us, event | category | flops | bytes accessed | tf_op | source)
XLA Modules:
  0.0 787.6 jit_solution(3632999396764079081)
XLA Ops:
  9.5 5.3 concatenate.30
  14.8 19.5 %gather_fusion = bf16[2040,2048]{1,0:T(8,128)(2,1)} fusion(bf16[1279,2048]{1,0:T(8,128)(2,1)} %concatenate.30, s32[2048]{0:T(1024)S(1)} %pad_clamp_fusion), kind=kCustom, calls=%fused_computation | custom fusion | bytes 16719840 | tf_op jit(solution)/shard_map/jit(_take)/gather | solution.py:70
  34.3 9.0 %reshape.423 = bf16[8,255,2048]{2,1,0:T(8,128)(2,1)} reshape(bf16[2040,2048]{1,0:T(8,128)(2,1)} %gather_fusion) | data formatting | bytes 16711680 | tf_op jit(solution)/shard_map/jit(_take)/gather | solution.py:70
  43.4 7.4 select_select_fusion
  50.8 7.3 all-to-all-start
  58.2 183.0 %all-to-all-done = bf16[8,255,2048]{2,1,0:T(8,128)(2,1)} async-done(((bf16[8,255,2048]{2,1,0:T(8,128)(2,1)}), bf16[8,255,2048]{2,1,0:T(8,128)(2,1)}, u32[]{:S(2)}, u32[]{:S(2)}) %all-to-all-start) | async-done | bytes 8355872 | tf_op jit(solution)/shard_map/all_to_all | solution.py:72
  241.2 9.0 %reshape.418 = bf16[2040,2048]{1,0:T(8,128)(2,1)} reshape(bf16[8,255,2048]{2,1,0:T(8,128)(2,1)} %all-to-all-done) | data formatting | bytes 16711680 | tf_op jit(solution)/shard_map/reshape | solution.py:83
  250.2 13.3 %gather_fusion.1 = bf16[1024,2048]{1,0:T(8,128)(2,1)} fusion(bf16[2040,2048]{1,0:T(8,128)(2,1)} %reshape.418, s32[1024]{0:T(1024)S(1)} %broadcast_clamp_fusion), kind=kCustom, calls=%fused_computation.1 | custom fusion | bytes 8392704 | tf_op jit(solution)/shard_map/jit(_take)/gather | solution.py:82
  263.5 4.7 broadcast_select_fusion
  270.3 1.9 multiply_cosine_fusion
  272.2 101.2 %all-gather.5.cloned.1.call-done = bf16[1024,8192]{1,0:T(8,128)(2,1)} async-done(((bf16[1024,2048]{1,0:T(8,128)(2,1)}), bf16[1024,8192]{1,0:T(8,128)(2,1)}) %all-gather.5.cloned.1.call-update) | async-done | bytes 16777232 | tf_op jit(solution)/shard_map/all_gather | solution.py:87
  373.4 7.2 fusion.18
  380.6 44.2 %all-gather.11.cloned.1.call-done = bf16[8192,128]{1,0:T(8,128)(2,1)} async-done(((bf16[1024,128]{1,0:T(8,128)(2,1)}), bf16[8192,128]{1,0:T(8,128)(2,1)}) %all-gather.11.cloned.1.call-update) | async-done | bytes 2097168 | tf_op jit(solution)/shard_map/all_gather | solution.py:94
  424.8 11.0 %fusion.25 = bf16[1024,1,128]{2,0,1:T(8,128)(2,1)S(1)} fusion(bf16[8192,128]{1,0:T(8,128)(2,1)} %all-gather.11.cloned.1.call-done, f32[128]{0:T(128)S(1)} %copy-done.2, bf16[1024,8192]{1,0:T(8,128)(2,1)} %all-gather.5.cloned.1.call-done, f32[8192]{0:T(1024)S(1)} %copy-done, f32[1024]{0:T(1024)S(1)} %add_rsqrt_fusion), kind=kOutput, calls=%fused_computation.40 | convolution fusion | flops 2181300224 | bytes 19173888 | tf_op jit(solution)/shard_map/dot_general | solution.py:98
  436.7 38.1 %all-gather.9.cloned.1.call-done = bf16[8192,128]{1,0:T(8,128)(2,1)} async-done(((bf16[1024,128]{1,0:T(8,128)(2,1)}), bf16[8192,128]{1,0:T(8,128)(2,1)}) %all-gather.9.cloned.1.call-update) | async-done | bytes 2097168 | tf_op jit(solution)/shard_map/all_gather | solution.py:93
  474.8 10.3 %fusion.24 = f32[1024,1,128]{0,2,1:T(8,128)S(1)} fusion(bf16[8192,128]{1,0:T(8,128)(2,1)} %all-gather.9.cloned.1.call-done, f32[128]{0:T(128)S(1)} %copy-done.3, bf16[1024,8192]{1,0:T(8,128)(2,1)} %all-gather.5.cloned.1.call-done, f32[8192]{0:T(1024)S(1)} %copy-done, f32[1024]{0:T(1024)S(1)} %add_rsqrt_fusion), kind=kOutput, calls=%fused_computation.39 | convolution fusion | flops 2181169152 | bytes 19436032 | tf_op jit(solution)/shard_map/dot_general | solution.py:97
  485.0 1.2 fusion.31
  486.4 216.5 %all-gather.7.cloned.1.call-done = bf16[8192,1024]{1,0:T(8,128)(2,1)} async-done(((bf16[1024,1024]{1,0:T(8,128)(2,1)}), bf16[8192,1024]{1,0:T(8,128)(2,1)}) %all-gather.7.cloned.1.call-update) | async-done | bytes 16777232 | tf_op jit(solution)/shard_map/all_gather | solution.py:92
  702.9 24.4 %convolution_add_fusion = f32[1024,1024]{0,1:T(8,128)S(1)} fusion(bf16[8192,1024]{1,0:T(8,128)(2,1)} %all-gather.7.cloned.1.call-done, f32[1024]{0:T(1024)S(1)} %copy-done.1, bf16[1024,8192]{1,0:T(8,128)(2,1)} %all-gather.5.cloned.1.call-done, f32[8192]{0:T(1024)S(1)} %copy-done, f32[1024]{0:T(1024)S(1)} %add_rsqrt_fusion), kind=kOutput, calls=%fused_computation.32 | convolution fusion | flops 17214472192 | bytes 37789696 | tf_op jit(solution)/shard_map/dot_general | solution.py:96
  727.3 1.7 fusion.45
  729.0 3.8 copy.29
  732.8 2.7 copy.30
  735.5 4.6 fusion.21
  740.1 2.5 pad_maximum_fusion
  742.6 38.5 %while.11 = (s32[]{:T(128)}, bf16[2,512,1024]{2,1,0:T(8,128)(2,1)}, s32[1024]{0:T(1024)S(1)}, s32[2]{0:T(128)S(1)}, bf16[1024,1,8,128]{3,0,2,1:T(8,128)(2,1)}, /...) while((s32[]{:T(128)}, bf16[2,512,1024]{2,1,0:T(8,128)(2,1)}, ...), condition=%wide.region_11.12_spmd.clone, body=%wide.region_8.11_spmd.clone.sunk | while | flops 2199904768 | bytes 59341488 | solution.py:133
  744.6 4.4 fusion.58
  749.0 4.5 fusion.59
  753.5 6.8 fusion.60
  760.8 1.0 constant_dynamic-update-slice_fusion.2
  763.8 4.4 fusion.58
  768.2 4.5 fusion.59
  772.7 6.8 fusion.60
  (54 shorter events, 11.0 us)
Async XLA Ops:
  50.8 190.4 %all-to-all-start = ((bf16[8,255,2048]{2,1,0:T(8,128)(2,1)}), bf16[8,255,2048]{2,1,0:T(8,128)(2,1)}, u32[]{:S(2)}, u32[]{:S(2)}) async-start(bf16[8,255,2048]{2,1,0:T(8,128)(2,1)} %select_select_fusion), calls=%async_computation | async-start | bytes 16777216 | tf_op jit(solution)/shard_map/all_to_all | solution.py:72
  58.0 315.3 %all-gather.5.cloned.1.call-start = ((), (), s32[]{:S(2)}) async-start(), calls=%async_computation.1 | async-start | bytes 20971520 | tf_op jit(solution)/shard_map/all_gather | solution.py:87
  268.2 156.6 %all-gather.11.cloned.1.call-start = ((), (), s32[]{:S(2)}) async-start(), calls=%async_computation.4 | async-start | bytes 2359296 | tf_op jit(solution)/shard_map/all_gather | solution.py:94
  268.9 205.8 %all-gather.9.cloned.1.call-start = ((), (), s32[]{:S(2)}) async-start(), calls=%async_computation.3 | async-start | bytes 2359296 | tf_op jit(solution)/shard_map/all_gather | solution.py:93
  269.7 433.2 %all-gather.7.cloned.1.call-start = ((), (), s32[]{:S(2)}) async-start(), calls=%async_computation.2 | async-start | bytes 18874368 | tf_op jit(solution)/shard_map/all_gather | solution.py:92
  272.2 152.6 %copy-start = (f32[8192]{0:T(1024)S(1)}, f32[8192]{0:T(1024)}, u32[]{:S(2)}) copy-start(f32[8192]{0:T(1024)} %param.14) | copy-start | bytes 98308
  272.2 152.6 %copy-start.2 = (f32[128]{0:T(128)S(1)}, f32[128]{0:T(128)}, u32[]{:S(2)}) copy-start(f32[128]{0:T(128)} %param.20) | copy-start | bytes 1540
  380.6 94.2 %copy-start.3 = (f32[128]{0:T(128)S(1)}, f32[128]{0:T(128)}, u32[]{:S(2)}) copy-start(f32[128]{0:T(128)} %param.19) | copy-start | bytes 1540
  436.7 266.2 %copy-start.1 = (f32[1024]{0:T(1024)S(1)}, f32[1024]{0:T(1024)}, u32[]{:S(2)}) copy-start(f32[1024]{0:T(1024)} %param.18) | copy-start | bytes 12292
Sparse Core Ops, SparseCore 0:
  268.3 105.0 all-gather.4
  375.5 49.2 all-gather.10
  426.9 47.7 all-gather.8
  476.7 226.0 all-gather.6
where the time goes:
time: 788 us
  waiting for transfers between devices  585 us (74%)
  local copies, waits for them, and re-layouts  72.3 us (9%)
  matrix products  68 us (9%)
  other arithmetic  40.4 us (5%)
  between operations  13.3 us (2%)
    all_gather x1, waiting for transfers between devices, local(): lax.all_gather(w_query, 'dp', axis=0, tiled=True)  216 us
    all_to_all x1, waiting for transfers between devices, local(): lax.all_to_all(outgoing, 'dp', split_axis=0, concat_axis=0, tiled=True)  183 us
    all_gather x1, waiting for transfers between devices, local(): gathered = lax.all_gather(arrived, 'tensor', axis=1, tiled=True)  101 us
    all_gather x1, waiting for transfers between devices, local(): lax.all_gather(w_value, 'dp', axis=0, tiled=True)  44.2 us
    all_gather x1, waiting for transfers between devices, local(): lax.all_gather(w_key, 'dp', axis=0, tiled=True)  38.1 us
    gather x2, local copies, waits for them, and re-layouts, local(): jnp.take(padded, pick_rows, axis=0)  28.5 us
    dot_general x1, matrix products, local(): query = jnp.dot(normed, full_query, preferred_element_type=jnp.float32)  24.4 us
  transfers between devices with their start and end apart: 5, of which 5 were waited for; matrix products, arithmetic and copies ran while one was open for 4% of the time, Pallas kernels for 0%

commit v1 on v0

--- a/solution.py
+++ b/solution.py
@@ -1,13 +1,17 @@
+import functools
+
 import jax
 import jax.numpy as jnp
 from jax import lax
+from jax.experimental import pallas as pl
+from jax.experimental.pallas import tpu as pltpu
 from jax.sharding import PartitionSpec as P
 
 HD = 128
-
 
 rope_base = 1000000.0
 norm_eps = 1e-06
+mask_value = -1e30
 
 
 def rope_tables(positions):
@@ -32,7 +36,7 @@
     )
 
 
-def local(
+def local_any(
     rollout_states,
     norm_gain,
     w_query,
@@ -121,7 +125,7 @@
         allowed = (source_ids[None, :] == query_source[:, None]) & (
             rows[None, :] <= query_rows[:, None]
         )
-        scores = jnp.where(allowed[None, None], scores, -1e30)
+        scores = jnp.where(allowed[None, None], scores, mask_value)
         peak = jnp.max(scores, axis=-1, keepdims=True)
         raised = jnp.exp(scores - peak)
         weights = (raised / jnp.sum(raised, axis=-1, keepdims=True)).astype(jnp.bfloat16)
@@ -132,6 +136,329 @@
 
     outputs = lax.map(one_block, jnp.arange(row_count // block_rows, dtype=jnp.int32))
     return outputs.reshape(row_count, heads_here * HD)
+
+
+def project_kernel(chunks, off_ref, *refs):
+    x_refs = refs[:4]
+    w_refs = refs[4 : 4 + 7 * chunks]
+    bias_ref, cos_ref, sin_ref, out_ref, w_buf, sems = refs[4 + 7 * chunks :]
+
+    @pl.when(pl.program_id(0) == 0)
+    def _():
+        for i in range(4):
+            for c in range(chunks):
+                for place in range(7):
+
+                    @pl.when(off_ref[i] == place - 3)
+                    def _(i=i, c=c, place=place):
+                        pltpu.make_async_copy(
+                            w_refs[7 * c + place],
+                            w_buf.at[i, :, pl.ds(c * HD, HD)],
+                            sems.at[i, c],
+                        ).start()
+
+        for i in range(4):
+            for c in range(chunks):
+                pltpu.make_async_copy(
+                    w_refs[7 * c], w_buf.at[i, :, pl.ds(c * HD, HD)], sems.at[i, c]
+                ).wait()
+
+    total = jnp.dot(x_refs[0][...], w_buf[0], preferred_element_type=jnp.float32)
+    for i in range(1, 4):
+        total += jnp.dot(x_refs[i][...], w_buf[i], preferred_element_type=jnp.float32)
+    for c in range(chunks):
+        part = total[:, c * HD : (c + 1) * HD] + bias_ref[:, c * HD : (c + 1) * HD]
+        rot = part * cos_ref[c] + pltpu.roll(part, HD // 2, 1) * sin_ref[c]
+        out_ref[:, c * HD : (c + 1) * HD] = rot.astype(out_ref.dtype)
+
+
+def project(off, x_blocks, w_places, bias, cos, sin):
+    chunks = len(w_places)
+    rows, feats = x_blocks[0].shape
+    tile = min(256, rows)
+    flat = [w for places in w_places for w in places]
+    grid_spec = pltpu.PrefetchScalarGridSpec(
+        num_scalar_prefetch=1,
+        grid=(rows // tile,),
+        in_specs=[pl.BlockSpec((tile, feats), lambda r, off: (r, 0))] * 4
+        + [pl.BlockSpec(memory_space=pl.ANY)] * len(flat)
+        + [
+            pl.BlockSpec((1, chunks * HD), lambda r, off: (0, 0)),
+            pl.BlockSpec((chunks, tile, HD), lambda r, off: (0, r, 0)),
+            pl.BlockSpec((chunks, tile, HD), lambda r, off: (0, r, 0)),
+        ],
+        out_specs=pl.BlockSpec((tile, chunks * HD), lambda r, off: (r, 0)),
+        scratch_shapes=[
+            pltpu.VMEM((4, feats, chunks * HD), jnp.bfloat16),
+            pltpu.SemaphoreType.DMA((4, chunks)),
+        ],
+    )
+    return pl.pallas_call(
+        functools.partial(project_kernel, chunks),
+        grid_spec=grid_spec,
+        out_shape=jax.ShapeDtypeStruct((rows, chunks * HD), jnp.bfloat16),
+        compiler_params=pltpu.CompilerParams(vmem_limit_bytes=40 * 2**20),
+        cost_estimate=pl.CostEstimate(
+            flops=2 * rows * 4 * feats * chunks * HD,
+            bytes_accessed=8 * rows * feats + 8 * feats * chunks * HD,
+            transcendentals=0,
+        ),
+    )(off, *x_blocks, *flat, bias, cos, sin)
+
+
+def attend_kernel(heads, slot, window, start_ref, len_ref, q_ref, k_ref, v_ref, out_ref):
+    which = pl.program_id(0)
+    rows = q_ref.shape[0]
+    start = start_ref[which]
+    first = pl.multiple_of(jnp.minimum((start // 16) * 16, rows - window), 16)
+    row_at = lax.broadcasted_iota(jnp.int32, (slot, window), 0)
+    col_at = lax.broadcasted_iota(jnp.int32, (slot, window), 1)
+    pick = jnp.where(
+        (col_at == row_at + (start - first)) & (row_at < len_ref[which]), 1.0, 0.0
+    ).astype(jnp.bfloat16)
+
+    def picked(ref, lanes):
+        rows_here = ref[pl.ds(first, window), lanes]
+        return jnp.dot(pick, rows_here, preferred_element_type=jnp.float32).astype(jnp.bfloat16)
+
+    key = picked(k_ref, pl.ds(0, HD))
+    value = picked(v_ref, pl.ds(0, HD))
+    causal = lax.broadcasted_iota(jnp.int32, (slot, slot), 1) <= lax.broadcasted_iota(
+        jnp.int32, (slot, slot), 0
+    )
+    for h in range(heads):
+        query = picked(q_ref, pl.ds(h * HD, HD))
+        scores = lax.dot_general(
+            query, key, (((1,), (1,)), ((), ())), preferred_element_type=jnp.float32
+        )
+        scores = jnp.where(causal, scores * HD ** (-0.5), mask_value)
+        peak = jnp.max(scores, axis=-1, keepdims=True)
+        raised = jnp.exp(scores - peak)
+        weights = (raised / jnp.sum(raised, axis=-1, keepdims=True)).astype(jnp.bfloat16)
+        context = jnp.dot(weights, value, preferred_element_type=jnp.float32)
+        out_ref[0, :, h * HD : (h + 1) * HD] = context.astype(out_ref.dtype)
+
+
+def attend(starts, lens, query, key, value, slot):
+    rows, columns = query.shape
+    count = starts.shape[0]
+    window = min(rows, -(-(slot + 16) // 128) * 128)
+    heads = columns // HD
+    grid_spec = pltpu.PrefetchScalarGridSpec(
+        num_scalar_prefetch=2,
+        grid=(count,),
+        in_specs=[
+            pl.BlockSpec((rows, columns), lambda s, a, b: (0, 0)),
+            pl.BlockSpec((rows, HD), lambda s, a, b: (0, 0)),
+            pl.BlockSpec((rows, HD), lambda s, a, b: (0, 0)),
+        ],
+        out_specs=pl.BlockSpec((1, slot, columns), lambda s, a, b: (s, 0, 0)),
+    )
+    return pl.pallas_call(
+        functools.partial(attend_kernel, heads, slot, window),
+        grid_spec=grid_spec,
+        out_shape=jax.ShapeDtypeStruct((count, slot, columns), jnp.bfloat16),
+        compiler_params=pltpu.CompilerParams(vmem_limit_bytes=32 * 2**20),
+        cost_estimate=pl.CostEstimate(
+            flops=2 * count * slot * (2 * slot + window) * columns,
+            bytes_accessed=2 * (rows * (columns + 2 * HD) + count * slot * columns),
+            transcendentals=count * heads * slot * slot,
+        ),
+    )(starts, lens, query, key, value)
+
+
+def place_kernel(count, slot, window, start_ref, len_ref, in_ref, out_ref, total):
+    learner = pl.program_id(0)
+    rows = total.shape[0]
+    total[...] = jnp.zeros_like(total)
+    row_at = lax.broadcasted_iota(jnp.int32, (window, slot), 0)
+    col_at = lax.broadcasted_iota(jnp.int32, (window, slot), 1)
+    for s in range(count):
+        start = start_ref[learner, s]
+        first = pl.multiple_of(jnp.minimum((start // 8) * 8, rows - window), 8)
+        pick = jnp.where(
+            (row_at == col_at + (start - first)) & (col_at < len_ref[learner, s]), 1.0, 0.0
+        ).astype(jnp.bfloat16)
+        total[pl.ds(first, window), :] += jnp.dot(
+            pick, in_ref[s, 0], preferred_element_type=jnp.float32
+        )
+    out_ref[0] = total[...].astype(out_ref.dtype)
+
+
+def place(starts, lens, slots, rows):
+    count, learners, slot, columns = slots.shape
+    window = min(rows, slot + 8)
+    grid_spec = pltpu.PrefetchScalarGridSpec(
+        num_scalar_prefetch=2,
+        grid=(learners,),
+        in_specs=[pl.BlockSpec((count, 1, slot, columns), lambda r, a, b: (0, r, 0, 0))],
+        out_specs=pl.BlockSpec((1, rows, columns), lambda r, a, b: (r, 0, 0)),
+        scratch_shapes=[pltpu.VMEM((rows, columns), jnp.float32)],
+    )
+    return pl.pallas_call(
+        functools.partial(place_kernel, count, slot, window),
+        grid_spec=grid_spec,
+        out_shape=jax.ShapeDtypeStruct((learners, rows, columns), jnp.bfloat16),
+        compiler_params=pltpu.CompilerParams(vmem_limit_bytes=32 * 2**20),
+        cost_estimate=pl.CostEstimate(
+            flops=2 * learners * count * slot * window * columns,
+            bytes_accessed=2 * learners * columns * (count * slot + rows),
+            transcendentals=0,
+        ),
+    )(starts, lens, slots)
+
+
+def local_line(
+    rollout_states,
+    norm_gain,
+    w_query,
+    w_key,
+    w_value,
+    b_query,
+    b_key,
+    b_value,
+    seq_lengths,
+    seq_dest,
+    seq_offset,
+):
+    learners = lax.axis_size("dp")
+    line = learners // 2
+    me = lax.axis_index("dp")
+    z, x = me // 2, me % 2
+    t = lax.axis_index("tensor")
+    row_count, feature_count = rollout_states.shape
+    slot = 2 * row_count // learners
+    half = w_query.shape[1] // 2
+    heads = half // HD
+
+    def swap_x(array):
+        return lax.ppermute(array, "dp", [(i, i ^ 1) for i in range(learners)])
+
+    def swap_y(array):
+        return lax.ppermute(array, "tensor", [(i, i ^ 2) for i in range(4)])
+
+    def swap_core(array):
+        return lax.ppermute(array, "tensor", [(i, i ^ 1) for i in range(4)])
+
+    def up(array, first):
+        return lax.ppermute(array, "dp", [(i, i + 2) for i in range(2 * first, learners - 2)])
+
+    def down(array, first):
+        return lax.ppermute(array, "dp", [(i, i - 2) for i in range(2, learners - 2 * first)])
+
+    def by_x(at_zero, at_one):
+        return jnp.where(x == 0, at_zero, at_one)
+
+    lengths = seq_lengths.reshape(learners, learners)
+    dests = seq_dest.reshape(learners, learners)
+    offsets = seq_offset.reshape(learners, learners)
+    starts = jnp.cumsum(lengths, axis=1) - lengths
+    peer_ids = jnp.arange(learners, dtype=jnp.int32)
+    rows = jnp.arange(row_count, dtype=jnp.int32)
+
+    def sends(rollout):
+        length = lax.dynamic_index_in_dim(lengths, rollout, 0, keepdims=False)
+        start = lax.dynamic_index_in_dim(starts, rollout, 0, keepdims=False)
+        dest = lax.dynamic_index_in_dim(dests, rollout, 0, keepdims=False)
+        match = (dest[None, :] == peer_ids[:, None]).astype(jnp.int32)
+        inside = (rows[:, None] >= start[None, :]) & (rows[:, None] < (start + length)[None, :])
+        position = rows - jnp.sum(inside.astype(jnp.int32) * start[None, :], axis=1)
+        cosine, sine = rope_tables(position)
+        cosine = jnp.concatenate([cosine, cosine], axis=1)
+        sine = jnp.concatenate([-sine, sine], axis=1)
+        return (
+            jnp.sum(match * start[None, :], axis=1),
+            jnp.sum(match * length[None, :], axis=1),
+            cosine,
+            sine,
+        )
+
+    def receives(learner):
+        matched = (dests == learner).astype(jnp.int32)
+        return jnp.sum(matched * offsets, axis=1), jnp.sum(matched * lengths, axis=1)
+
+    other = me ^ 1
+    own_table, other_table = sends(me), sends(other)
+
+    kv_mine, kv_give = by_x(w_key, w_value), by_x(w_value, w_key)
+    q_mine = lax.dynamic_slice_in_dim(w_query, x * half, half, 1)
+    q_give = lax.dynamic_slice_in_dim(w_query, (1 - x) * half, half, 1)
+    places = []
+    for c in range(heads + 1):
+        if c == 0:
+            mine, give = kv_mine, kv_give
+        else:
+            mine, give = (w[:, (c - 1) * HD : c * HD] for w in (q_mine, q_give))
+        got = swap_x(give)
+        own = by_x(jnp.concatenate([mine, got], axis=0), jnp.concatenate([got, mine], axis=0))
+        ups, downs = [own], [own]
+        for step in range(line - 1):
+            ups.append(up(ups[-1], step))
+            downs.append(down(downs[-1], step))
+        places.append(ups[:0:-1] + downs)
+    bias_kv = by_x(b_key, b_value)
+    bias_q = lax.dynamic_slice_in_dim(b_query, x * half, half, 0)
+    bias = jnp.concatenate([bias_kv, bias_q])[None, :]
+
+    widened = rollout_states.astype(jnp.float32)
+    squares = jnp.sum(widened * widened, axis=-1)
+    squares = squares + swap_core(squares)
+    squares = squares + swap_y(squares)
+    statistic = squares[:, None] / (4 * feature_count)
+    gain = lax.dynamic_slice_in_dim(norm_gain, t * feature_count, feature_count, 0)
+    normed = (widened * lax.rsqrt(statistic + norm_eps) * gain[None, :]).astype(jnp.bfloat16)
+
+    middle = row_count // 2
+    own_y = swap_y(normed)
+    near = swap_x(normed)
+    near_y = jnp.concatenate([swap_y(near[:middle]), swap_x(own_y[middle:])], axis=0)
+    own_x = [normed, swap_core(normed), own_y, swap_core(own_y)]
+    near_x = [near, swap_core(near), near_y, swap_core(near_y)]
+    off = jnp.stack([(t ^ i) - z for i in range(4)]).astype(jnp.int32)
+
+    def tables(table):
+        cosine, sine = table[2], table[3]
+        cos_kv = by_x(cosine, jnp.ones_like(cosine))
+        sin_kv = by_x(sine, jnp.zeros_like(sine))
+        return cos_kv[None], sin_kv[None], cosine[None], sine[None]
+
+    def one(x_blocks, table, c):
+        cos_kv, sin_kv, cosine, sine = table
+        pick = (cos_kv, sin_kv) if c == 0 else (cosine, sine)
+        return project(off, x_blocks, places[c : c + 1], bias[:, c * HD : (c + 1) * HD], *pick)
+
+    own_tables, other_tables = tables(own_table), tables(other_table)
+    own_kv = one(own_x, own_tables, 0)
+    other_kv = one(near_x, other_tables, 0)
+    own_kv_got, other_kv_got = swap_x(other_kv), swap_x(own_kv)
+    own_k, own_v = by_x(own_kv, own_kv_got), by_x(own_kv_got, own_kv)
+    other_k, other_v = by_x(other_kv, other_kv_got), by_x(other_kv_got, other_kv)
+
+    z_ids = jnp.arange(line, dtype=jnp.int32)
+    order = jnp.stack([2 * z_ids + x, 2 * z_ids + 1 - x], axis=1).reshape(-1)
+    at_zero, at_one = receives(2 * z), receives(2 * z + 1)
+    run_start = jnp.stack([at_zero[0][order], at_one[0][order]])
+    run_length = jnp.stack([at_zero[1][order], at_one[1][order]])
+    groups = [[2 * i + j for i in range(line)] for j in range(2)]
+
+    kept, got = [], []
+    for c in range(1, heads + 1):
+        own_q = one(own_x, own_tables, c)
+        other_q = one(near_x, other_tables, c)
+        own_slots = attend(own_table[0], own_table[1], own_q, own_k, own_v, slot)
+        other_slots = attend(other_table[0], other_table[1], other_q, other_k, other_v, slot)
+        outgoing = jnp.stack(
+            [own_slots.reshape(line, 2, slot, HD), other_slots.reshape(line, 2, slot, HD)], axis=1
+        )
+        incoming = lax.all_to_all(
+            outgoing, "dp", split_axis=0, concat_axis=0, tiled=True, axis_index_groups=groups
+        )
+        placed = place(run_start, run_length, incoming.reshape(2 * line, 2, slot, HD), row_count)
+        kept.append(by_x(placed[0], placed[1]))
+        got.append(swap_x(by_x(placed[1], placed[0])))
+    kept = jnp.concatenate(kept, axis=1)
+    got = jnp.concatenate(got, axis=1)
+    return by_x(jnp.concatenate([kept, got], axis=1), jnp.concatenate([got, kept], axis=1))
 
 
 def solution(mesh):
@@ -148,6 +475,11 @@
         P(),
         P(),
     )
+    fits_line = mesh.shape["dp"] == 8 and mesh.shape["tensor"] == 4
     return jax.shard_map(
-        local, mesh=mesh, in_specs=placed, out_specs=P("dp", "tensor"), check_vma=False
-    )
+        local_line if fits_line else local_any,
+        mesh=mesh,
+        in_specs=placed,
+        out_specs=P("dp", "tensor"),
+        check_vma=False,
+    )

time: 788 us -> 612 us (0.78)
  waiting for transfers between devices: 585 us -> 283 us
  Pallas kernels: 0 us -> 171 us
  starting transfers between devices: 7.59 us -> 96 us
  matrix products: 68 us -> 0 us
  local copies, waits for them, and re-layouts: 72.3 us -> 19.4 us
  between operations: 13.3 us -> 1.65 us
    all_gather x4 -> x0, waiting for transfers between devices: 400 us -> none  [the longest x1 216 us: local(): lax.all_gather(w_query, 'dp', axis=0, tiled=True)]
    ppermute x0 -> x51, waiting for transfers between devices: none -> 276 us  [the longest x13 146 us: swap_x(): return lax.ppermute(array, 'dp', [(i, i ^ 1) for i in range(learners)])]
    all_to_all x1 -> x4, waiting for transfers between devices: 183 us -> 7.18 us  [local_line(): lax.all_to_all(outgoing, 'dp', split_axis=0, concat_axis=0, tiled=True, a...]
    pallas_call x0 -> x22, Pallas kernels: none -> 171 us  [the longest x10 105 us: project(): pl.pallas_call(functools.partial(project_kernel, chunks), grid_spec=grid_...]
    ppermute x0 -> x51, starting transfers between devices: none -> 74 us  [the longest x15 33.5 us: up(): lax.ppermute(array, 'dp', [(i, i + 2) for i in range(2 * first, learners...]
    dot_general x7 -> x0, matrix products: 68 us -> none  [the longest x1 24.4 us: local(): query = jnp.dot(normed, full_query, preferred_element_type=jnp.float32)]
    gather x3 -> x4, local copies, waits for them, and re-layouts: 41.8 us -> 2.59 us  [the longest x2 1.3 us: local_line(): run_start = jnp.stack([at_zero[0][order], at_one[0][order]])]
    all_to_all x1 -> x4, starting transfers between devices: 7.25 us -> 22 us  [local_line(): lax.all_to_all(outgoing, 'dp', split_axis=0, concat_axis=0, tiled=True, a...]
  transfers between devices with their start and end apart: 5 -> 55, of which waited for: 5 -> 21; matrix products, arithmetic and copies ran while one was open for 4% -> 7% of each run, Pallas kernels for 0% -> 28%
where the time goes in v1:
time: 612 us; the launch traced here: 604 us
  waiting for transfers between devices  283 us (46%)
  Pallas kernels  171 us (28%)
  starting transfers between devices  96 us (16%)
  other arithmetic  33.2 us (5%)
  local copies, waits for them, and re-layouts  19.4 us (3%)
    ppermute x13, waiting for transfers between devices, swap_x(): return lax.ppermute(array, 'dp', [(i, i ^ 1) for i in range(learners)])  146 us
    ppermute x15, waiting for transfers between devices, down(): lax.ppermute(array, 'dp', [(i, i - 2) for i in range(2, learners - 2 * fi...  109 us
    pallas_call x10, Pallas kernels, project(): pl.pallas_call(functools.partial(project_kernel, chunks), grid_spec=grid_...  105 us
    pallas_call x8, Pallas kernels, attend(): pl.pallas_call(functools.partial(attend_kernel, heads, slot, window), gri...  55.8 us
    ppermute x15, starting transfers between devices, up(): lax.ppermute(array, 'dp', [(i, i + 2) for i in range(2 * first, learners...  33.5 us
    all_to_all x4, starting transfers between devices, local_line(): lax.all_to_all(outgoing, 'dp', split_axis=0, concat_axis=0, tiled=True, a...  22 us
    ppermute x15, starting transfers between devices, down(): lax.ppermute(array, 'dp', [(i, i - 2) for i in range(2, learners - 2 * fi...  19.9 us
    ppermute x15, waiting for transfers between devices, up(): lax.ppermute(array, 'dp', [(i, i + 2) for i in range(2 * first, learners...  19.2 us
  transfers between devices with their start and end apart: 55, of which 21 were waited for; matrix products, arithmetic and copies ran while one was open for 7% of the time, Pallas kernels for 28%

profile of v1, /device:TPU:0, one launch (start us, length us, event | category | flops | bytes accessed | tf_op | source)
XLA Modules:
  0.0 604.0 jit_solution(6150760502252012164)
XLA Ops:
  17.6 88.6 %collective-permute-done.19.refs_0_ = bf16[1024,2048]{1,0:T(8,128)(2,1)} collective-permute-done((bf16[1024,2048]{1,0:T(8,128)(2,1)}, bf16[1024,2048]{1,0:T(8,128)(2,1)}, u32[]{:S(2)}, u32[]{:S(2)}) %collective-permute-start.19) | collective-permute-done | bytes 4194336 | tf_op jit(solution)/shard_map/ppermute | solution.py:335
  120.5 48.2 %collective-permute-done.12 = bf16[1024,128]{1,0:T(8,128)(2,1)S(1)} collective-permute-done((bf16[1024,128]{1,0:T(8,128)(2,1)}, bf16[1024,128]{1,0:T(8,128)(2,1)S(1)}, u32[]{:S(2)}, u32[]{:S(2)}) %collective-permute-start.12) | collective-permute-done | bytes 262176 | tf_op jit(solution)/shard_map/ppermute | solution.py:335
  200.0 6.9 %collective-permute-done.37.refs_8_ = bf16[2048,128]{1,0:T(8,128)(2,1)S(1)} collective-permute-done((bf16[2048,128]{1,0:T(8,128)(2,1)S(1)}, bf16[2048,128]{1,0:T(8,128)(2,1)S(1)}, u32[]{:S(2)}, u32[]{:S(2)}) %collective-permute-start.37) | collective-permute-done | bytes 524320 | tf_op jit(solution)/shard_map/ppermute | solution.py:347
  207.9 7.9 %collective-permute-done.17.refs_9_ = bf16[2048,128]{1,0:T(8,128)(2,1)} collective-permute-done((bf16[2048,128]{1,0:T(8,128)(2,1)S(1)}, bf16[2048,128]{1,0:T(8,128)(2,1)}, u32[]{:S(2)}, u32[]{:S(2)}) %collective-permute-start.17) | collective-permute-done | bytes 524320 | tf_op jit(solution)/shard_map/ppermute | solution.py:347
  219.0 20.0 %collective-permute-done.38.refs_9_ = bf16[2048,128]{1,0:T(8,128)(2,1)S(1)} collective-permute-done((bf16[2048,128]{1,0:T(8,128)(2,1)S(1)}, bf16[2048,128]{1,0:T(8,128)(2,1)S(1)}, u32[]{:S(2)}, u32[]{:S(2)}) %collective-permute-start.38) | collective-permute-done | bytes 524320 | tf_op jit(solution)/shard_map/ppermute | solution.py:347
  248.4 9.0 %collective-permute-done.18.refs_10_ = bf16[2048,128]{1,0:T(8,128)(2,1)S(1)} collective-permute-done((bf16[2048,128]{1,0:T(8,128)(2,1)}, bf16[2048,128]{1,0:T(8,128)(2,1)S(1)}, u32[]{:S(2)}, u32[]{:S(2)}) %collective-permute-start.18) | collective-permute-done | bytes 524320 | tf_op jit(solution)/shard_map/ppermute | solution.py:347
  272.4 10.7 %shard_map.110 = bf16[1024,128]{1,0:T(8,128)(2,1)S(1)} custom-call(s32[4]{0:T(128)S(1)} %pad_add_fusion.3.off_ref, bf16[1024,2048]{1,0:T(8,128)(2,1)} %fusion.2.refs_0_, bf16[1024,2048]{1,0:T(8,128)(2,1)} %collective-permute-done.2.refs_1_, bf16[1024,2048]{1,0:T(8,128)(2,1)} %collective-permute-done.3.refs_2_, ...), custom_call_target="tpu_custom_call" | custom-call | flops 2147483648 | bytes 18874368 | tf_op jit(solution)/shard_map/pallas_call | solution.py:196
  284.7 9.4 %shard_map.121.q_ref = bf16[1024,128]{1,0:T(8,128)(2,1)S(1)} custom-call(s32[4]{0:T(128)S(1)} %pad_add_fusion.3.off_ref, bf16[1024,2048]{1,0:T(8,128)(2,1)} %fusion.2.refs_0_, bf16[1024,2048]{1,0:T(8,128)(2,1)} %collective-permute-done.2.refs_1_, bf16[1024,2048]{1,0:T(8,128)(2,1)} %collective-permute-done.3.refs_2_, ...), custom_call_target="tpu_custom_call" | custom-call | flops 2147483648 | bytes 18874368 | tf_op jit(solution)/shard_map/pallas_call | solution.py:196
  297.5 10.7 %shard_map.111 = bf16[1024,128]{1,0:T(8,128)(2,1)S(1)} custom-call(s32[4]{0:T(128)S(1)} %pad_add_fusion.3.off_ref, bf16[1024,2048]{1,0:T(8,128)(2,1)} %collective-permute-done.19.refs_0_, bf16[1024,2048]{1,0:T(8,128)(2,1)} %collective-permute-done.20.refs_1_, bf16[1024,2048]{1,0:T(8,128)(2,1)} %constant_dynamic-update-slice_fusion.refs_2_, ...), custom_call_target="tpu_custom_call" | custom-call | flops 2147483648 | bytes 18874368 | tf_op jit(solution)/shard_map/pallas_call | solution.py:196
  309.8 9.4 %shard_map.123.q_ref = bf16[1024,128]{1,0:T(8,128)(2,1)S(1)} custom-call(s32[4]{0:T(128)S(1)} %pad_add_fusion.3.off_ref, bf16[1024,2048]{1,0:T(8,128)(2,1)} %collective-permute-done.19.refs_0_, bf16[1024,2048]{1,0:T(8,128)(2,1)} %collective-permute-done.20.refs_1_, bf16[1024,2048]{1,0:T(8,128)(2,1)} %constant_dynamic-update-slice_fusion.refs_2_, ...), custom_call_target="tpu_custom_call" | custom-call | flops 2147483648 | bytes 18874368 | tf_op jit(solution)/shard_map/pallas_call | solution.py:196
  319.3 7.0 %shard_map.124 = bf16[8,256,128]{2,1,0:T(8,128)(2,1)S(1)} custom-call(s32[8]{0:T(128)S(1)} %get-tuple-element.14.start_ref, s32[8]{0:T(128)S(1)} %get-tuple-element.13.len_ref, bf16[1024,128]{1,0:T(8,128)(2,1)S(1)} %shard_map.123.q_ref, bf16[1024,128]{1,0:T(8,128)(2,1)S(1)} %get-tuple-element.34.k_ref, bf16[1024,128]{1,0:T(8,128)(2,1)S(1)} %get-tuple-element.33.v_ref), custom_call_target="tpu_custom_call" | custom-call | flops 469762048 | bytes 1310720 | tf_op jit(solution)/shard_map/pallas_call | solution.py:257
  326.3 7.0 %shard_map.122 = bf16[8,256,128]{2,1,0:T(8,128)(2,1)S(1)} custom-call(s32[8]{0:T(128)S(1)} %get-tuple-element.12.start_ref, s32[8]{0:T(128)S(1)} %get-tuple-element.11.len_ref, bf16[1024,128]{1,0:T(8,128)(2,1)S(1)} %shard_map.121.q_ref, bf16[1024,128]{1,0:T(8,128)(2,1)S(1)} %get-tuple-element.32.k_ref, bf16[1024,128]{1,0:T(8,128)(2,1)S(1)} %get-tuple-element.31.v_ref), custom_call_target="tpu_custom_call" | custom-call | flops 469762048 | bytes 1310720 | tf_op jit(solution)/shard_map/pallas_call | solution.py:257
  334.4 7.6 %all-to-all-start.2 = ((bf16[4,2,2,256,128]{4,3,2,1,0:T(8,128)(2,1)}), bf16[4,2,2,256,128]{4,3,2,1,0:T(8,128)(2,1)}, u32[]{:S(2)}, u32[]{:S(2)}) async-start(bf16[4,2,2,256,128]{4,3,2,1,0:T(8,128)(2,1)} %pad_maximum_fusion.2), calls=%async_computation.2 | async-start | bytes 2097152 | tf_op jit(solution)/shard_map/all_to_all | solution.py:453
  352.6 18.1 %collective-permute-done.9.refs_8_ = bf16[2048,128]{1,0:T(8,128)(2,1)} collective-permute-done((bf16[2048,128]{1,0:T(8,128)(2,1)S(1)}, bf16[2048,128]{1,0:T(8,128)(2,1)}, u32[]{:S(2)}, u32[]{:S(2)}) %collective-permute-start.9) | collective-permute-done | bytes 524320 | tf_op jit(solution)/shard_map/ppermute | solution.py:347
  373.7 7.2 %collective-permute-done.32.refs_10_ = bf16[2048,128]{1,0:T(8,128)(2,1)S(1)} collective-permute-done((bf16[2048,128]{1,0:T(8,128)(2,1)}, bf16[2048,128]{1,0:T(8,128)(2,1)S(1)}, u32[]{:S(2)}, u32[]{:S(2)}) %collective-permute-start.32) | collective-permute-done | bytes 524320 | tf_op jit(solution)/shard_map/ppermute | solution.py:347
  380.9 10.8 %shard_map.116.q_ref = bf16[1024,128]{1,0:T(8,128)(2,1)S(1)} custom-call(s32[4]{0:T(128)S(1)} %pad_add_fusion.3.off_ref, bf16[1024,2048]{1,0:T(8,128)(2,1)} %fusion.2.refs_0_, bf16[1024,2048]{1,0:T(8,128)(2,1)} %collective-permute-done.2.refs_1_, bf16[1024,2048]{1,0:T(8,128)(2,1)} %collective-permute-done.3.refs_2_, ...), custom_call_target="tpu_custom_call" | custom-call | flops 2147483648 | bytes 18874368 | tf_op jit(solution)/shard_map/pallas_call | solution.py:196
  391.8 10.8 %shard_map.118.q_ref = bf16[1024,128]{1,0:T(8,128)(2,1)S(1)} custom-call(s32[4]{0:T(128)S(1)} %pad_add_fusion.3.off_ref, bf16[1024,2048]{1,0:T(8,128)(2,1)} %collective-permute-done.19.refs_0_, bf16[1024,2048]{1,0:T(8,128)(2,1)} %collective-permute-done.20.refs_1_, bf16[1024,2048]{1,0:T(8,128)(2,1)} %constant_dynamic-update-slice_fusion.refs_2_, ...), custom_call_target="tpu_custom_call" | custom-call | flops 2147483648 | bytes 18874368 | tf_op jit(solution)/shard_map/pallas_call | solution.py:196
  402.6 7.0 %shard_map.119 = bf16[8,256,128]{2,1,0:T(8,128)(2,1)S(1)} custom-call(s32[8]{0:T(128)S(1)} %get-tuple-element.14.start_ref, s32[8]{0:T(128)S(1)} %get-tuple-element.13.len_ref, bf16[1024,128]{1,0:T(8,128)(2,1)S(1)} %shard_map.118.q_ref, bf16[1024,128]{1,0:T(8,128)(2,1)S(1)} %copy-done.21, bf16[1024,128]{1,0:T(8,128)(2,1)S(1)} %get-tuple-element.33.v_ref), custom_call_target="tpu_custom_call" | custom-call | flops 469762048 | bytes 1310720 | tf_op jit(solution)/shard_map/pallas_call | solution.py:257
  409.6 7.0 %shard_map.117 = bf16[8,256,128]{2,1,0:T(8,128)(2,1)S(1)} custom-call(s32[8]{0:T(128)S(1)} %get-tuple-element.12.start_ref, s32[8]{0:T(128)S(1)} %get-tuple-element.11.len_ref, bf16[1024,128]{1,0:T(8,128)(2,1)S(1)} %shard_map.116.q_ref, bf16[1024,128]{1,0:T(8,128)(2,1)S(1)} %copy-done.29, bf16[1024,128]{1,0:T(8,128)(2,1)S(1)} %copy-done.25), custom_call_target="tpu_custom_call" | custom-call | flops 469762048 | bytes 1310720 | tf_op jit(solution)/shard_map/pallas_call | solution.py:257
  432.3 13.4 %collective-permute-done.41.refs_6_ = bf16[2048,128]{1,0:T(8,128)(2,1)} collective-permute-done((bf16[2048,128]{1,0:T(8,128)(2,1)S(1)}, bf16[2048,128]{1,0:T(8,128)(2,1)}, u32[]{:S(2)}, u32[]{:S(2)}) %collective-permute-start.41) | collective-permute-done | bytes 524320 | tf_op jit(solution)/shard_map/ppermute | solution.py:344
  452.8 8.2 %collective-permute-done.11.refs_10_ = bf16[2048,128]{1,0:T(8,128)(2,1)S(1)} collective-permute-done((bf16[2048,128]{1,0:T(8,128)(2,1)}, bf16[2048,128]{1,0:T(8,128)(2,1)S(1)}, u32[]{:S(2)}, u32[]{:S(2)}) %collective-permute-start.11) | collective-permute-done | bytes 524320 | tf_op jit(solution)/shard_map/ppermute | solution.py:347
  461.1 10.8 %shard_map.109.q_ref = bf16[1024,128]{1,0:T(8,128)(2,1)S(1)} custom-call(s32[4]{0:T(128)S(1)} %pad_add_fusion.3.off_ref, bf16[1024,2048]{1,0:T(8,128)(2,1)} %fusion.2.refs_0_, bf16[1024,2048]{1,0:T(8,128)(2,1)} %collective-permute-done.2.refs_1_, bf16[1024,2048]{1,0:T(8,128)(2,1)} %collective-permute-done.3.refs_2_, ...), custom_call_target="tpu_custom_call" | custom-call | flops 2147483648 | bytes 18874368 | tf_op jit(solution)/shard_map/pallas_call | solution.py:196
  471.9 10.8 %shard_map.113.q_ref = bf16[1024,128]{1,0:T(8,128)(2,1)S(1)} custom-call(s32[4]{0:T(128)S(1)} %pad_add_fusion.3.off_ref, bf16[1024,2048]{1,0:T(8,128)(2,1)} %collective-permute-done.19.refs_0_, bf16[1024,2048]{1,0:T(8,128)(2,1)} %collective-permute-done.20.refs_1_, bf16[1024,2048]{1,0:T(8,128)(2,1)} %constant_dynamic-update-slice_fusion.refs_2_, ...), custom_call_target="tpu_custom_call" | custom-call | flops 2147483648 | bytes 18874368 | tf_op jit(solution)/shard_map/pallas_call | solution.py:196
  482.8 7.0 %shard_map.114 = bf16[8,256,128]{2,1,0:T(8,128)(2,1)S(1)} custom-call(s32[8]{0:T(128)S(1)} %get-tuple-element.14.start_ref, s32[8]{0:T(128)S(1)} %get-tuple-element.13.len_ref, bf16[1024,128]{1,0:T(8,128)(2,1)S(1)} %shard_map.113.q_ref, bf16[1024,128]{1,0:T(8,128)(2,1)S(1)} %copy-done.22, bf16[1024,128]{1,0:T(8,128)(2,1)S(1)} %get-tuple-element.33.v_ref), custom_call_target="tpu_custom_call" | custom-call | flops 469762048 | bytes 1310720 | tf_op jit(solution)/shard_map/pallas_call | solution.py:257
  489.8 7.0 %shard_map.112 = bf16[8,256,128]{2,1,0:T(8,128)(2,1)S(1)} custom-call(s32[8]{0:T(128)S(1)} %get-tuple-element.12.start_ref, s32[8]{0:T(128)S(1)} %get-tuple-element.11.len_ref, bf16[1024,128]{1,0:T(8,128)(2,1)S(1)} %shard_map.109.q_ref, bf16[1024,128]{1,0:T(8,128)(2,1)S(1)} %copy-done.30, bf16[1024,128]{1,0:T(8,128)(2,1)S(1)} %copy-done.26), custom_call_target="tpu_custom_call" | custom-call | flops 469762048 | bytes 1310720 | tf_op jit(solution)/shard_map/pallas_call | solution.py:257
  505.8 23.5 %collective-permute-done.46.refs_10_ = bf16[2048,128]{1,0:T(8,128)(2,1)S(1)} collective-permute-done((bf16[2048,128]{1,0:T(8,128)(2,1)}, bf16[2048,128]{1,0:T(8,128)(2,1)S(1)}, u32[]{:S(2)}, u32[]{:S(2)}) %collective-permute-start.46) | collective-permute-done | bytes 524320 | tf_op jit(solution)/shard_map/ppermute | solution.py:347
  529.2 10.8 %shard_map.126.q_ref = bf16[1024,128]{1,0:T(8,128)(2,1)S(1)} custom-call(s32[4]{0:T(128)S(1)} %pad_add_fusion.3.off_ref, bf16[1024,2048]{1,0:T(8,128)(2,1)} %fusion.2.refs_0_, bf16[1024,2048]{1,0:T(8,128)(2,1)} %collective-permute-done.2.refs_1_, bf16[1024,2048]{1,0:T(8,128)(2,1)} %collective-permute-done.3.refs_2_, ...), custom_call_target="tpu_custom_call" | custom-call | flops 2147483648 | bytes 18874368 | tf_op jit(solution)/shard_map/pallas_call | solution.py:196
  540.1 10.8 %shard_map.128.q_ref = bf16[1024,128]{1,0:T(8,128)(2,1)S(1)} custom-call(s32[4]{0:T(128)S(1)} %pad_add_fusion.3.off_ref, bf16[1024,2048]{1,0:T(8,128)(2,1)} %collective-permute-done.19.refs_0_, bf16[1024,2048]{1,0:T(8,128)(2,1)} %collective-permute-done.20.refs_1_, bf16[1024,2048]{1,0:T(8,128)(2,1)} %constant_dynamic-update-slice_fusion.refs_2_, ...), custom_call_target="tpu_custom_call" | custom-call | flops 2147483648 | bytes 18874368 | tf_op jit(solution)/shard_map/pallas_call | solution.py:196
  551.0 7.0 %shard_map.129 = bf16[8,256,128]{2,1,0:T(8,128)(2,1)S(1)} custom-call(s32[8]{0:T(128)S(1)} %get-tuple-element.14.start_ref, s32[8]{0:T(128)S(1)} %get-tuple-element.13.len_ref, bf16[1024,128]{1,0:T(8,128)(2,1)S(1)} %shard_map.128.q_ref, bf16[1024,128]{1,0:T(8,128)(2,1)S(1)} %copy-done.23, bf16[1024,128]{1,0:T(8,128)(2,1)S(1)} %get-tuple-element.33.v_ref), custom_call_target="tpu_custom_call" | custom-call | flops 469762048 | bytes 1310720 | tf_op jit(solution)/shard_map/pallas_call | solution.py:257
  558.0 7.0 %shard_map.127 = bf16[8,256,128]{2,1,0:T(8,128)(2,1)S(1)} custom-call(s32[8]{0:T(128)S(1)} %get-tuple-element.12.start_ref, s32[8]{0:T(128)S(1)} %get-tuple-element.11.len_ref, bf16[1024,128]{1,0:T(8,128)(2,1)S(1)} %shard_map.126.q_ref, bf16[1024,128]{1,0:T(8,128)(2,1)S(1)} %copy-done.31, bf16[1024,128]{1,0:T(8,128)(2,1)S(1)} %copy-done.27), custom_call_target="tpu_custom_call" | custom-call | flops 469762048 | bytes 1310720 | tf_op jit(solution)/shard_map/pallas_call | solution.py:257
  585.3 7.2 %all-to-all-done.3 = bf16[4,2,2,256,128]{4,3,2,1,0:T(8,128)(2,1)S(1)} async-done(((bf16[4,2,2,256,128]{4,3,2,1,0:T(8,128)(2,1)}), bf16[4,2,2,256,128]{4,3,2,1,0:T(8,128)(2,1)S(1)}, u32[]{:S(2)}, u32[]{:S(2)}) %all-to-all-start.3) | async-done | bytes 1048608 | tf_op jit(solution)/shard_map/all_to_all | solution.py:453
  595.1 5.8 collective-permute-done.50
  (262 shorter events, 169.7 us)
Async XLA Ops:
  14.1 92.1 %collective-permute-start.19 = (bf16[1024,2048]{1,0:T(8,128)(2,1)}, bf16[1024,2048]{1,0:T(8,128)(2,1)}, u32[]{:S(2)}, u32[]{:S(2)}) collective-permute-start(bf16[1024,2048]{1,0:T(8,128)(2,1)} %fusion.2.refs_0_), channel_id=1, source_target_pairs={{0,4},{4,0},{8,12},{12,8},{16,20},{20,16},{24,28},{28,24},{1,5},{5... | collective-permute-start | bytes 12582920 | tf_op jit(solution)/shard_map/ppermute | solution.py:335
  16.1 95.0 %collective-permute-start.3 = (bf16[1024,2048]{1,0:T(8,128)(2,1)}, bf16[1024,2048]{1,0:T(8,128)(2,1)}, u32[]{:S(2)}, u32[]{:S(2)}) collective-permute-start(bf16[1024,2048]{1,0:T(8,128)(2,1)} %fusion.2.refs_0_), channel_id=1, source_target_pairs={{0,2},{1,3},{2,0},{3,1},{4,6},{5,7},{6,4},{7,5},{8,10},{9,11},{10,... | collective-permute-start | bytes 12582920 | tf_op jit(solution)/shard_map/ppermute | solution.py:338
  109.4 82.1 %collective-permute-start.21 = (bf16[512,2048]{1,0:T(8,128)(2,1)}, bf16[512,2048]{1,0:T(8,128)(2,1)}, u32[]{:S(2)}, u32[]{:S(2)}) collective-permute-start(bf16[512,2048]{1,0:T(8,128)(2,1)} %slice.115), channel_id=1, source_target_pairs={{0,2},{1,3},{2,0},{3,1},{4,6},{5,7},{6,4},{7,5},{8,10},{9,11},{10,... | collective-permute-start | bytes 6291464 | tf_op jit(solution)/shard_map/ppermute | solution.py:338
  114.3 81.1 %collective-permute-start.22 = (bf16[512,2048]{1,0:T(8,128)(2,1)}, bf16[512,2048]{1,0:T(8,128)(2,1)}, u32[]{:S(2)}, u32[]{:S(2)}) collective-permute-start(bf16[512,2048]{1,0:T(8,128)(2,1)} %slice.116), channel_id=1, source_target_pairs={{0,4},{4,0},{8,12},{12,8},{16,20},{20,16},{24,28},{28,24},{1,5},{5... | collective-permute-start | bytes 6291464 | tf_op jit(solution)/shard_map/ppermute | solution.py:335
  116.5 52.2 %collective-permute-start.12 = (bf16[1024,128]{1,0:T(8,128)(2,1)}, bf16[1024,128]{1,0:T(8,128)(2,1)S(1)}, u32[]{:S(2)}, u32[]{:S(2)}) collective-permute-start(bf16[1024,128]{1,0:T(8,128)(2,1)} %get-tuple-element.36), channel_id=1, source_target_pairs={{0,4},{4,0},{8,12},{12,8},{16,20},{20,16},{24,28},{28,24},{1,5},{5... | collective-permute-start | bytes 786440 | tf_op jit(solution)/shard_map/ppermute | solution.py:335
  118.4 55.4 %collective-permute-start.33 = (bf16[1024,128]{1,0:T(8,128)(2,1)S(1)}, bf16[1024,128]{1,0:T(8,128)(2,1)S(1)}, u32[]{:S(2)}, u32[]{:S(2)}) collective-permute-start(bf16[1024,128]{1,0:T(8,128)(2,1)S(1)} %get-tuple-element.16), channel_id=1, source_target_pairs={{0,4},{4,0},{8,12},{12,8},{16,20},{20,16},{24,28},{28,24},{1,5},{5... | collective-permute-start | bytes 786440 | tf_op jit(solution)/shard_map/ppermute | solution.py:335
  119.9 56.7 %collective-permute-start.26 = (bf16[1024,128]{1,0:T(8,128)(2,1)S(1)}, bf16[1024,128]{1,0:T(8,128)(2,1)S(1)}, u32[]{:S(2)}, u32[]{:S(2)}) collective-permute-start(bf16[1024,128]{1,0:T(8,128)(2,1)S(1)} %get-tuple-element.18), channel_id=1, source_target_pairs={{0,4},{4,0},{8,12},{12,8},{16,20},{20,16},{24,28},{28,24},{1,5},{5... | collective-permute-start | bytes 786440 | tf_op jit(solution)/shard_map/ppermute | solution.py:335
  180.7 84.5 %collective-permute-start.2 = (bf16[1024,2048]{1,0:T(8,128)(2,1)}, bf16[1024,2048]{1,0:T(8,128)(2,1)}, u32[]{:S(2)}, u32[]{:S(2)}) collective-permute-start(bf16[1024,2048]{1,0:T(8,128)(2,1)} %fusion.2.refs_0_), channel_id=1, source_target_pairs={{0,1},{1,0},{2,3},{3,2},{4,5},{5,4},{6,7},{7,6},{8,9},{9,8},{10,11... | collective-permute-start | bytes 12582920 | tf_op jit(solution)/shard_map/ppermute | solution.py:341
  184.9 85.7 %collective-permute-start.4 = (bf16[1024,2048]{1,0:T(8,128)(2,1)}, bf16[1024,2048]{1,0:T(8,128)(2,1)}, u32[]{:S(2)}, u32[]{:S(2)}) collective-permute-start(bf16[1024,2048]{1,0:T(8,128)(2,1)} %collective-permute-done.3.refs_2_), channel_id=1, source_target_pairs={{0,1},{1,0},{2,3},{3,2},{4,5},{5,4},{6,7},{7,6},{8,9},{9,8},{10,11... | collective-permute-start | bytes 12582920 | tf_op jit(solution)/shard_map/ppermute | solution.py:341
  206.9 89.2 %collective-permute-start.20 = (bf16[1024,2048]{1,0:T(8,128)(2,1)}, bf16[1024,2048]{1,0:T(8,128)(2,1)}, u32[]{:S(2)}, u32[]{:S(2)}) collective-permute-start(bf16[1024,2048]{1,0:T(8,128)(2,1)} %collective-permute-done.19.refs_0_), channel_id=1, source_target_pairs={{0,1},{1,0},{2,3},{3,2},{4,5},{5,4},{6,7},{7,6},{8,9},{9,8},{10,11... | collective-permute-start | bytes 12582920 | tf_op jit(solution)/shard_map/ppermute | solution.py:341
  207.0 90.5 %collective-permute-start.23 = (bf16[1024,2048]{1,0:T(8,128)(2,1)}, bf16[1024,2048]{1,0:T(8,128)(2,1)}, u32[]{:S(2)}, u32[]{:S(2)}) collective-permute-start(bf16[1024,2048]{1,0:T(8,128)(2,1)} %constant_dynamic-update-slice_fusion.refs_2_), channel_id=1, source_target_pairs={{0,1},{1,0},{2,3},{3,2},{4,5},{5,4},{6,7},{7,6},{8,9},{9,8},{10,11... | collective-permute-start | bytes 12582920 | tf_op jit(solution)/shard_map/ppermute | solution.py:341
  265.2 28.9 %collective-permute-start.27 = (bf16[2048,128]{1,0:T(8,128)(2,1)S(1)}, bf16[2048,128]{1,0:T(8,128)(2,1)}, u32[]{:S(2)}, u32[]{:S(2)}) collective-permute-start(bf16[2048,128]{1,0:T(8,128)(2,1)S(1)} %maximum_select_fusion.6.refs_7_), channel_id=1, source_target_pairs={{0,8},{4,12},{8,16},{12,20},{16,24},{20,28},{1,9},{5,13},{9,17},{1... | collective-permute-start | bytes 1572872 | tf_op jit(solution)/shard_map/ppermute | solution.py:344
  270.6 24.1 %collective-permute-start.30 = (bf16[2048,128]{1,0:T(8,128)(2,1)S(1)}, bf16[2048,128]{1,0:T(8,128)(2,1)}, u32[]{:S(2)}, u32[]{:S(2)}) collective-permute-start(bf16[2048,128]{1,0:T(8,128)(2,1)S(1)} %maximum_select_fusion.6.refs_7_), channel_id=1, source_target_pairs={{8,0},{12,4},{16,8},{20,12},{24,16},{28,20},{9,1},{13,5},{17,9},{2... | collective-permute-start | bytes 1572872 | tf_op jit(solution)/shard_map/ppermute | solution.py:347
  283.1 26.7 %collective-permute-start.25 = (bf16[1024,128]{1,0:T(8,128)(2,1)S(1)}, bf16[1024,128]{1,0:T(8,128)(2,1)S(1)}, u32[]{:S(2)}, u32[]{:S(2)}) collective-permute-start(bf16[1024,128]{1,0:T(8,128)(2,1)S(1)} %shard_map.110), channel_id=1, source_target_pairs={{0,4},{4,0},{8,12},{12,8},{16,20},{20,16},{24,28},{28,24},{1,5},{5... | collective-permute-start | bytes 786440 | tf_op jit(solution)/shard_map/ppermute | solution.py:335
  294.1 47.9 %collective-permute-start.5 = (bf16[1024,128]{1,0:T(8,128)(2,1)}, bf16[1024,128]{1,0:T(8,128)(2,1)}, u32[]{:S(2)}, u32[]{:S(2)}) collective-permute-start(bf16[1024,128]{1,0:T(8,128)(2,1)} %get-tuple-element.20), channel_id=1, source_target_pairs={{0,4},{4,0},{8,12},{12,8},{16,20},{20,16},{24,28},{28,24},{1,5},{5... | collective-permute-start | bytes 786440 | tf_op jit(solution)/shard_map/ppermute | solution.py:335
  294.7 55.3 %collective-permute-start.28 = (bf16[2048,128]{1,0:T(8,128)(2,1)}, bf16[2048,128]{1,0:T(8,128)(2,1)}, u32[]{:S(2)}, u32[]{:S(2)}) collective-permute-start(bf16[2048,128]{1,0:T(8,128)(2,1)} %collective-permute-done.27.refs_6_), channel_id=1, source_target_pairs={{8,16},{12,20},{16,24},{20,28},{9,17},{13,21},{17,25},{21,29},{10,... | collective-permute-start | bytes 1572872 | tf_op jit(solution)/shard_map/ppermute | solution.py:344
  296.2 54.5 %collective-permute-start.31 = (bf16[2048,128]{1,0:T(8,128)(2,1)}, bf16[2048,128]{1,0:T(8,128)(2,1)}, u32[]{:S(2)}, u32[]{:S(2)}) collective-permute-start(bf16[2048,128]{1,0:T(8,128)(2,1)} %collective-permute-done.30.refs_8_), channel_id=1, source_target_pairs={{8,0},{12,4},{16,8},{20,12},{9,1},{13,5},{17,9},{21,13},{10,2},{14... | collective-permute-start | bytes 1572872 | tf_op jit(solution)/shard_map/ppermute | solution.py:347
  334.4 83.3 %all-to-all-start.2 = ((bf16[4,2,2,256,128]{4,3,2,1,0:T(8,128)(2,1)}), bf16[4,2,2,256,128]{4,3,2,1,0:T(8,128)(2,1)}, u32[]{:S(2)}, u32[]{:S(2)}) async-start(bf16[4,2,2,256,128]{4,3,2,1,0:T(8,128)(2,1)} %pad_maximum_fusion.2), calls=%async_computation.2 | async-start | bytes 2097152 | tf_op jit(solution)/shard_map/all_to_all | solution.py:453
  343.3 27.4 %collective-permute-start.9 = (bf16[2048,128]{1,0:T(8,128)(2,1)S(1)}, bf16[2048,128]{1,0:T(8,128)(2,1)}, u32[]{:S(2)}, u32[]{:S(2)}) collective-permute-start(bf16[2048,128]{1,0:T(8,128)(2,1)S(1)} %maximum_select_fusion.refs_7_), channel_id=1, source_target_pairs={{8,0},{12,4},{16,8},{20,12},{24,16},{28,20},{9,1},{13,5},{17,9},{2... | collective-permute-start | bytes 1572872 | tf_op jit(solution)/shard_map/ppermute | solution.py:347
  344.6 27.4 %collective-permute-start.6 = (bf16[2048,128]{1,0:T(8,128)(2,1)S(1)}, bf16[2048,128]{1,0:T(8,128)(2,1)}, u32[]{:S(2)}, u32[]{:S(2)}) collective-permute-start(bf16[2048,128]{1,0:T(8,128)(2,1)S(1)} %maximum_select_fusion.refs_7_), channel_id=1, source_target_pairs={{0,8},{4,12},{8,16},{12,20},{16,24},{20,28},{1,9},{5,13},{9,17},{1... | collective-permute-start | bytes 1572872 | tf_op jit(solution)/shard_map/ppermute | solution.py:344
  350.7 30.2 %collective-permute-start.32 = (bf16[2048,128]{1,0:T(8,128)(2,1)}, bf16[2048,128]{1,0:T(8,128)(2,1)S(1)}, u32[]{:S(2)}, u32[]{:S(2)}) collective-permute-start(bf16[2048,128]{1,0:T(8,128)(2,1)} %collective-permute-done.31.refs_9_), channel_id=1, source_target_pairs={{8,0},{12,4},{9,1},{13,5},{10,2},{14,6},{11,3},{15,7}} | collective-permute-start | bytes 1572872 | tf_op jit(solution)/shard_map/ppermute | solution.py:347
  352.0 70.7 %collective-permute-start.40 = (bf16[1024,128]{1,0:T(8,128)(2,1)}, bf16[1024,128]{1,0:T(8,128)(2,1)}, u32[]{:S(2)}, u32[]{:S(2)}) collective-permute-start(bf16[1024,128]{1,0:T(8,128)(2,1)} %get-tuple-element.22), channel_id=1, source_target_pairs={{0,4},{4,0},{8,12},{12,8},{16,20},{20,16},{24,28},{28,24},{1,5},{5... | collective-permute-start | bytes 786440 | tf_op jit(solution)/shard_map/ppermute | solution.py:335
  370.7 59.5 %collective-permute-start.10 = (bf16[2048,128]{1,0:T(8,128)(2,1)}, bf16[2048,128]{1,0:T(8,128)(2,1)}, u32[]{:S(2)}, u32[]{:S(2)}) collective-permute-start(bf16[2048,128]{1,0:T(8,128)(2,1)} %collective-permute-done.9.refs_8_), channel_id=1, source_target_pairs={{8,0},{12,4},{16,8},{20,12},{9,1},{13,5},{17,9},{21,13},{10,2},{14... | collective-permute-start | bytes 1572872 | tf_op jit(solution)/shard_map/ppermute | solution.py:347
  372.0 59.5 %collective-permute-start.7 = (bf16[2048,128]{1,0:T(8,128)(2,1)}, bf16[2048,128]{1,0:T(8,128)(2,1)}, u32[]{:S(2)}, u32[]{:S(2)}) collective-permute-start(bf16[2048,128]{1,0:T(8,128)(2,1)} %collective-permute-done.6.refs_6_), channel_id=1, source_target_pairs={{8,16},{12,20},{16,24},{20,28},{9,17},{13,21},{17,25},{21,29},{10,... | collective-permute-start | bytes 1572872 | tf_op jit(solution)/shard_map/ppermute | solution.py:344
  417.7 80.1 %all-to-all-start.1 = ((bf16[4,2,2,256,128]{4,3,2,1,0:T(8,128)(2,1)}), bf16[4,2,2,256,128]{4,3,2,1,0:T(8,128)(2,1)}, u32[]{:S(2)}, u32[]{:S(2)}) async-start(bf16[4,2,2,256,128]{4,3,2,1,0:T(8,128)(2,1)} %pad_maximum_fusion.1), calls=%async_computation.1 | async-start | bytes 2097152 | tf_op jit(solution)/shard_map/all_to_all | solution.py:453
  430.2 30.8 %collective-permute-start.11 = (bf16[2048,128]{1,0:T(8,128)(2,1)}, bf16[2048,128]{1,0:T(8,128)(2,1)S(1)}, u32[]{:S(2)}, u32[]{:S(2)}) collective-permute-start(bf16[2048,128]{1,0:T(8,128)(2,1)} %collective-permute-done.10.refs_9_), channel_id=1, source_target_pairs={{8,0},{12,4},{9,1},{13,5},{10,2},{14,6},{11,3},{15,7}} | collective-permute-start | bytes 1572872 | tf_op jit(solution)/shard_map/ppermute | solution.py:347
  431.6 29.5 %collective-permute-start.8 = (bf16[2048,128]{1,0:T(8,128)(2,1)}, bf16[2048,128]{1,0:T(8,128)(2,1)S(1)}, u32[]{:S(2)}, u32[]{:S(2)}) collective-permute-start(bf16[2048,128]{1,0:T(8,128)(2,1)} %collective-permute-done.7.refs_5_), channel_id=1, source_target_pairs={{16,24},{20,28},{17,25},{21,29},{18,26},{22,30},{19,27},{23,31}} | collective-permute-start | bytes 1572872 | tf_op jit(solution)/shard_map/ppermute | solution.py:344
  445.7 57.9 %collective-permute-start.42 = (bf16[2048,128]{1,0:T(8,128)(2,1)}, bf16[2048,128]{1,0:T(8,128)(2,1)}, u32[]{:S(2)}, u32[]{:S(2)}) collective-permute-start(bf16[2048,128]{1,0:T(8,128)(2,1)} %collective-permute-done.41.refs_6_), channel_id=1, source_target_pairs={{8,16},{12,20},{16,24},{20,28},{9,17},{13,21},{17,25},{21,29},{10,... | collective-permute-start | bytes 1572872 | tf_op jit(solution)/shard_map/ppermute | solution.py:344
  451.5 52.7 %collective-permute-start.45 = (bf16[2048,128]{1,0:T(8,128)(2,1)}, bf16[2048,128]{1,0:T(8,128)(2,1)}, u32[]{:S(2)}, u32[]{:S(2)}) collective-permute-start(bf16[2048,128]{1,0:T(8,128)(2,1)} %collective-permute-done.44.refs_8_), channel_id=1, source_target_pairs={{8,0},{12,4},{16,8},{20,12},{9,1},{13,5},{17,9},{21,13},{10,2},{14... | collective-permute-start | bytes 1572872 | tf_op jit(solution)/shard_map/ppermute | solution.py:347
  497.9 68.2 %all-to-all-start = ((bf16[4,2,2,256,128]{4,3,2,1,0:T(8,128)(2,1)}), bf16[4,2,2,256,128]{4,3,2,1,0:T(8,128)(2,1)}, u32[]{:S(2)}, u32[]{:S(2)}) async-start(bf16[4,2,2,256,128]{4,3,2,1,0:T(8,128)(2,1)} %pad_maximum_fusion), calls=%async_computation | async-start | bytes 2097152 | tf_op jit(solution)/shard_map/all_to_all | solution.py:453
  504.2 25.0 %collective-permute-start.46 = (bf16[2048,128]{1,0:T(8,128)(2,1)}, bf16[2048,128]{1,0:T(8,128)(2,1)S(1)}, u32[]{:S(2)}, u32[]{:S(2)}) collective-permute-start(bf16[2048,128]{1,0:T(8,128)(2,1)} %collective-permute-done.45.refs_9_), channel_id=1, source_target_pairs={{8,0},{12,4},{9,1},{13,5},{10,2},{14,6},{11,3},{15,7}} | collective-permute-start | bytes 1572872 | tf_op jit(solution)/shard_map/ppermute | solution.py:347
  566.0 26.4 %all-to-all-start.3 = ((bf16[4,2,2,256,128]{4,3,2,1,0:T(8,128)(2,1)}), bf16[4,2,2,256,128]{4,3,2,1,0:T(8,128)(2,1)S(1)}, u32[]{:S(2)}, u32[]{:S(2)}) async-start(bf16[4,2,2,256,128]{4,3,2,1,0:T(8,128)(2,1)} %pad_maximum_fusion.3), calls=%async_computation.3 | async-start | bytes 2097152 | tf_op jit(solution)/shard_map/all_to_all | solution.py:453
  (66 other events, 876.9 us)

commit v2 on v1

--- a/solution.py
+++ b/solution.py
@@ -138,72 +138,87 @@
     return outputs.reshape(row_count, heads_here * HD)
 
 
-def project_kernel(chunks, off_ref, *refs):
-    x_refs = refs[:4]
-    w_refs = refs[4 : 4 + 7 * chunks]
-    bias_ref, cos_ref, sin_ref, out_ref, w_buf, sems = refs[4 + 7 * chunks :]
-
-    @pl.when(pl.program_id(0) == 0)
-    def _():
-        for i in range(4):
-            for c in range(chunks):
-                for place in range(7):
-
-                    @pl.when(off_ref[i] == place - 3)
-                    def _(i=i, c=c, place=place):
-                        pltpu.make_async_copy(
-                            w_refs[7 * c + place],
-                            w_buf.at[i, :, pl.ds(c * HD, HD)],
-                            sems.at[i, c],
-                        ).start()
-
-        for i in range(4):
-            for c in range(chunks):
-                pltpu.make_async_copy(
-                    w_refs[7 * c], w_buf.at[i, :, pl.ds(c * HD, HD)], sems.at[i, c]
-                ).wait()
-
+def pick_weights(off_ref, w_refs, w_buf, sems):
+    for i in range(4):
+        for place in range(7):
+
+            @pl.when(off_ref[i] == place - 3)
+            def _(i=i, place=place):
+                pltpu.make_async_copy(w_refs[place], w_buf.at[i], sems.at[i]).start()
+
+    for i in range(4):
+        pltpu.make_async_copy(w_refs[0], w_buf.at[i], sems.at[i]).wait()
+
+
+def product(x_refs, w_buf):
     total = jnp.dot(x_refs[0][...], w_buf[0], preferred_element_type=jnp.float32)
     for i in range(1, 4):
         total += jnp.dot(x_refs[i][...], w_buf[i], preferred_element_type=jnp.float32)
-    for c in range(chunks):
-        part = total[:, c * HD : (c + 1) * HD] + bias_ref[:, c * HD : (c + 1) * HD]
-        rot = part * cos_ref[c] + pltpu.roll(part, HD // 2, 1) * sin_ref[c]
-        out_ref[:, c * HD : (c + 1) * HD] = rot.astype(out_ref.dtype)
-
-
-def project(off, x_blocks, w_places, bias, cos, sin):
-    chunks = len(w_places)
+    return total
+
+
+def partial_kernel(off_ref, *refs):
+    x_refs, w_refs, (out_ref, w_buf, sems) = refs[:4], refs[4:11], refs[11:]
+
+    @pl.when(pl.program_id(0) == 0)
+    def _():
+        pick_weights(off_ref, w_refs, w_buf, sems)
+
+    out_ref[...] = product(x_refs, w_buf)
+
+
+def project_kernel(ropes, off_ref, *refs):
+    x_refs, w_refs = refs[:4], refs[4:11]
+    part_ref, bias_ref, cos_ref, sin_ref, out_ref, w_buf, sems = refs[11:]
+
+    @pl.when(pl.program_id(0) == 0)
+    def _():
+        pick_weights(off_ref, w_refs, w_buf, sems)
+
+    total = product(x_refs, w_buf) + part_ref[...] + bias_ref[...]
+    for c, rope in enumerate(ropes):
+        part = total[:, c * HD : (c + 1) * HD]
+        if rope:
+            part = part * cos_ref[...] + pltpu.roll(part, HD // 2, 1) * sin_ref[...]
+        out_ref[:, c * HD : (c + 1) * HD] = part.astype(out_ref.dtype)
+
+
+def projection(off, x_blocks, places, finish=None):
     rows, feats = x_blocks[0].shape
-    tile = min(256, rows)
-    flat = [w for places in w_places for w in places]
+    columns = places[0].shape[1]
+    tile = min(512, rows)
+    wide = pl.BlockSpec((tile, columns), lambda r, off: (r, 0))
+    in_specs = [pl.BlockSpec((tile, feats), lambda r, off: (r, 0))] * 4
+    in_specs += [pl.BlockSpec(memory_space=pl.ANY)] * 7
+    operands = [*x_blocks, *places]
+    body, out_type = partial_kernel, jnp.float32
+    if finish is not None:
+        ropes, *rest = finish
+        table = pl.BlockSpec((tile, HD), lambda r, off: (r, 0))
+        in_specs += [wide, pl.BlockSpec((1, columns), lambda r, off: (0, 0)), table, table]
+        operands += rest
+        body, out_type = functools.partial(project_kernel, ropes), jnp.bfloat16
     grid_spec = pltpu.PrefetchScalarGridSpec(
         num_scalar_prefetch=1,
         grid=(rows // tile,),
-        in_specs=[pl.BlockSpec((tile, feats), lambda r, off: (r, 0))] * 4
-        + [pl.BlockSpec(memory_space=pl.ANY)] * len(flat)
-        + [
-            pl.BlockSpec((1, chunks * HD), lambda r, off: (0, 0)),
-            pl.BlockSpec((chunks, tile, HD), lambda r, off: (0, r, 0)),
-            pl.BlockSpec((chunks, tile, HD), lambda r, off: (0, r, 0)),
+        in_specs=in_specs,
+        out_specs=wide,
+        scratch_shapes=[
+            pltpu.VMEM((4, feats, columns), jnp.bfloat16),
+            pltpu.SemaphoreType.DMA((4,)),
         ],
-        out_specs=pl.BlockSpec((tile, chunks * HD), lambda r, off: (r, 0)),
-        scratch_shapes=[
-            pltpu.VMEM((4, feats, chunks * HD), jnp.bfloat16),
-            pltpu.SemaphoreType.DMA((4, chunks)),
-        ],
     )
     return pl.pallas_call(
-        functools.partial(project_kernel, chunks),
+        body,
         grid_spec=grid_spec,
-        out_shape=jax.ShapeDtypeStruct((rows, chunks * HD), jnp.bfloat16),
-        compiler_params=pltpu.CompilerParams(vmem_limit_bytes=40 * 2**20),
+        out_shape=jax.ShapeDtypeStruct((rows, columns), out_type),
+        compiler_params=pltpu.CompilerParams(vmem_limit_bytes=32 * 2**20),
         cost_estimate=pl.CostEstimate(
-            flops=2 * rows * 4 * feats * chunks * HD,
-            bytes_accessed=8 * rows * feats + 8 * feats * chunks * HD,
+            flops=8 * rows * feats * columns,
+            bytes_accessed=8 * rows * feats + 8 * feats * columns + 4 * rows * columns,
             transcendentals=0,
         ),
-    )(off, *x_blocks, *flat, bias, cos, sin)
+    )(off, *operands)
 
 
 def attend_kernel(heads, slot, window, start_ref, len_ref, q_ref, k_ref, v_ref, out_ref):
@@ -328,8 +343,11 @@
     t = lax.axis_index("tensor")
     row_count, feature_count = rollout_states.shape
     slot = 2 * row_count // learners
-    half = w_query.shape[1] // 2
-    heads = half // HD
+    half = feature_count // 2
+    middle = row_count // 2
+
+    def after(array, *others):
+        return lax.optimization_barrier((array, *others))[0]
 
     def swap_x(array):
         return lax.ppermute(array, "dp", [(i, i ^ 1) for i in range(learners)])
@@ -346,8 +364,46 @@
     def down(array, first):
         return lax.ppermute(array, "dp", [(i, i - 2) for i in range(2, learners - 2 * first)])
 
-    def by_x(at_zero, at_one):
-        return jnp.where(x == 0, at_zero, at_one)
+    chunks = [jnp.concatenate([w_key, w_value], axis=1)]
+    edges = [0, 2, 4, 6, 7, 8]
+    for low, high in zip(edges, edges[1:]):
+        chunks.append(w_query[:, low * HD : high * HD])
+    places, marks = [], []
+    for c, own in enumerate(chunks):
+        if c >= 2:
+            own = after(own, *marks[c - 2][-1])
+        ups, downs = [own], [own]
+        for step in range(line - 1):
+            ups.append(up(ups[-1], step))
+            downs.append(down(downs[-1], step))
+        places.append(ups[:0:-1] + downs)
+        marks.append(list(zip(ups[1:], downs[1:])))
+
+    widened = rollout_states.astype(jnp.float32)
+    squares = jnp.sum(widened * widened, axis=-1)
+    squares = squares + swap_core(squares)
+    squares = squares + swap_y(squares)
+    scale = lax.rsqrt(squares[:, None] / (4 * feature_count) + norm_eps)
+
+    def normed(first):
+        part = lax.dynamic_slice_in_dim(rollout_states, first, half, 1).astype(jnp.float32)
+        gain = lax.dynamic_slice_in_dim(norm_gain, t * feature_count + first, half, 0)
+        return (part * scale * gain[None, :]).astype(jnp.bfloat16)
+
+    own, give = normed(x * half), normed((1 - x) * half)
+
+    near_a = swap_x(give[:middle])
+    own_a = swap_y(own[:middle])
+    near_b = swap_x(after(give[middle:], near_a, *marks[0][0]))
+    diag_a = swap_y(after(near_a, own_a, *marks[0][0]))
+    near = jnp.concatenate([near_a, near_b], axis=0)
+    diag_b = swap_y(after(near_b, diag_a, *marks[0][1]))
+    own_b = swap_y(after(own[middle:], diag_b, *marks[1][1]))
+    diag = jnp.concatenate([diag_a, diag_b], axis=0)
+    own_y = jnp.concatenate([own_a, own_b], axis=0)
+    own_x = [own, swap_core(own), own_y, swap_core(own_y)]
+    near_x = [near, swap_core(near), diag, swap_core(diag)]
+    off = jnp.stack([(t ^ i) - z for i in range(4)]).astype(jnp.int32)
 
     lengths = seq_lengths.reshape(learners, learners)
     dests = seq_dest.reshape(learners, learners)
@@ -355,110 +411,45 @@
     starts = jnp.cumsum(lengths, axis=1) - lengths
     peer_ids = jnp.arange(learners, dtype=jnp.int32)
     rows = jnp.arange(row_count, dtype=jnp.int32)
-
-    def sends(rollout):
-        length = lax.dynamic_index_in_dim(lengths, rollout, 0, keepdims=False)
-        start = lax.dynamic_index_in_dim(starts, rollout, 0, keepdims=False)
-        dest = lax.dynamic_index_in_dim(dests, rollout, 0, keepdims=False)
-        match = (dest[None, :] == peer_ids[:, None]).astype(jnp.int32)
-        inside = (rows[:, None] >= start[None, :]) & (rows[:, None] < (start + length)[None, :])
-        position = rows - jnp.sum(inside.astype(jnp.int32) * start[None, :], axis=1)
-        cosine, sine = rope_tables(position)
-        cosine = jnp.concatenate([cosine, cosine], axis=1)
-        sine = jnp.concatenate([-sine, sine], axis=1)
-        return (
-            jnp.sum(match * start[None, :], axis=1),
-            jnp.sum(match * length[None, :], axis=1),
-            cosine,
-            sine,
-        )
-
-    def receives(learner):
-        matched = (dests == learner).astype(jnp.int32)
-        return jnp.sum(matched * offsets, axis=1), jnp.sum(matched * lengths, axis=1)
-
-    other = me ^ 1
-    own_table, other_table = sends(me), sends(other)
-
-    kv_mine, kv_give = by_x(w_key, w_value), by_x(w_value, w_key)
-    q_mine = lax.dynamic_slice_in_dim(w_query, x * half, half, 1)
-    q_give = lax.dynamic_slice_in_dim(w_query, (1 - x) * half, half, 1)
-    places = []
-    for c in range(heads + 1):
+    length = lax.dynamic_index_in_dim(lengths, me, 0, keepdims=False)
+    start = lax.dynamic_index_in_dim(starts, me, 0, keepdims=False)
+    dest = lax.dynamic_index_in_dim(dests, me, 0, keepdims=False)
+    match = (dest[None, :] == peer_ids[:, None]).astype(jnp.int32)
+    send_start = jnp.sum(match * start[None, :], axis=1)
+    send_length = jnp.sum(match * length[None, :], axis=1)
+    inside = (rows[:, None] >= start[None, :]) & (rows[:, None] < (start + length)[None, :])
+    position = rows - jnp.sum(inside.astype(jnp.int32) * start[None, :], axis=1)
+    cosine, sine = rope_tables(position)
+    cosine = jnp.concatenate([cosine, cosine], axis=1)
+    sine = jnp.concatenate([-sine, sine], axis=1)
+    matched = (dests == me).astype(jnp.int32)
+    run_start = jnp.sum(matched * offsets, axis=1)[None, :]
+    run_length = jnp.sum(matched * lengths, axis=1)[None, :]
+
+    biases = [jnp.concatenate([b_key, b_value])]
+    for low, high in zip(edges, edges[1:]):
+        biases.append(b_query[low * HD : high * HD])
+    parts = []
+    for c, own_places in enumerate(places):
+        near_blocks = near_x
+        if parts:
+            near_blocks = [after(near_x[0], parts[-1])] + near_x[1:]
+        parts.append(projection(off, near_blocks, own_places))
+    columns = []
+    for c, own_places in enumerate(places):
+        ropes = (True, False) if c == 0 else (True,) * (own_places[0].shape[1] // HD)
+        got = swap_x(parts[c])
+        rot = projection(
+            off, own_x, own_places, (ropes, got, biases[c][None, :], cosine, sine)
+        )
         if c == 0:
-            mine, give = kv_mine, kv_give
-        else:
-            mine, give = (w[:, (c - 1) * HD : c * HD] for w in (q_mine, q_give))
-        got = swap_x(give)
-        own = by_x(jnp.concatenate([mine, got], axis=0), jnp.concatenate([got, mine], axis=0))
-        ups, downs = [own], [own]
-        for step in range(line - 1):
-            ups.append(up(ups[-1], step))
-            downs.append(down(downs[-1], step))
-        places.append(ups[:0:-1] + downs)
-    bias_kv = by_x(b_key, b_value)
-    bias_q = lax.dynamic_slice_in_dim(b_query, x * half, half, 0)
-    bias = jnp.concatenate([bias_kv, bias_q])[None, :]
-
-    widened = rollout_states.astype(jnp.float32)
-    squares = jnp.sum(widened * widened, axis=-1)
-    squares = squares + swap_core(squares)
-    squares = squares + swap_y(squares)
-    statistic = squares[:, None] / (4 * feature_count)
-    gain = lax.dynamic_slice_in_dim(norm_gain, t * feature_count, feature_count, 0)
-    normed = (widened * lax.rsqrt(statistic + norm_eps) * gain[None, :]).astype(jnp.bfloat16)
-
-    middle = row_count // 2
-    own_y = swap_y(normed)
-    near = swap_x(normed)
-    near_y = jnp.concatenate([swap_y(near[:middle]), swap_x(own_y[middle:])], axis=0)
-    own_x = [normed, swap_core(normed), own_y, swap_core(own_y)]
-    near_x = [near, swap_core(near), near_y, swap_core(near_y)]
-    off = jnp.stack([(t ^ i) - z for i in range(4)]).astype(jnp.int32)
-
-    def tables(table):
-        cosine, sine = table[2], table[3]
-        cos_kv = by_x(cosine, jnp.ones_like(cosine))
-        sin_kv = by_x(sine, jnp.zeros_like(sine))
-        return cos_kv[None], sin_kv[None], cosine[None], sine[None]
-
-    def one(x_blocks, table, c):
-        cos_kv, sin_kv, cosine, sine = table
-        pick = (cos_kv, sin_kv) if c == 0 else (cosine, sine)
-        return project(off, x_blocks, places[c : c + 1], bias[:, c * HD : (c + 1) * HD], *pick)
-
-    own_tables, other_tables = tables(own_table), tables(other_table)
-    own_kv = one(own_x, own_tables, 0)
-    other_kv = one(near_x, other_tables, 0)
-    own_kv_got, other_kv_got = swap_x(other_kv), swap_x(own_kv)
-    own_k, own_v = by_x(own_kv, own_kv_got), by_x(own_kv_got, own_kv)
-    other_k, other_v = by_x(other_kv, other_kv_got), by_x(other_kv_got, other_kv)
-
-    z_ids = jnp.arange(line, dtype=jnp.int32)
-    order = jnp.stack([2 * z_ids + x, 2 * z_ids + 1 - x], axis=1).reshape(-1)
-    at_zero, at_one = receives(2 * z), receives(2 * z + 1)
-    run_start = jnp.stack([at_zero[0][order], at_one[0][order]])
-    run_length = jnp.stack([at_zero[1][order], at_one[1][order]])
-    groups = [[2 * i + j for i in range(line)] for j in range(2)]
-
-    kept, got = [], []
-    for c in range(1, heads + 1):
-        own_q = one(own_x, own_tables, c)
-        other_q = one(near_x, other_tables, c)
-        own_slots = attend(own_table[0], own_table[1], own_q, own_k, own_v, slot)
-        other_slots = attend(other_table[0], other_table[1], other_q, other_k, other_v, slot)
-        outgoing = jnp.stack(
-            [own_slots.reshape(line, 2, slot, HD), other_slots.reshape(line, 2, slot, HD)], axis=1
-        )
-        incoming = lax.all_to_all(
-            outgoing, "dp", split_axis=0, concat_axis=0, tiled=True, axis_index_groups=groups
-        )
-        placed = place(run_start, run_length, incoming.reshape(2 * line, 2, slot, HD), row_count)
-        kept.append(by_x(placed[0], placed[1]))
-        got.append(swap_x(by_x(placed[1], placed[0])))
-    kept = jnp.concatenate(kept, axis=1)
-    got = jnp.concatenate(got, axis=1)
-    return by_x(jnp.concatenate([kept, got], axis=1), jnp.concatenate([got, kept], axis=1))
+            key, value = rot[:, :HD], rot[:, HD:]
+            continue
+        outgoing = attend(send_start, send_length, rot, key, value, slot)
+        incoming = lax.all_to_all(outgoing, "dp", split_axis=0, concat_axis=0, tiled=True)
+        placed = place(run_start, run_length, incoming[:, None], row_count)
+        columns.append(placed[0])
+    return jnp.concatenate(columns, axis=1)
 
 
 def solution(mesh):

time: 612 us -> 501 us (0.82)
  waiting for transfers between devices: 283 us -> 193 us
  local copies, waits for them, and re-layouts: 19.4 us -> 58.3 us
  Pallas kernels: 171 us -> 137 us
  other arithmetic: 33.2 us -> 11.8 us
    ppermute x13 -> x8, waiting for transfers between devices: 146 us -> 79.7 us  [swap_x(): return lax.ppermute(array, 'dp', [(i, i ^ 1) for i in range(learners)])]
    unnamed x94 -> x194, local copies, waits for them, and re-layouts: 4.69 us -> 48.9 us
    pallas_call x10 -> x12, Pallas kernels: 105 us -> 79.5 us  [projection(): pl.pallas_call(body, grid_spec=grid_spec, out_shape=jax.ShapeDtypeStruct(...]
    ppermute x15 -> x18, waiting for transfers between devices: 109 us -> 88.6 us  [down(): lax.ppermute(array, 'dp', [(i, i - 2) for i in range(2, learners - 2 * fi...]
    ppermute x15 -> x18, waiting for transfers between devices: 19.2 us -> 8.07 us  [up(): lax.ppermute(array, 'dp', [(i, i + 2) for i in range(2 * first, learners...]
    select_n x17 -> x0, other arithmetic: 11.1 us -> none  [the longest x16 11.1 us: by_x(): return jnp.where(x == 0, at_zero, at_one)]
    pallas_call x8 -> x5, Pallas kernels: 55.8 us -> 47.2 us  [attend(): pl.pallas_call(functools.partial(attend_kernel, heads, slot, window), gri...]
    all_to_all x4 -> x5, waiting for transfers between devices: 7.18 us -> 14.8 us  [local_line(): lax.all_to_all(outgoing, 'dp', split_axis=0, concat_axis=0, tiled=True)]
  transfers between devices with their start and end apart: 55 -> 59, of which waited for: 21 -> 21; matrix products, arithmetic and copies ran while one was open for 7% -> 5% of each run, Pallas kernels for 28% -> 27%
where the time goes in v2:
time: 501 us; the launch traced here: 498 us
  waiting for transfers between devices  193 us (39%)
  Pallas kernels  137 us (27%)
  starting transfers between devices  97.7 us (20%)
  local copies, waits for them, and re-layouts  58.3 us (12%)
  other arithmetic  11.8 us (2%)
    ppermute x18, waiting for transfers between devices, down(): lax.ppermute(array, 'dp', [(i, i - 2) for i in range(2, learners - 2 * fi...  88.6 us
    ppermute x8, waiting for transfers between devices, swap_x(): return lax.ppermute(array, 'dp', [(i, i ^ 1) for i in range(learners)])  79.7 us
    pallas_call x12, Pallas kernels, projection(): pl.pallas_call(body, grid_spec=grid_spec, out_shape=jax.ShapeDtypeStruct(...  79.5 us
    unnamed x194, local copies, waits for them, and re-layouts  48.9 us
    pallas_call x5, Pallas kernels, attend(): pl.pallas_call(functools.partial(attend_kernel, heads, slot, window), gri...  47.2 us
    ppermute x18, starting transfers between devices, up(): lax.ppermute(array, 'dp', [(i, i + 2) for i in range(2 * first, learners...  29.7 us
    all_to_all x5, starting transfers between devices, local_line(): lax.all_to_all(outgoing, 'dp', split_axis=0, concat_axis=0, tiled=True)  26 us
    ppermute x18, starting transfers between devices, down(): lax.ppermute(array, 'dp', [(i, i - 2) for i in range(2, learners - 2 * fi...  23.3 us
  transfers between devices with their start and end apart: 59, of which 21 were waited for; matrix products, arithmetic and copies ran while one was open for 5% of the time, Pallas kernels for 27%

profile of v2, /device:TPU:0, one launch (start us, length us, event | category | flops | bytes accessed | tf_op | source)
XLA Modules:
  0.0 498.5 jit_solution(10311654836774909530)
XLA Ops:
  29.8 8.0 %collective-permute-done.12.refs_6_ = bf16[1024,256]{1,0:T(8,128)(2,1)S(1)} collective-permute-done((bf16[1024,256]{1,0:T(8,128)(2,1)S(1)}, bf16[1024,256]{1,0:T(8,128)(2,1)S(1)}, u32[]{:S(2)}, u32[]{:S(2)}) %collective-permute-start.12) | collective-permute-done | bytes 524320 | tf_op jit(solution)/shard_map/ppermute | solution.py:362
  39.2 6.3 %collective-permute-done.4 = bf16[512,1024]{1,0:T(8,128)(2,1)S(1)} collective-permute-done((bf16[512,1024]{1,0:T(8,128)(2,1)S(1)}, bf16[512,1024]{1,0:T(8,128)(2,1)S(1)}, u32[]{:S(2)}, u32[]{:S(2)}) %collective-permute-start.4) | collective-permute-done | bytes 1048608 | tf_op jit(solution)/shard_map/ppermute | solution.py:353
  56.9 11.6 %collective-permute-done.15.refs_9_ = bf16[1024,256]{1,0:T(8,128)(2,1)S(1)} collective-permute-done((bf16[1024,256]{1,0:T(8,128)(2,1)S(1)}, bf16[1024,256]{1,0:T(8,128)(2,1)S(1)}, u32[]{:S(2)}, u32[]{:S(2)}) %collective-permute-start.15) | collective-permute-done | bytes 524320 | tf_op jit(solution)/shard_map/ppermute | solution.py:365
  72.9 6.8 %collective-permute-done.23.refs_10_ = bf16[1024,256]{1,0:T(8,128)(2,1)S(1)} collective-permute-done((bf16[1024,256]{1,0:T(8,128)(2,1)S(1)}, bf16[1024,256]{1,0:T(8,128)(2,1)S(1)}, u32[]{:S(2)}, u32[]{:S(2)}) %collective-permute-start.23) | collective-permute-done | bytes 524320 | tf_op jit(solution)/shard_map/ppermute | solution.py:365
  96.0 6.2 %collective-permute-done.29.refs_8_ = bf16[1024,256]{1,0:T(8,128)(2,1)S(1)} collective-permute-done((bf16[1024,256]{1,0:T(8,128)(2,1)S(1)}, bf16[1024,256]{1,0:T(8,128)(2,1)S(1)}, u32[]{:S(2)}, u32[]{:S(2)}) %collective-permute-start.29) | collective-permute-done | bytes 524320 | tf_op jit(solution)/shard_map/ppermute | solution.py:365
  104.2 9.2 %collective-permute-done.36.refs_8_ = bf16[1024,256]{1,0:T(8,128)(2,1)S(1)} collective-permute-done((bf16[1024,256]{1,0:T(8,128)(2,1)S(1)}, bf16[1024,256]{1,0:T(8,128)(2,1)S(1)}, u32[]{:S(2)}, u32[]{:S(2)}) %collective-permute-start.36) | collective-permute-done | bytes 524320 | tf_op jit(solution)/shard_map/ppermute | solution.py:365
  118.5 6.3 %collective-permute-done.30.refs_9_ = bf16[1024,256]{1,0:T(8,128)(2,1)} collective-permute-done((bf16[1024,256]{1,0:T(8,128)(2,1)S(1)}, bf16[1024,256]{1,0:T(8,128)(2,1)}, u32[]{:S(2)}, u32[]{:S(2)}) %collective-permute-start.30) | collective-permute-done | bytes 524320 | tf_op jit(solution)/shard_map/ppermute | solution.py:365
  129.7 6.2 %collective-permute-done.37.refs_9_ = bf16[1024,256]{1,0:T(8,128)(2,1)S(1)} collective-permute-done((bf16[1024,256]{1,0:T(8,128)(2,1)S(1)}, bf16[1024,256]{1,0:T(8,128)(2,1)S(1)}, u32[]{:S(2)}, u32[]{:S(2)}) %collective-permute-start.37) | collective-permute-done | bytes 524320 | tf_op jit(solution)/shard_map/ppermute | solution.py:365
  146.3 9.8 %collective-permute-done.38.refs_10_ = bf16[1024,256]{1,0:T(8,128)(2,1)} collective-permute-done((bf16[1024,256]{1,0:T(8,128)(2,1)}, bf16[1024,256]{1,0:T(8,128)(2,1)}, u32[]{:S(2)}, u32[]{:S(2)}) %collective-permute-start.38) | collective-permute-done | bytes 524320 | tf_op jit(solution)/shard_map/ppermute | solution.py:365
  173.4 10.2 %collective-permute-done.44.refs_9_ = bf16[1024,128]{1,0:T(8,128)(2,1)} collective-permute-done((bf16[1024,128]{1,0:T(8,128)(2,1)}, bf16[1024,128]{1,0:T(8,128)(2,1)}, u32[]{:S(2)}, u32[]{:S(2)}) %collective-permute-start.44) | collective-permute-done | bytes 262176 | tf_op jit(solution)/shard_map/ppermute | solution.py:365
  189.9 7.0 %shard_map.109 = f32[1024,256]{1,0:T(8,128)S(1)} custom-call(s32[4]{0:T(128)S(1)} %pad_add_fusion.off_ref, bf16[1024,1024]{1,0:T(8,128)(2,1)} %constant_dynamic-update-slice_fusion.4.refs_0_, bf16[1024,1024]{1,0:T(8,128)(2,1)} %collective-permute-done.20.refs_1_, bf16[1024,1024]{1,0:T(8,128)(2,1)} %constant_dynamic-update-slice_fusion.6.refs_2_, ...), custom_call_target="tpu_custom_call" | custom-call | flops 2147483648 | bytes 11534336 | tf_op jit(solution)/shard_map/pallas_call | solution.py:211
  198.6 6.4 %shard_map.110 = f32[1024,256]{1,0:T(8,128)} custom-call(s32[4]{0:T(128)S(1)} %pad_add_fusion.off_ref, bf16[1024,1024]{1,0:T(8,128)(2,1)} %constant_dynamic-update-slice_fusion.4.refs_0_, bf16[1024,1024]{1,0:T(8,128)(2,1)} %collective-permute-done.20.refs_1_, bf16[1024,1024]{1,0:T(8,128)(2,1)} %constant_dynamic-update-slice_fusion.6.refs_2_, ...), custom_call_target="tpu_custom_call" | custom-call | flops 2147483648 | bytes 11534336 | tf_op jit(solution)/shard_map/pallas_call | solution.py:211
  205.1 7.1 %shard_map.115 = f32[1024,256]{1,0:T(8,128)S(1)} custom-call(s32[4]{0:T(128)S(1)} %pad_add_fusion.off_ref, bf16[1024,1024]{1,0:T(8,128)(2,1)} %constant_dynamic-update-slice_fusion.4.refs_0_, bf16[1024,1024]{1,0:T(8,128)(2,1)} %collective-permute-done.20.refs_1_, bf16[1024,1024]{1,0:T(8,128)(2,1)} %constant_dynamic-update-slice_fusion.6.refs_2_, ...), custom_call_target="tpu_custom_call" | custom-call | flops 2147483648 | bytes 11534336 | tf_op jit(solution)/shard_map/pallas_call | solution.py:211
  213.2 6.9 %shard_map.119 = f32[1024,256]{1,0:T(8,128)S(1)} custom-call(s32[4]{0:T(128)S(1)} %pad_add_fusion.off_ref, bf16[1024,1024]{1,0:T(8,128)(2,1)} %constant_dynamic-update-slice_fusion.4.refs_0_, bf16[1024,1024]{1,0:T(8,128)(2,1)} %collective-permute-done.20.refs_1_, bf16[1024,1024]{1,0:T(8,128)(2,1)} %constant_dynamic-update-slice_fusion.6.refs_2_, ...), custom_call_target="tpu_custom_call" | custom-call | flops 2147483648 | bytes 11534336 | tf_op jit(solution)/shard_map/pallas_call | solution.py:211
  225.9 6.8 %shard_map.123 = f32[1024,128]{1,0:T(8,128)S(1)} custom-call(s32[4]{0:T(128)S(1)} %pad_add_fusion.off_ref, bf16[1024,1024]{1,0:T(8,128)(2,1)} %constant_dynamic-update-slice_fusion.4.refs_0_, bf16[1024,1024]{1,0:T(8,128)(2,1)} %collective-permute-done.20.refs_1_, bf16[1024,1024]{1,0:T(8,128)(2,1)} %constant_dynamic-update-slice_fusion.6.refs_2_, ...), custom_call_target="tpu_custom_call" | custom-call | flops 1073741824 | bytes 9961472 | tf_op jit(solution)/shard_map/pallas_call | solution.py:211
  239.3 7.9 %collective-permute-done.51.refs_9_ = bf16[1024,128]{1,0:T(8,128)(2,1)} collective-permute-done((bf16[1024,128]{1,0:T(8,128)(2,1)S(1)}, bf16[1024,128]{1,0:T(8,128)(2,1)}, u32[]{:S(2)}, u32[]{:S(2)}) %collective-permute-start.51) | collective-permute-done | bytes 262176 | tf_op jit(solution)/shard_map/ppermute | solution.py:365
  248.5 6.5 %shard_map.124.q_ref = bf16[1024,128]{1,0:T(8,128)(2,1)S(1)} custom-call(s32[4]{0:T(128)S(1)} %pad_add_fusion.off_ref, bf16[1024,1024]{1,0:T(8,128)(2,1)S(1)} %get-tuple-element.36.refs_0_, bf16[1024,1024]{1,0:T(8,128)(2,1)} %collective-permute-done.2.refs_1_, bf16[1024,1024]{1,0:T(8,128)(2,1)} %constant_dynamic-update-slice_fusion.2.refs_2_, ...), custom_call_target="tpu_custom_call" | custom-call | flops 1073741824 | bytes 9961472 | tf_op jit(solution)/shard_map/pallas_call | solution.py:211
  255.0 6.6 %shard_map.112 = bf16[1024,256]{1,0:T(8,128)(2,1)S(1)} custom-call(s32[4]{0:T(128)S(1)} %pad_add_fusion.off_ref, bf16[1024,1024]{1,0:T(8,128)(2,1)S(1)} %get-tuple-element.36.refs_0_, bf16[1024,1024]{1,0:T(8,128)(2,1)} %collective-permute-done.2.refs_1_, bf16[1024,1024]{1,0:T(8,128)(2,1)} %constant_dynamic-update-slice_fusion.2.refs_2_, ...), custom_call_target="tpu_custom_call" | custom-call | flops 2147483648 | bytes 11534336 | tf_op jit(solution)/shard_map/pallas_call | solution.py:211
  261.7 7.0 %shard_map.125 = bf16[8,256,128]{2,1,0:T(8,128)(2,1)S(1)} custom-call(s32[8]{0:T(128)S(1)} %get-tuple-element.34.start_ref, s32[8]{0:T(128)S(1)} %get-tuple-element.33.len_ref, bf16[1024,128]{1,0:T(8,128)(2,1)S(1)} %shard_map.124.q_ref, bf16[1024,128]{1,0:T(8,128)(2,1)S(1)} %get-tuple-element.47.k_ref, bf16[1024,128]{1,0:T(8,128)(2,1)S(1)} %get-tuple-element.46.v_ref), custom_call_target="tpu_custom_call" | custom-call | flops 469762048 | bytes 1310720 | tf_op jit(solution)/shard_map/pallas_call | solution.py:272
  278.6 6.8 %shard_map.127 = f32[1024,128]{1,0:T(8,128)S(1)} custom-call(s32[4]{0:T(128)S(1)} %pad_add_fusion.off_ref, bf16[1024,1024]{1,0:T(8,128)(2,1)} %constant_dynamic-update-slice_fusion.4.refs_0_, bf16[1024,1024]{1,0:T(8,128)(2,1)} %collective-permute-done.20.refs_1_, bf16[1024,1024]{1,0:T(8,128)(2,1)} %constant_dynamic-update-slice_fusion.6.refs_2_, ...), custom_call_target="tpu_custom_call" | custom-call | flops 1073741824 | bytes 9961472 | tf_op jit(solution)/shard_map/pallas_call | solution.py:211
  287.6 12.8 %collective-permute-done.53.refs_11_ = f32[1024,128]{1,0:T(8,128)S(1)} collective-permute-done((f32[1024,128]{1,0:T(8,128)S(1)}, f32[1024,128]{1,0:T(8,128)S(1)}, u32[]{:S(2)}, u32[]{:S(2)}) %collective-permute-start.53) | collective-permute-done | bytes 524320 | tf_op jit(solution)/shard_map/ppermute | solution.py:353
  300.3 6.5 %shard_map.128.q_ref = bf16[1024,128]{1,0:T(8,128)(2,1)S(1)} custom-call(s32[4]{0:T(128)S(1)} %pad_add_fusion.off_ref, bf16[1024,1024]{1,0:T(8,128)(2,1)S(1)} %get-tuple-element.36.refs_0_, bf16[1024,1024]{1,0:T(8,128)(2,1)} %collective-permute-done.2.refs_1_, bf16[1024,1024]{1,0:T(8,128)(2,1)} %constant_dynamic-update-slice_fusion.2.refs_2_, ...), custom_call_target="tpu_custom_call" | custom-call | flops 1073741824 | bytes 9961472 | tf_op jit(solution)/shard_map/pallas_call | solution.py:211
  306.8 7.0 %shard_map.129 = bf16[8,256,128]{2,1,0:T(8,128)(2,1)S(1)} custom-call(s32[8]{0:T(128)S(1)} %get-tuple-element.34.start_ref, s32[8]{0:T(128)S(1)} %get-tuple-element.33.len_ref, bf16[1024,128]{1,0:T(8,128)(2,1)S(1)} %shard_map.128.q_ref, bf16[1024,128]{1,0:T(8,128)(2,1)S(1)} %copy-done.77, bf16[1024,128]{1,0:T(8,128)(2,1)S(1)} %copy-done.72), custom_call_target="tpu_custom_call" | custom-call | flops 469762048 | bytes 1310720 | tf_op jit(solution)/shard_map/pallas_call | solution.py:272
  314.7 5.9 %all-to-all-start.4 = ((bf16[8,256,128]{2,1,0:T(8,128)(2,1)}), bf16[8,256,128]{2,1,0:T(8,128)(2,1)}, u32[]{:S(2)}, u32[]{:S(2)}) async-start(bf16[8,256,128]{2,1,0:T(8,128)(2,1)} %copy-done.70), calls=%async_computation.4 | async-start | bytes 1048576 | tf_op jit(solution)/shard_map/all_to_all | solution.py:449
  334.6 10.8 %shard_map.113 = bf16[8,256,256]{2,1,0:T(8,128)(2,1)S(1)} custom-call(s32[8]{0:T(128)S(1)} %get-tuple-element.34.start_ref, s32[8]{0:T(128)S(1)} %get-tuple-element.33.len_ref, bf16[1024,256]{1,0:T(8,128)(2,1)S(1)} %shard_map.111.q_ref, bf16[1024,128]{1,0:T(8,128)(2,1)S(1)} %copy-done.78, bf16[1024,128]{1,0:T(8,128)(2,1)S(1)} %copy-done.73), custom_call_target="tpu_custom_call" | custom-call | flops 939524096 | bytes 2097152 | tf_op jit(solution)/shard_map/pallas_call | solution.py:272
  354.0 28.3 %collective-permute-done.32.refs_11_ = f32[1024,256]{1,0:T(8,128)S(1)} collective-permute-done((f32[1024,256]{1,0:T(8,128)}, f32[1024,256]{1,0:T(8,128)S(1)}, u32[]{:S(2)}, u32[]{:S(2)}) %collective-permute-start.32) | collective-permute-done | bytes 1048608 | tf_op jit(solution)/shard_map/ppermute | solution.py:353
  385.5 6.7 %shard_map.116.q_ref = bf16[1024,256]{1,0:T(8,128)(2,1)S(1)} custom-call(s32[4]{0:T(128)S(1)} %pad_add_fusion.off_ref, bf16[1024,1024]{1,0:T(8,128)(2,1)S(1)} %get-tuple-element.36.refs_0_, bf16[1024,1024]{1,0:T(8,128)(2,1)} %collective-permute-done.2.refs_1_, bf16[1024,1024]{1,0:T(8,128)(2,1)} %constant_dynamic-update-slice_fusion.2.refs_2_, ...), custom_call_target="tpu_custom_call" | custom-call | flops 2147483648 | bytes 11534336 | tf_op jit(solution)/shard_map/pallas_call | solution.py:211
  392.2 10.8 %shard_map.117 = bf16[8,256,256]{2,1,0:T(8,128)(2,1)S(1)} custom-call(s32[8]{0:T(128)S(1)} %get-tuple-element.34.start_ref, s32[8]{0:T(128)S(1)} %get-tuple-element.33.len_ref, bf16[1024,256]{1,0:T(8,128)(2,1)S(1)} %shard_map.116.q_ref, bf16[1024,128]{1,0:T(8,128)(2,1)S(1)} %copy-done.79, bf16[1024,128]{1,0:T(8,128)(2,1)S(1)} %copy-done.74), custom_call_target="tpu_custom_call" | custom-call | flops 939524096 | bytes 2097152 | tf_op jit(solution)/shard_map/pallas_call | solution.py:272
  410.6 31.3 %collective-permute-done.39.refs_11_ = f32[1024,256]{1,0:T(8,128)S(1)} collective-permute-done((f32[1024,256]{1,0:T(8,128)}, f32[1024,256]{1,0:T(8,128)S(1)}, u32[]{:S(2)}, u32[]{:S(2)}) %collective-permute-start.39) | collective-permute-done | bytes 1048608 | tf_op jit(solution)/shard_map/ppermute | solution.py:353
  447.1 6.6 %shard_map.120.q_ref = bf16[1024,256]{1,0:T(8,128)(2,1)S(1)} custom-call(s32[4]{0:T(128)S(1)} %pad_add_fusion.off_ref, bf16[1024,1024]{1,0:T(8,128)(2,1)S(1)} %get-tuple-element.36.refs_0_, bf16[1024,1024]{1,0:T(8,128)(2,1)} %collective-permute-done.2.refs_1_, bf16[1024,1024]{1,0:T(8,128)(2,1)} %constant_dynamic-update-slice_fusion.2.refs_2_, ...), custom_call_target="tpu_custom_call" | custom-call | flops 2147483648 | bytes 11534336 | tf_op jit(solution)/shard_map/pallas_call | solution.py:211
  453.8 11.5 %shard_map.121 = bf16[8,256,256]{2,1,0:T(8,128)(2,1)} custom-call(s32[8]{0:T(128)S(1)} %get-tuple-element.34.start_ref, s32[8]{0:T(128)S(1)} %get-tuple-element.33.len_ref, bf16[1024,256]{1,0:T(8,128)(2,1)S(1)} %shard_map.120.q_ref, bf16[1024,128]{1,0:T(8,128)(2,1)S(1)} %copy-done.80, bf16[1024,128]{1,0:T(8,128)(2,1)S(1)} %copy-done.75), custom_call_target="tpu_custom_call" | custom-call | flops 939524096 | bytes 2097152 | tf_op jit(solution)/shard_map/pallas_call | solution.py:272
  479.4 14.8 %all-to-all-done.2 = bf16[8,256,256]{2,1,0:T(8,128)(2,1)S(1)} async-done(((bf16[8,256,256]{2,1,0:T(8,128)(2,1)}), bf16[8,256,256]{2,1,0:T(8,128)(2,1)S(1)}, u32[]{:S(2)}, u32[]{:S(2)}) %all-to-all-start.2) | async-done | bytes 1048608 | tf_op jit(solution)/shard_map/all_to_all | solution.py:449
  (334 shorter events, 194.3 us)
Async XLA Ops:
  5.1 22.7 %collective-permute-start.5 = (bf16[1024,256]{1,0:T(8,128)(2,1)}, bf16[1024,256]{1,0:T(8,128)(2,1)}, u32[]{:S(2)}, u32[]{:S(2)}) collective-permute-start(bf16[1024,256]{1,0:T(8,128)(2,1)} %constant_dynamic-update-slice_fusion.refs_7_), channel_id=1, source_target_pairs={{0,8},{4,12},{8,16},{12,20},{16,24},{20,28},{1,9},{5,13},{9,17},{1... | collective-permute-start | bytes 1572872 | tf_op jit(solution)/shard_map/ppermute | solution.py:362
  19.8 27.1 %collective-permute-start.3 = (bf16[512,1024]{1,0:T(8,128)(2,1)S(1)}, bf16[512,1024]{1,0:T(8,128)(2,1)S(1)}, u32[]{:S(2)}, u32[]{:S(2)}) collective-permute-start(bf16[512,1024]{1,0:T(8,128)(2,1)S(1)} %get-tuple-element.45), channel_id=1, source_target_pairs={{0,2},{1,3},{2,0},{3,1},{4,6},{5,7},{6,4},{7,5},{8,10},{9,11},{10,... | collective-permute-start | bytes 3145736 | tf_op jit(solution)/shard_map/ppermute | solution.py:356
  21.5 23.9 %collective-permute-start.4 = (bf16[512,1024]{1,0:T(8,128)(2,1)S(1)}, bf16[512,1024]{1,0:T(8,128)(2,1)S(1)}, u32[]{:S(2)}, u32[]{:S(2)}) collective-permute-start(bf16[512,1024]{1,0:T(8,128)(2,1)S(1)} %get-tuple-element.42), channel_id=1, source_target_pairs={{0,4},{4,0},{8,12},{12,8},{16,20},{20,16},{24,28},{28,24},{1,5},{5... | collective-permute-start | bytes 3145736 | tf_op jit(solution)/shard_map/ppermute | solution.py:353
  27.8 20.6 %collective-permute-start.14 = (bf16[1024,256]{1,0:T(8,128)(2,1)S(1)}, bf16[1024,256]{1,0:T(8,128)(2,1)S(1)}, u32[]{:S(2)}, u32[]{:S(2)}) collective-permute-start(bf16[1024,256]{1,0:T(8,128)(2,1)S(1)} %get-tuple-element.41.refs_7_), channel_id=1, source_target_pairs={{8,0},{12,4},{16,8},{20,12},{24,16},{28,20},{9,1},{13,5},{17,9},{2... | collective-permute-start | bytes 1572872 | tf_op jit(solution)/shard_map/ppermute | solution.py:365
  47.0 35.0 %collective-permute-start.7 = (bf16[512,1024]{1,0:T(8,128)(2,1)S(1)}, bf16[512,1024]{1,0:T(8,128)(2,1)S(1)}, u32[]{:S(2)}, u32[]{:S(2)}) collective-permute-start(bf16[512,1024]{1,0:T(8,128)(2,1)S(1)} %get-tuple-element.18), channel_id=1, source_target_pairs={{0,4},{4,0},{8,12},{12,8},{16,20},{20,16},{24,28},{28,24},{1,5},{5... | collective-permute-start | bytes 3145736 | tf_op jit(solution)/shard_map/ppermute | solution.py:353
  48.5 34.9 %collective-permute-start.8 = (bf16[512,1024]{1,0:T(8,128)(2,1)S(1)}, bf16[512,1024]{1,0:T(8,128)(2,1)S(1)}, u32[]{:S(2)}, u32[]{:S(2)}) collective-permute-start(bf16[512,1024]{1,0:T(8,128)(2,1)S(1)} %collective-permute-done.4), channel_id=1, source_target_pairs={{0,2},{1,3},{2,0},{3,1},{4,6},{5,7},{6,4},{7,5},{8,10},{9,11},{10,... | collective-permute-start | bytes 3145736 | tf_op jit(solution)/shard_map/ppermute | solution.py:356
  54.8 25.0 %collective-permute-start.23 = (bf16[1024,256]{1,0:T(8,128)(2,1)S(1)}, bf16[1024,256]{1,0:T(8,128)(2,1)S(1)}, u32[]{:S(2)}, u32[]{:S(2)}) collective-permute-start(bf16[1024,256]{1,0:T(8,128)(2,1)S(1)} %collective-permute-done.10.refs_9_), channel_id=1, source_target_pairs={{8,0},{12,4},{9,1},{13,5},{10,2},{14,6},{11,3},{15,7}} | collective-permute-start | bytes 1572872 | tf_op jit(solution)/shard_map/ppermute | solution.py:365
  82.0 20.2 %collective-permute-start.29 = (bf16[1024,256]{1,0:T(8,128)(2,1)S(1)}, bf16[1024,256]{1,0:T(8,128)(2,1)S(1)}, u32[]{:S(2)}, u32[]{:S(2)}) collective-permute-start(bf16[1024,256]{1,0:T(8,128)(2,1)S(1)} %get-tuple-element.23.refs_7_), channel_id=1, source_target_pairs={{8,0},{12,4},{16,8},{20,12},{24,16},{28,20},{9,1},{13,5},{17,9},{2... | collective-permute-start | bytes 1572872 | tf_op jit(solution)/shard_map/ppermute | solution.py:365
  83.3 43.8 %collective-permute-start.11 = (bf16[512,1024]{1,0:T(8,128)(2,1)S(1)}, bf16[512,1024]{1,0:T(8,128)(2,1)S(1)}, u32[]{:S(2)}, u32[]{:S(2)}) collective-permute-start(bf16[512,1024]{1,0:T(8,128)(2,1)S(1)} %collective-permute-done.7), channel_id=1, source_target_pairs={{0,2},{1,3},{2,0},{3,1},{4,6},{5,7},{6,4},{7,5},{8,10},{9,11},{10,... | collective-permute-start | bytes 3145736 | tf_op jit(solution)/shard_map/ppermute | solution.py:356
  93.2 20.2 %collective-permute-start.36 = (bf16[1024,256]{1,0:T(8,128)(2,1)S(1)}, bf16[1024,256]{1,0:T(8,128)(2,1)S(1)}, u32[]{:S(2)}, u32[]{:S(2)}) collective-permute-start(bf16[1024,256]{1,0:T(8,128)(2,1)S(1)} %get-tuple-element.25.refs_7_), channel_id=1, source_target_pairs={{8,0},{12,4},{16,8},{20,12},{24,16},{28,20},{9,1},{13,5},{17,9},{2... | collective-permute-start | bytes 1572872 | tf_op jit(solution)/shard_map/ppermute | solution.py:365
  94.5 22.4 %collective-permute-start.27 = (bf16[1024,256]{1,0:T(8,128)(2,1)S(1)}, bf16[1024,256]{1,0:T(8,128)(2,1)}, u32[]{:S(2)}, u32[]{:S(2)}) collective-permute-start(bf16[1024,256]{1,0:T(8,128)(2,1)S(1)} %collective-permute-done.26.refs_6_), channel_id=1, source_target_pairs={{8,16},{12,20},{16,24},{20,28},{9,17},{13,21},{17,25},{21,29},{10,... | collective-permute-start | bytes 1572872 | tf_op jit(solution)/shard_map/ppermute | solution.py:362
  102.2 22.6 %collective-permute-start.30 = (bf16[1024,256]{1,0:T(8,128)(2,1)S(1)}, bf16[1024,256]{1,0:T(8,128)(2,1)}, u32[]{:S(2)}, u32[]{:S(2)}) collective-permute-start(bf16[1024,256]{1,0:T(8,128)(2,1)S(1)} %collective-permute-done.29.refs_8_), channel_id=1, source_target_pairs={{8,0},{12,4},{16,8},{20,12},{9,1},{13,5},{17,9},{21,13},{10,2},{14... | collective-permute-start | bytes 1572872 | tf_op jit(solution)/shard_map/ppermute | solution.py:365
  103.5 26.2 %collective-permute-start.34 = (bf16[1024,256]{1,0:T(8,128)(2,1)S(1)}, bf16[1024,256]{1,0:T(8,128)(2,1)S(1)}, u32[]{:S(2)}, u32[]{:S(2)}) collective-permute-start(bf16[1024,256]{1,0:T(8,128)(2,1)S(1)} %collective-permute-done.33.refs_6_), channel_id=1, source_target_pairs={{8,16},{12,20},{16,24},{20,28},{9,17},{13,21},{17,25},{21,29},{10,... | collective-permute-start | bytes 1572872 | tf_op jit(solution)/shard_map/ppermute | solution.py:362
  113.4 22.5 %collective-permute-start.37 = (bf16[1024,256]{1,0:T(8,128)(2,1)S(1)}, bf16[1024,256]{1,0:T(8,128)(2,1)S(1)}, u32[]{:S(2)}, u32[]{:S(2)}) collective-permute-start(bf16[1024,256]{1,0:T(8,128)(2,1)S(1)} %collective-permute-done.36.refs_8_), channel_id=1, source_target_pairs={{8,0},{12,4},{16,8},{20,12},{9,1},{13,5},{17,9},{21,13},{10,2},{14... | collective-permute-start | bytes 1572872 | tf_op jit(solution)/shard_map/ppermute | solution.py:365
  127.1 30.5 %collective-permute-start.16 = (bf16[512,1024]{1,0:T(8,128)(2,1)}, bf16[512,1024]{1,0:T(8,128)(2,1)}, u32[]{:S(2)}, u32[]{:S(2)}) collective-permute-start(bf16[512,1024]{1,0:T(8,128)(2,1)} %get-tuple-element.21), channel_id=1, source_target_pairs={{0,2},{1,3},{2,0},{3,1},{4,6},{5,7},{6,4},{7,5},{8,10},{9,11},{10,... | collective-permute-start | bytes 3145736 | tf_op jit(solution)/shard_map/ppermute | solution.py:356
  129.7 54.6 %collective-permute-start.20 = (bf16[1024,1024]{1,0:T(8,128)(2,1)}, bf16[1024,1024]{1,0:T(8,128)(2,1)}, u32[]{:S(2)}, u32[]{:S(2)}) collective-permute-start(bf16[1024,1024]{1,0:T(8,128)(2,1)} %constant_dynamic-update-slice_fusion.4.refs_0_), channel_id=1, source_target_pairs={{0,1},{1,0},{2,3},{3,2},{4,5},{5,4},{6,7},{7,6},{8,9},{9,8},{10,11... | collective-permute-start | bytes 6291464 | tf_op jit(solution)/shard_map/ppermute | solution.py:359
  136.7 49.1 %collective-permute-start.21 = (bf16[1024,1024]{1,0:T(8,128)(2,1)}, bf16[1024,1024]{1,0:T(8,128)(2,1)}, u32[]{:S(2)}, u32[]{:S(2)}) collective-permute-start(bf16[1024,1024]{1,0:T(8,128)(2,1)} %constant_dynamic-update-slice_fusion.6.refs_2_), channel_id=1, source_target_pairs={{0,1},{1,0},{2,3},{3,2},{4,5},{5,4},{6,7},{7,6},{8,9},{9,8},{10,11... | collective-permute-start | bytes 6291464 | tf_op jit(solution)/shard_map/ppermute | solution.py:359
  146.2 86.6 %collective-permute-start.2 = (bf16[1024,1024]{1,0:T(8,128)(2,1)S(1)}, bf16[1024,1024]{1,0:T(8,128)(2,1)}, u32[]{:S(2)}, u32[]{:S(2)}) collective-permute-start(bf16[1024,1024]{1,0:T(8,128)(2,1)S(1)} %get-tuple-element.36.refs_0_), channel_id=1, source_target_pairs={{0,1},{1,0},{2,3},{3,2},{4,5},{5,4},{6,7},{7,6},{8,9},{9,8},{10,11... | collective-permute-start | bytes 6291464 | tf_op jit(solution)/shard_map/ppermute | solution.py:359
  166.6 81.9 %collective-permute-start.17 = (bf16[1024,1024]{1,0:T(8,128)(2,1)}, bf16[1024,1024]{1,0:T(8,128)(2,1)}, u32[]{:S(2)}, u32[]{:S(2)}) collective-permute-start(bf16[1024,1024]{1,0:T(8,128)(2,1)} %constant_dynamic-update-slice_fusion.2.refs_2_), channel_id=1, source_target_pairs={{0,1},{1,0},{2,3},{3,2},{4,5},{5,4},{6,7},{7,6},{8,9},{9,8},{10,11... | collective-permute-start | bytes 6291464 | tf_op jit(solution)/shard_map/ppermute | solution.py:359
  183.6 37.5 %collective-permute-start.42 = (bf16[1024,128]{1,0:T(8,128)(2,1)}, bf16[1024,128]{1,0:T(8,128)(2,1)S(1)}, u32[]{:S(2)}, u32[]{:S(2)}) collective-permute-start(bf16[1024,128]{1,0:T(8,128)(2,1)} %copy-done.61), channel_id=1, source_target_pairs={{16,24},{20,28},{17,25},{21,29},{18,26},{22,30},{19,27},{23,31}} | collective-permute-start | bytes 786440 | tf_op jit(solution)/shard_map/ppermute | solution.py:362
  184.3 40.3 %collective-permute-start.45 = (bf16[1024,128]{1,0:T(8,128)(2,1)}, bf16[1024,128]{1,0:T(8,128)(2,1)S(1)}, u32[]{:S(2)}, u32[]{:S(2)}) collective-permute-start(bf16[1024,128]{1,0:T(8,128)(2,1)} %collective-permute-done.44.refs_9_), channel_id=1, source_target_pairs={{8,0},{12,4},{9,1},{13,5},{10,2},{14,6},{11,3},{15,7}} | collective-permute-start | bytes 786440 | tf_op jit(solution)/shard_map/ppermute | solution.py:365
  197.0 58.0 %collective-permute-start.25 = (f32[1024,256]{1,0:T(8,128)S(1)}, f32[1024,256]{1,0:T(8,128)S(1)}, u32[]{:S(2)}, u32[]{:S(2)}) collective-permute-start(f32[1024,256]{1,0:T(8,128)S(1)} %shard_map.109), channel_id=1, source_target_pairs={{0,4},{4,0},{8,12},{12,8},{16,20},{20,16},{24,28},{28,24},{1,5},{5... | collective-permute-start | bytes 3145736 | tf_op jit(solution)/shard_map/ppermute | solution.py:353
  237.9 38.7 %collective-permute-start.49 = (bf16[1024,128]{1,0:T(8,128)(2,1)}, bf16[1024,128]{1,0:T(8,128)(2,1)}, u32[]{:S(2)}, u32[]{:S(2)}) collective-permute-start(bf16[1024,128]{1,0:T(8,128)(2,1)} %collective-permute-done.48.refs_5_), channel_id=1, source_target_pairs={{16,24},{20,28},{17,25},{21,29},{18,26},{22,30},{19,27},{23,31}} | collective-permute-start | bytes 786440 | tf_op jit(solution)/shard_map/ppermute | solution.py:362
  247.2 29.4 %collective-permute-start.52 = (bf16[1024,128]{1,0:T(8,128)(2,1)}, bf16[1024,128]{1,0:T(8,128)(2,1)}, u32[]{:S(2)}, u32[]{:S(2)}) collective-permute-start(bf16[1024,128]{1,0:T(8,128)(2,1)} %collective-permute-done.51.refs_9_), channel_id=1, source_target_pairs={{8,0},{12,4},{9,1},{13,5},{10,2},{14,6},{11,3},{15,7}} | collective-permute-start | bytes 786440 | tf_op jit(solution)/shard_map/ppermute | solution.py:365
  270.9 43.8 %all-to-all-start.3 = ((bf16[8,256,128]{2,1,0:T(8,128)(2,1)}), bf16[8,256,128]{2,1,0:T(8,128)(2,1)}, u32[]{:S(2)}, u32[]{:S(2)}) async-start(bf16[8,256,128]{2,1,0:T(8,128)(2,1)} %copy-done.69), calls=%async_computation.3 | async-start | bytes 1048576 | tf_op jit(solution)/shard_map/all_to_all | solution.py:449
  287.5 34.1 %collective-permute-start.24 = (f32[1024,256]{1,0:T(8,128)}, f32[1024,256]{1,0:T(8,128)}, u32[]{:S(2)}, u32[]{:S(2)}) collective-permute-start(f32[1024,256]{1,0:T(8,128)} %shard_map.110), channel_id=1, source_target_pairs={{0,4},{4,0},{8,12},{12,8},{16,20},{20,16},{24,28},{28,24},{1,5},{5... | collective-permute-start | bytes 3145736 | tf_op jit(solution)/shard_map/ppermute | solution.py:353
  314.7 31.8 %all-to-all-start.4 = ((bf16[8,256,128]{2,1,0:T(8,128)(2,1)}), bf16[8,256,128]{2,1,0:T(8,128)(2,1)}, u32[]{:S(2)}, u32[]{:S(2)}) async-start(bf16[8,256,128]{2,1,0:T(8,128)(2,1)} %copy-done.70), calls=%async_computation.4 | async-start | bytes 1048576 | tf_op jit(solution)/shard_map/all_to_all | solution.py:449
  346.5 57.6 %all-to-all-start = ((bf16[8,256,256]{2,1,0:T(8,128)(2,1)}), bf16[8,256,256]{2,1,0:T(8,128)(2,1)}, u32[]{:S(2)}, u32[]{:S(2)}) async-start(bf16[8,256,256]{2,1,0:T(8,128)(2,1)} %copy-done.68), calls=%async_computation | async-start | bytes 2097152 | tf_op jit(solution)/shard_map/all_to_all | solution.py:449
  352.0 30.3 %collective-permute-start.32 = (f32[1024,256]{1,0:T(8,128)}, f32[1024,256]{1,0:T(8,128)S(1)}, u32[]{:S(2)}, u32[]{:S(2)}) collective-permute-start(f32[1024,256]{1,0:T(8,128)} %copy-done.58), channel_id=1, source_target_pairs={{0,4},{4,0},{8,12},{12,8},{16,20},{20,16},{24,28},{28,24},{1,5},{5... | collective-permute-start | bytes 3145736 | tf_op jit(solution)/shard_map/ppermute | solution.py:353
  404.1 61.2 %all-to-all-start.1 = ((bf16[8,256,256]{2,1,0:T(8,128)(2,1)}), bf16[8,256,256]{2,1,0:T(8,128)(2,1)}, u32[]{:S(2)}, u32[]{:S(2)}) async-start(bf16[8,256,256]{2,1,0:T(8,128)(2,1)} %copy-done.67), calls=%async_computation.1 | async-start | bytes 2097152 | tf_op jit(solution)/shard_map/all_to_all | solution.py:449
  408.6 33.4 %collective-permute-start.39 = (f32[1024,256]{1,0:T(8,128)}, f32[1024,256]{1,0:T(8,128)S(1)}, u32[]{:S(2)}, u32[]{:S(2)}) collective-permute-start(f32[1024,256]{1,0:T(8,128)} %copy-done.57), channel_id=1, source_target_pairs={{0,4},{4,0},{8,12},{12,8},{16,20},{20,16},{24,28},{28,24},{1,5},{5... | collective-permute-start | bytes 3145736 | tf_op jit(solution)/shard_map/ppermute | solution.py:353
  465.3 28.9 %all-to-all-start.2 = ((bf16[8,256,256]{2,1,0:T(8,128)(2,1)}), bf16[8,256,256]{2,1,0:T(8,128)(2,1)S(1)}, u32[]{:S(2)}, u32[]{:S(2)}) async-start(bf16[8,256,256]{2,1,0:T(8,128)(2,1)} %shard_map.121), calls=%async_computation.2 | async-start | bytes 2097152 | tf_op jit(solution)/shard_map/all_to_all | solution.py:449
  (120 other events, 1460.6 us)

commit v3 on v2

--- a/solution.py
+++ b/solution.py
@@ -138,81 +138,108 @@
     return outputs.reshape(row_count, heads_here * HD)
 
 
-def pick_weights(off_ref, w_refs, w_buf, sems):
+def start_pieces(pieces, buf, sems):
+    copies, first = [], 0
+    for n, piece in enumerate(pieces):
+        rows = piece.shape[0]
+        copies.append(pltpu.make_async_copy(piece, buf.at[pl.ds(first, rows)], sems.at[n]))
+        copies[-1].start()
+        first += rows
+    return copies
+
+
+def product_kernel(counts, ropes, off_ref, *refs):
+    refs = list(refs)
+    x_refs = [[refs.pop(0) for _ in range(n)] for n in counts[:4]]
+    w_refs = [refs.pop(0) for _ in range(7)]
+    part_refs = [refs.pop(0) for _ in range(counts[4])]
+    if ropes:
+        bias_ref, cos_ref, sin_ref = (refs.pop(0) for _ in range(3))
+        out_ref, x_buf, w_buf, x_sems, w_sems, total, part_buf, cos_buf, sin_buf, sems = refs
+    else:
+        out_ref, x_buf, w_buf, x_sems, w_sems = refs
+        total = out_ref
+    rows = x_buf.shape[1]
+    tile = min(256, rows)
+
+    copies = []
     for i in range(4):
-        for place in range(7):
-
-            @pl.when(off_ref[i] == place - 3)
-            def _(i=i, place=place):
-                pltpu.make_async_copy(w_refs[place], w_buf.at[i], sems.at[i]).start()
+        for spot in range(7):
+
+            @pl.when(off_ref[i] == spot - 3)
+            def _(i=i, spot=spot):
+                pltpu.make_async_copy(w_refs[spot], w_buf.at[i], w_sems.at[i]).start()
+
+        copies.append(start_pieces(x_refs[i], x_buf.at[i], x_sems.at[i]))
+    if ropes:
+        late = start_pieces(part_refs, part_buf, sems)
+        late.append(pltpu.make_async_copy(cos_ref, cos_buf, sems.at[2]))
+        late[-1].start()
+        late.append(pltpu.make_async_copy(sin_ref, sin_buf, sems.at[3]))
+        late[-1].start()
 
     for i in range(4):
-        pltpu.make_async_copy(w_refs[0], w_buf.at[i], sems.at[i]).wait()
-
-
-def product(x_refs, w_buf):
-    total = jnp.dot(x_refs[0][...], w_buf[0], preferred_element_type=jnp.float32)
-    for i in range(1, 4):
-        total += jnp.dot(x_refs[i][...], w_buf[i], preferred_element_type=jnp.float32)
-    return total
-
-
-def partial_kernel(off_ref, *refs):
-    x_refs, w_refs, (out_ref, w_buf, sems) = refs[:4], refs[4:11], refs[11:]
-
-    @pl.when(pl.program_id(0) == 0)
-    def _():
-        pick_weights(off_ref, w_refs, w_buf, sems)
-
-    out_ref[...] = product(x_refs, w_buf)
-
-
-def project_kernel(ropes, off_ref, *refs):
-    x_refs, w_refs = refs[:4], refs[4:11]
-    part_ref, bias_ref, cos_ref, sin_ref, out_ref, w_buf, sems = refs[11:]
-
-    @pl.when(pl.program_id(0) == 0)
-    def _():
-        pick_weights(off_ref, w_refs, w_buf, sems)
-
-    total = product(x_refs, w_buf) + part_ref[...] + bias_ref[...]
-    for c, rope in enumerate(ropes):
-        part = total[:, c * HD : (c + 1) * HD]
-        if rope:
-            part = part * cos_ref[...] + pltpu.roll(part, HD // 2, 1) * sin_ref[...]
-        out_ref[:, c * HD : (c + 1) * HD] = part.astype(out_ref.dtype)
+        pltpu.make_async_copy(w_refs[0], w_buf.at[i], w_sems.at[i]).wait()
+        for copy in copies[i]:
+            copy.wait()
+        if ropes and i == 3:
+            for copy in late:
+                copy.wait()
+
+        @pl.loop(0, rows // tile)
+        def _(r, i=i):
+            here = pl.ds(pl.multiple_of(r * tile, tile), tile)
+            term = jnp.dot(x_buf[i, here, :], w_buf[i], preferred_element_type=jnp.float32)
+            if i > 0:
+                term = total[here, :] + term
+            if not ropes or i < 3:
+                total[here, :] = term
+                return
+            term = term + part_buf[here, :] + bias_ref[...]
+            for c, rope in enumerate(ropes):
+                head = term[:, c * HD : (c + 1) * HD]
+                if rope:
+                    head = head * cos_buf[here, :] + pltpu.roll(head, HD // 2, 1) * sin_buf[here, :]
+                out_ref[here, c * HD : (c + 1) * HD] = head.astype(out_ref.dtype)
 
 
 def projection(off, x_blocks, places, finish=None):
-    rows, feats = x_blocks[0].shape
-    columns = places[0].shape[1]
-    tile = min(512, rows)
-    wide = pl.BlockSpec((tile, columns), lambda r, off: (r, 0))
-    in_specs = [pl.BlockSpec((tile, feats), lambda r, off: (r, 0))] * 4
-    in_specs += [pl.BlockSpec(memory_space=pl.ANY)] * 7
-    operands = [*x_blocks, *places]
-    body, out_type = partial_kernel, jnp.float32
-    if finish is not None:
-        ropes, *rest = finish
-        table = pl.BlockSpec((tile, HD), lambda r, off: (r, 0))
-        in_specs += [wide, pl.BlockSpec((1, columns), lambda r, off: (0, 0)), table, table]
-        operands += rest
-        body, out_type = functools.partial(project_kernel, ropes), jnp.bfloat16
-    grid_spec = pltpu.PrefetchScalarGridSpec(
-        num_scalar_prefetch=1,
-        grid=(rows // tile,),
-        in_specs=in_specs,
-        out_specs=wide,
-        scratch_shapes=[
-            pltpu.VMEM((4, feats, columns), jnp.bfloat16),
+    rows = sum(piece.shape[0] for piece in x_blocks[0])
+    feats, columns = places[0].shape
+    counts = [len(pieces) for pieces in x_blocks]
+    operands = [piece for pieces in x_blocks for piece in pieces] + list(places)
+    anywhere = pl.BlockSpec(memory_space=pl.ANY)
+    in_specs = [anywhere] * len(operands)
+    scratch = [
+        pltpu.VMEM((4, rows, feats), jnp.bfloat16),
+        pltpu.VMEM((4, feats, columns), jnp.bfloat16),
+        pltpu.SemaphoreType.DMA((4, 2)),
+        pltpu.SemaphoreType.DMA((4,)),
+    ]
+    ropes, out_type = None, jnp.float32
+    if finish is None:
+        counts.append(0)
+    else:
+        ropes, parts, bias, cosine, sine = finish
+        counts.append(len(parts))
+        operands += [*parts, bias, cosine, sine]
+        in_specs += [anywhere] * len(parts)
+        in_specs += [pl.BlockSpec(memory_space=pltpu.VMEM), anywhere, anywhere]
+        scratch += [
+            pltpu.VMEM((rows, columns), jnp.float32),
+            pltpu.VMEM((rows, columns), jnp.float32),
+            pltpu.VMEM((rows, HD), jnp.float32),
+            pltpu.VMEM((rows, HD), jnp.float32),
             pltpu.SemaphoreType.DMA((4,)),
-        ],
-    )
+        ]
+        out_type = jnp.bfloat16
     return pl.pallas_call(
-        body,
-        grid_spec=grid_spec,
+        functools.partial(product_kernel, tuple(counts), ropes),
+        in_specs=[pl.BlockSpec(memory_space=pltpu.SMEM)] + in_specs,
+        out_specs=pl.BlockSpec(memory_space=pltpu.VMEM),
+        scratch_shapes=scratch,
         out_shape=jax.ShapeDtypeStruct((rows, columns), out_type),
-        compiler_params=pltpu.CompilerParams(vmem_limit_bytes=32 * 2**20),
+        compiler_params=pltpu.CompilerParams(vmem_limit_bytes=56 * 2**20),
         cost_estimate=pl.CostEstimate(
             flops=8 * rows * feats * columns,
             bytes_accessed=8 * rows * feats + 8 * feats * columns + 4 * rows * columns,
@@ -221,65 +248,103 @@
     )(off, *operands)
 
 
-def attend_kernel(heads, slot, window, start_ref, len_ref, q_ref, k_ref, v_ref, out_ref):
-    which = pl.program_id(0)
-    rows = q_ref.shape[0]
-    start = start_ref[which]
-    first = pl.multiple_of(jnp.minimum((start // 16) * 16, rows - window), 16)
+def pick_rows(start, length, slot, window, ref):
+    first = pl.multiple_of(jnp.minimum((start // 16) * 16, ref.shape[0] - window), 16)
     row_at = lax.broadcasted_iota(jnp.int32, (slot, window), 0)
     col_at = lax.broadcasted_iota(jnp.int32, (slot, window), 1)
-    pick = jnp.where(
-        (col_at == row_at + (start - first)) & (row_at < len_ref[which]), 1.0, 0.0
-    ).astype(jnp.bfloat16)
-
-    def picked(ref, lanes):
-        rows_here = ref[pl.ds(first, window), lanes]
-        return jnp.dot(pick, rows_here, preferred_element_type=jnp.float32).astype(jnp.bfloat16)
-
-    key = picked(k_ref, pl.ds(0, HD))
-    value = picked(v_ref, pl.ds(0, HD))
-    causal = lax.broadcasted_iota(jnp.int32, (slot, slot), 1) <= lax.broadcasted_iota(
-        jnp.int32, (slot, slot), 0
-    )
-    for h in range(heads):
-        query = picked(q_ref, pl.ds(h * HD, HD))
-        scores = lax.dot_general(
-            query, key, (((1,), (1,)), ((), ())), preferred_element_type=jnp.float32
-        )
-        scores = jnp.where(causal, scores * HD ** (-0.5), mask_value)
-        peak = jnp.max(scores, axis=-1, keepdims=True)
-        raised = jnp.exp(scores - peak)
-        weights = (raised / jnp.sum(raised, axis=-1, keepdims=True)).astype(jnp.bfloat16)
-        context = jnp.dot(weights, value, preferred_element_type=jnp.float32)
-        out_ref[0, :, h * HD : (h + 1) * HD] = context.astype(out_ref.dtype)
-
-
-def attend(starts, lens, query, key, value, slot):
+    pick = jnp.where((col_at == row_at + (start - first)) & (row_at < length), 1.0, 0.0)
+    rows = jnp.dot(
+        pick.astype(jnp.bfloat16), ref[pl.ds(first, window), :], preferred_element_type=jnp.float32
+    )
+    return rows.astype(jnp.bfloat16)
+
+
+def slots_kernel(slot, window, start_ref, len_ref, in_ref, out_ref):
+    for s in range(out_ref.shape[0]):
+        out_ref[s] = pick_rows(start_ref[s], len_ref[s], slot, window, in_ref)
+
+
+def to_slots(starts, lens, array, slot, window):
+    count, columns = starts.shape[0], array.shape[1]
+    scalars = pl.BlockSpec(memory_space=pltpu.SMEM)
+    vmem = pl.BlockSpec(memory_space=pltpu.VMEM)
+    return pl.pallas_call(
+        functools.partial(slots_kernel, slot, window),
+        in_specs=[scalars, scalars, vmem],
+        out_specs=vmem,
+        out_shape=jax.ShapeDtypeStruct((count, slot, columns), jnp.bfloat16),
+        compiler_params=pltpu.CompilerParams(vmem_limit_bytes=56 * 2**20),
+        cost_estimate=pl.CostEstimate(
+            flops=2 * count * slot * window * columns,
+            bytes_accessed=2 * columns * (array.shape[0] + count * slot),
+            transcendentals=0,
+        ),
+    )(starts, lens, array)
+
+
+def attend_kernel(heads, window, start_ref, len_ref, q_ref, kv_ref, out_ref):
+    batch, slot = out_ref.shape[:2]
+    half = slot // 2
+    group = pl.program_id(0) * batch
+    for s in range(batch):
+        query = pick_rows(start_ref[group + s], len_ref[group + s], slot, window, q_ref)
+        for block in range(2):
+            width = (block + 1) * half
+            stacked = jnp.concatenate(
+                [
+                    query[block * half : width, h * HD : (h + 1) * HD]
+                    for h in range(heads)
+                ],
+                axis=0,
+            )
+            scores = lax.dot_general(
+                stacked,
+                kv_ref[s, :width, :HD],
+                (((1,), (1,)), ((), ())),
+                preferred_element_type=jnp.float32,
+            )
+            row_at = lax.broadcasted_iota(jnp.int32, scores.shape, 0) & (half - 1)
+            col_at = lax.broadcasted_iota(jnp.int32, scores.shape, 1)
+            scores = jnp.where(
+                col_at <= row_at + block * half, scores * HD ** (-0.5), mask_value
+            )
+            peak = jnp.max(scores, axis=-1, keepdims=True)
+            raised = jnp.exp(scores - peak)
+            weights = raised * (1.0 / jnp.sum(raised, axis=-1, keepdims=True))
+            context = jnp.dot(
+                weights.astype(jnp.bfloat16), kv_ref[s, :width, HD:], preferred_element_type=jnp.float32
+            ).astype(out_ref.dtype)
+            for h in range(heads):
+                out_ref[s, block * half : width, h * HD : (h + 1) * HD] = context[
+                    h * half : (h + 1) * half
+                ]
+
+
+def attend(starts, lens, query, kv_slots, window):
     rows, columns = query.shape
-    count = starts.shape[0]
-    window = min(rows, -(-(slot + 16) // 128) * 128)
+    count, slot = kv_slots.shape[:2]
+    batch = 2
     heads = columns // HD
     grid_spec = pltpu.PrefetchScalarGridSpec(
         num_scalar_prefetch=2,
-        grid=(count,),
+        grid=(count // batch,),
         in_specs=[
             pl.BlockSpec((rows, columns), lambda s, a, b: (0, 0)),
-            pl.BlockSpec((rows, HD), lambda s, a, b: (0, 0)),
-            pl.BlockSpec((rows, HD), lambda s, a, b: (0, 0)),
+            pl.BlockSpec((batch, slot, 2 * HD), lambda s, a, b: (s, 0, 0)),
         ],
-        out_specs=pl.BlockSpec((1, slot, columns), lambda s, a, b: (s, 0, 0)),
+        out_specs=pl.BlockSpec((batch, slot, columns), lambda s, a, b: (s, 0, 0)),
     )
     return pl.pallas_call(
-        functools.partial(attend_kernel, heads, slot, window),
+        functools.partial(attend_kernel, heads, window),
         grid_spec=grid_spec,
         out_shape=jax.ShapeDtypeStruct((count, slot, columns), jnp.bfloat16),
-        compiler_params=pltpu.CompilerParams(vmem_limit_bytes=32 * 2**20),
+        compiler_params=pltpu.CompilerParams(vmem_limit_bytes=56 * 2**20),
         cost_estimate=pl.CostEstimate(
             flops=2 * count * slot * (2 * slot + window) * columns,
-            bytes_accessed=2 * (rows * (columns + 2 * HD) + count * slot * columns),
+            bytes_accessed=2 * (rows * columns + 2 * count * slot * columns),
             transcendentals=count * heads * slot * slot,
         ),
-    )(starts, lens, query, key, value)
+    )(starts, lens, query, kv_slots)
 
 
 def place_kernel(count, slot, window, start_ref, len_ref, in_ref, out_ref, total):
@@ -314,7 +379,7 @@
         functools.partial(place_kernel, count, slot, window),
         grid_spec=grid_spec,
         out_shape=jax.ShapeDtypeStruct((learners, rows, columns), jnp.bfloat16),
-        compiler_params=pltpu.CompilerParams(vmem_limit_bytes=32 * 2**20),
+        compiler_params=pltpu.CompilerParams(vmem_limit_bytes=56 * 2**20),
         cost_estimate=pl.CostEstimate(
             flops=2 * learners * count * slot * window * columns,
             bytes_accessed=2 * learners * columns * (count * slot + rows),
@@ -379,14 +444,15 @@
         places.append(ups[:0:-1] + downs)
         marks.append(list(zip(ups[1:], downs[1:])))
 
-    widened = rollout_states.astype(jnp.float32)
+    states = after(rollout_states, *chunks[:2])
+    widened = states.astype(jnp.float32)
     squares = jnp.sum(widened * widened, axis=-1)
     squares = squares + swap_core(squares)
     squares = squares + swap_y(squares)
     scale = lax.rsqrt(squares[:, None] / (4 * feature_count) + norm_eps)
 
     def normed(first):
-        part = lax.dynamic_slice_in_dim(rollout_states, first, half, 1).astype(jnp.float32)
+        part = lax.dynamic_slice_in_dim(states, first, half, 1).astype(jnp.float32)
         gain = lax.dynamic_slice_in_dim(norm_gain, t * feature_count + first, half, 0)
         return (part * scale * gain[None, :]).astype(jnp.bfloat16)
 
@@ -396,13 +462,19 @@
     own_a = swap_y(own[:middle])
     near_b = swap_x(after(give[middle:], near_a, *marks[0][0]))
     diag_a = swap_y(after(near_a, own_a, *marks[0][0]))
-    near = jnp.concatenate([near_a, near_b], axis=0)
+    own_a_core = swap_core(after(own_a, near_a))
+    own_core = swap_core(own)
     diag_b = swap_y(after(near_b, diag_a, *marks[0][1]))
-    own_b = swap_y(after(own[middle:], diag_b, *marks[1][1]))
-    diag = jnp.concatenate([diag_a, diag_b], axis=0)
-    own_y = jnp.concatenate([own_a, own_b], axis=0)
-    own_x = [own, swap_core(own), own_y, swap_core(own_y)]
-    near_x = [near, swap_core(near), diag, swap_core(diag)]
+    near_a_core = swap_core(after(near_a, near_b, *marks[0][1]))
+    near_b_core = swap_core(after(near_b, diag_a, *marks[0][1]))
+    diag_a_core = swap_core(diag_a)
+    diag_b_core = swap_core(diag_b)
+    own_b = swap_y(after(own[middle:], diag_b, *marks[1][2]))
+    own_b_core = swap_core(own_b)
+    own_x = [[own], [own_core], [own_a, own_b], [own_a_core, own_b_core]]
+    near_ax = [[near_a], [near_a_core], [diag_a], [diag_a_core]]
+    near_bx = [[near_b], [near_b_core], [diag_b], [diag_b_core]]
+    near_x = [a + b for a, b in zip(near_ax, near_bx)]
     off = jnp.stack([(t ^ i) - z for i in range(4)]).astype(jnp.int32)
 
     lengths = seq_lengths.reshape(learners, learners)
@@ -429,26 +501,47 @@
     biases = [jnp.concatenate([b_key, b_value])]
     for low, high in zip(edges, edges[1:]):
         biases.append(b_query[low * HD : high * HD])
-    parts = []
-    for c, own_places in enumerate(places):
-        near_blocks = near_x
-        if parts:
-            near_blocks = [after(near_x[0], parts[-1])] + near_x[1:]
-        parts.append(projection(off, near_blocks, own_places))
-    columns = []
-    for c, own_places in enumerate(places):
-        ropes = (True, False) if c == 0 else (True,) * (own_places[0].shape[1] // HD)
-        got = swap_x(parts[c])
-        rot = projection(
-            off, own_x, own_places, (ropes, got, biases[c][None, :], cosine, sine)
-        )
-        if c == 0:
-            key, value = rot[:, :HD], rot[:, HD:]
-            continue
-        outgoing = attend(send_start, send_length, rot, key, value, slot)
-        incoming = lax.all_to_all(outgoing, "dp", split_axis=0, concat_axis=0, tiled=True)
-        placed = place(run_start, run_length, incoming[:, None], row_count)
-        columns.append(placed[0])
+    window = min(row_count, -(-(slot + 16) // 128) * 128)
+
+    def partial(c, blocks, *others):
+        return projection(after(off, *others), blocks, places[c])
+
+    def finish(c, got, *others):
+        ropes = (True, False) if c == 0 else (True,) * (places[c][0].shape[1] // HD)
+        ending = (ropes, got, biases[c][None, :], cosine, sine)
+        return projection(after(off, *others), own_x, places[c], ending)
+
+    def heads_of(c, got, *others):
+        rot = finish(c, got, *others)
+        return attend(send_start, send_length, rot, kv_slots, window)
+
+    def send(outgoing):
+        return lax.all_to_all(outgoing, "dp", split_axis=0, concat_axis=0, tiled=True)
+
+    def receive(incoming, *others):
+        return place(after(run_start, *others), run_length, incoming[:, None], row_count)[0]
+
+    part_a = partial(0, near_ax)
+    got_a = swap_x(part_a)
+    part_b = partial(0, near_bx, part_a, *marks[2][0])
+    got_b = swap_x(after(part_b, got_a))
+    parts = [None, partial(1, near_x, part_b)]
+    got = [None, swap_x(after(parts[1], got_b))]
+    kv = finish(0, [got_a, got_b], parts[1], *marks[2][1])
+    kv_slots = to_slots(send_start, send_length, kv, slot, window)
+    parts.append(partial(2, near_x, kv_slots))
+    out, incoming, columns = [None], [None], []
+    for c in range(1, len(places)):
+        if c + 1 < len(places):
+            got.append(swap_x(after(parts[c + 1], got[c])))
+        ties = marks[c + 2][1] if c + 2 < len(places) else ()
+        out.append(heads_of(c, [got[c]], parts[-1], *ties))
+        incoming.append(send(out[c]))
+        if c + 2 < len(places):
+            parts.append(partial(c + 2, near_x, out[c]))
+        if c >= 2:
+            columns.append(receive(incoming[c - 1], out[c]))
+    columns.append(receive(incoming[-1]))
     return jnp.concatenate(columns, axis=1)
 
 

time: 501 us -> 473 us (0.944)
  waiting for transfers between devices: 193 us -> 133 us
  Pallas kernels: 137 us -> 168 us
  local copies, waits for them, and re-layouts: 58.3 us -> 29 us
  blocking collectives: 0 us -> 23.6 us
    ppermute x8 -> x9, waiting for transfers between devices: 79.7 us -> 24.7 us  [swap_x(): return lax.ppermute(array, 'dp', [(i, i ^ 1) for i in range(learners)])]
    unnamed x194 -> x141, local copies, waits for them, and re-layouts: 48.9 us -> 18.3 us
    ppermute x18, waiting for transfers between devices: 8.07 us -> 35.2 us  [up(): lax.ppermute(array, 'dp', [(i, i + 2) for i in range(2 * first, learners...]
    pallas_call x17 -> x19, Pallas kernels: 127 us -> 153 us  [the longest x13 107 us: projection(): pl.pallas_call(functools.partial(product_kernel, tuple(counts), ropes), i...]
    all_to_all x0 -> x1, blocking collectives: none -> 23.6 us  [send(): lax.all_to_all(outgoing, 'dp', split_axis=0, concat_axis=0, tiled=True)]
    ppermute x18, waiting for transfers between devices: 88.6 us -> 69.3 us  [down(): lax.ppermute(array, 'dp', [(i, i - 2) for i in range(2, learners - 2 * fi...]
    all_to_all x5 -> x4, waiting for transfers between devices: 14.8 us -> 0.01 us  [send(): lax.all_to_all(outgoing, 'dp', split_axis=0, concat_axis=0, tiled=True)]
    pallas_call x5, Pallas kernels: 10 us -> 15.9 us  [place(): pl.pallas_call(functools.partial(place_kernel, count, slot, window), grid...]
  transfers between devices with their start and end apart: 59 -> 62, of which waited for: 21 -> 23; matrix products, arithmetic and copies ran while one was open for 5% -> 4% of each run, Pallas kernels for 27% -> 31%
where the time goes in v3:
time: 473 us; the launch traced here: 471 us
  Pallas kernels  168 us (36%)
  waiting for transfers between devices  133 us (28%)
  starting transfers between devices  101 us (21%)
  local copies, waits for them, and re-layouts  29 us (6%)
  blocking collectives  23.6 us (5%)
  other arithmetic  14.7 us (3%)
    pallas_call x13, Pallas kernels, projection(): pl.pallas_call(functools.partial(product_kernel, tuple(counts), ropes), i...  107 us
    ppermute x18, waiting for transfers between devices, down(): lax.ppermute(array, 'dp', [(i, i - 2) for i in range(2, learners - 2 * fi...  69.3 us
    pallas_call x5, Pallas kernels, attend(): pl.pallas_call(functools.partial(attend_kernel, heads, window), grid_spec...  43.2 us
    ppermute x18, waiting for transfers between devices, up(): lax.ppermute(array, 'dp', [(i, i + 2) for i in range(2 * first, learners...  35.2 us
    ppermute x18, starting transfers between devices, up(): lax.ppermute(array, 'dp', [(i, i + 2) for i in range(2 * first, learners...  30.2 us
    all_to_all x4, starting transfers between devices, send(): lax.all_to_all(outgoing, 'dp', split_axis=0, concat_axis=0, tiled=True)  25.1 us
    ppermute x9, waiting for transfers between devices, swap_x(): return lax.ppermute(array, 'dp', [(i, i ^ 1) for i in range(learners)])  24.7 us
    ppermute x18, starting transfers between devices, down(): lax.ppermute(array, 'dp', [(i, i - 2) for i in range(2, learners - 2 * fi...  23.7 us
  transfers between devices with their start and end apart: 62, of which 23 were waited for; matrix products, arithmetic and copies ran while one was open for 4% of the time, Pallas kernels for 31%

profile of v3, /device:TPU:0, one launch (start us, length us, event | category | flops | bytes accessed | tf_op | source)
XLA Modules:
  0.0 471.2 jit_solution(13051280852413500388)
XLA Ops:
  30.4 6.7 %collective-permute-done.3.refs_6_.refs_8_ = bf16[1024,256]{1,0:T(8,128)(2,1)S(1)} collective-permute-done((bf16[1024,256]{1,0:T(8,128)(2,1)}, bf16[1024,256]{1,0:T(8,128)(2,1)S(1)}, u32[]{:S(2)}, u32[]{:S(2)}) %collective-permute-start.3) | collective-permute-done | bytes 524320 | tf_op jit(solution)/shard_map/ppermute | solution.py:427
  51.9 12.8 %collective-permute-done.7.refs_9_.refs_11_ = bf16[1024,256]{1,0:T(8,128)(2,1)S(1)} collective-permute-done((bf16[1024,256]{1,0:T(8,128)(2,1)S(1)}, bf16[1024,256]{1,0:T(8,128)(2,1)S(1)}, u32[]{:S(2)}, u32[]{:S(2)}) %collective-permute-start.7) | collective-permute-done | bytes 524320 | tf_op jit(solution)/shard_map/ppermute | solution.py:430
  68.7 7.9 %collective-permute-done.23.refs_13_.refs_11_ = bf16[1024,256]{1,0:T(8,128)(2,1)S(1)} collective-permute-done((bf16[1024,256]{1,0:T(8,128)(2,1)S(1)}, bf16[1024,256]{1,0:T(8,128)(2,1)S(1)}, u32[]{:S(2)}, u32[]{:S(2)}) %collective-permute-start.23) | collective-permute-done | bytes 524320 | tf_op jit(solution)/shard_map/ppermute | solution.py:430
  77.9 8.5 %collective-permute-done.13.refs_10_.refs_12_ = bf16[1024,256]{1,0:T(8,128)(2,1)S(1)} collective-permute-done((bf16[1024,256]{1,0:T(8,128)(2,1)S(1)}, bf16[1024,256]{1,0:T(8,128)(2,1)S(1)}, u32[]{:S(2)}, u32[]{:S(2)}) %collective-permute-start.13) | collective-permute-done | bytes 524320 | tf_op jit(solution)/shard_map/ppermute | solution.py:430
  87.9 7.4 %collective-permute-done.24.refs_14_.refs_12_ = bf16[1024,256]{1,0:T(8,128)(2,1)S(1)} collective-permute-done((bf16[1024,256]{1,0:T(8,128)(2,1)S(1)}, bf16[1024,256]{1,0:T(8,128)(2,1)S(1)}, u32[]{:S(2)}, u32[]{:S(2)}) %collective-permute-start.24) | collective-permute-done | bytes 524320 | tf_op jit(solution)/shard_map/ppermute | solution.py:430
  104.9 5.9 %shard_map.109 = f32[512,256]{1,0:T(8,128)} custom-call(s32[4]{0:T(128)} %pad_add_fusion.off_ref, bf16[512,1024]{1,0:T(8,128)(2,1)} %collective-permute-done.2.refs_0_, bf16[512,1024]{1,0:T(8,128)(2,1)} %collective-permute-done.8.refs_1_.refs_2_, bf16[512,1024]{1,0:T(8,128)(2,1)} %copy-done.4, bf16[512,1024]{1,0:T(8,128)(2,1)} %copy-done.5, ...), custom_call_target="tpu_custom_call" | custom-call | flops 1073741824 | bytes 6815744 | tf_op jit(solution)/shard_map/pallas_call | solution.py:236
  110.8 9.6 %collective-permute-done.15.refs_12_.refs_10_ = bf16[1024,256]{1,0:T(8,128)(2,1)} collective-permute-done((bf16[1024,256]{1,0:T(8,128)(2,1)}, bf16[1024,256]{1,0:T(8,128)(2,1)}, u32[]{:S(2)}, u32[]{:S(2)}) %collective-permute-start.15) | collective-permute-done | bytes 524320 | tf_op jit(solution)/shard_map/ppermute | solution.py:430
  128.5 5.7 %shard_map.110 = f32[512,256]{1,0:T(8,128)} custom-call(s32[4]{0:T(128)} %pad_add_fusion.off_ref, bf16[512,1024]{1,0:T(8,128)(2,1)} %collective-permute-done.5.refs_0_.refs_1_, bf16[512,1024]{1,0:T(8,128)(2,1)} %collective-permute-done.16.refs_1_.refs_3_, bf16[512,1024]{1,0:T(8,128)(2,1)} %collective-permute-done.17.refs_2_.refs_5_, ...), custom_call_target="tpu_custom_call" | custom-call | flops 1073741824 | bytes 6815744 | tf_op jit(solution)/shard_map/pallas_call | solution.py:236
  148.5 8.7 %shard_map.111 = f32[1024,256]{1,0:T(8,128)} custom-call(s32[4]{0:T(128)} %pad_add_fusion.off_ref, bf16[512,1024]{1,0:T(8,128)(2,1)} %collective-permute-done.2.refs_0_, bf16[512,1024]{1,0:T(8,128)(2,1)} %collective-permute-done.5.refs_0_.refs_1_, bf16[512,1024]{1,0:T(8,128)(2,1)} %collective-permute-done.8.refs_1_.refs_2_, ...), custom_call_target="tpu_custom_call" | custom-call | flops 2147483648 | bytes 11534336 | tf_op jit(solution)/shard_map/pallas_call | solution.py:236
  168.7 9.0 %shard_map.112.in_ref = bf16[1024,256]{1,0:T(8,128)(2,1)} custom-call(s32[4]{0:T(128)} %pad_add_fusion.off_ref, bf16[1024,1024]{1,0:T(8,128)(2,1)} %copy-done, bf16[1024,1024]{1,0:T(8,128)(2,1)} %collective-permute-done.27.refs_1_, bf16[512,1024]{1,0:T(8,128)(2,1)} %copy-done.1, bf16[512,1024]{1,0:T(8,128)(2,1)} %collective-permute-done.28.refs_3_, ...), custom_call_target="tpu_custom_call" | custom-call | flops 2147483648 | bytes 11534336 | tf_op jit(solution)/shard_map/pallas_call | solution.py:236
  182.1 8.7 %shard_map.114 = f32[1024,256]{1,0:T(8,128)} custom-call(s32[4]{0:T(128)} %pad_add_fusion.off_ref, bf16[512,1024]{1,0:T(8,128)(2,1)} %collective-permute-done.2.refs_0_, bf16[512,1024]{1,0:T(8,128)(2,1)} %collective-permute-done.5.refs_0_.refs_1_, bf16[512,1024]{1,0:T(8,128)(2,1)} %collective-permute-done.8.refs_1_.refs_2_, ...), custom_call_target="tpu_custom_call" | custom-call | flops 2147483648 | bytes 11534336 | tf_op jit(solution)/shard_map/pallas_call | solution.py:236
  192.0 9.0 %shard_map.115.q_ref = bf16[1024,256]{1,0:T(8,128)(2,1)} custom-call(s32[4]{0:T(128)} %pad_add_fusion.off_ref, bf16[1024,1024]{1,0:T(8,128)(2,1)} %copy-done, bf16[1024,1024]{1,0:T(8,128)(2,1)} %collective-permute-done.27.refs_1_, bf16[512,1024]{1,0:T(8,128)(2,1)} %copy-done.1, bf16[512,1024]{1,0:T(8,128)(2,1)} %collective-permute-done.28.refs_3_, ...), custom_call_target="tpu_custom_call" | custom-call | flops 2147483648 | bytes 11534336 | tf_op jit(solution)/shard_map/pallas_call | solution.py:236
  201.0 9.8 %shard_map.116 = bf16[8,256,256]{2,1,0:T(8,128)(2,1)} custom-call(s32[8]{0:T(128)} %get-tuple-element.72.start_ref, s32[8]{0:T(128)} %get-tuple-element.71.len_ref, bf16[1024,256]{1,0:T(8,128)(2,1)} %shard_map.115.q_ref, bf16[8,256,256]{2,1,0:T(8,128)(2,1)} %shard_map.113.kv_ref), custom_call_target="tpu_custom_call" | custom-call | flops 939524096 | bytes 2621440 | tf_op jit(solution)/shard_map/pallas_call | solution.py:337
  210.8 10.4 %all-to-all-start = ((bf16[8,256,256]{2,1,0:T(8,128)(2,1)}), bf16[8,256,256]{2,1,0:T(8,128)(2,1)S(1)}, u32[]{:S(2)}, u32[]{:S(2)}) async-start(bf16[8,256,256]{2,1,0:T(8,128)(2,1)} %shard_map.116), calls=%async_computation | async-start | bytes 2097152 | tf_op jit(solution)/shard_map/all_to_all | solution.py:519
  232.3 8.8 %collective-permute-done.42.refs_10_.refs_8_ = bf16[1024,128]{1,0:T(8,128)(2,1)S(1)} collective-permute-done((bf16[1024,128]{1,0:T(8,128)(2,1)S(1)}, bf16[1024,128]{1,0:T(8,128)(2,1)S(1)}, u32[]{:S(2)}, u32[]{:S(2)}) %collective-permute-start.42) | collective-permute-done | bytes 262176 | tf_op jit(solution)/shard_map/ppermute | solution.py:427
  241.7 12.9 %collective-permute-done.44.refs_12_.refs_10_ = bf16[1024,128]{1,0:T(8,128)(2,1)S(1)} collective-permute-done((bf16[1024,128]{1,0:T(8,128)(2,1)S(1)}, bf16[1024,128]{1,0:T(8,128)(2,1)S(1)}, u32[]{:S(2)}, u32[]{:S(2)}) %collective-permute-start.44) | collective-permute-done | bytes 262176 | tf_op jit(solution)/shard_map/ppermute | solution.py:430
  257.6 8.7 %shard_map.117 = f32[1024,256]{1,0:T(8,128)} custom-call(s32[4]{0:T(128)} %pad_add_fusion.off_ref, bf16[512,1024]{1,0:T(8,128)(2,1)} %collective-permute-done.2.refs_0_, bf16[512,1024]{1,0:T(8,128)(2,1)} %collective-permute-done.5.refs_0_.refs_1_, bf16[512,1024]{1,0:T(8,128)(2,1)} %collective-permute-done.8.refs_1_.refs_2_, ...), custom_call_target="tpu_custom_call" | custom-call | flops 2147483648 | bytes 11534336 | tf_op jit(solution)/shard_map/pallas_call | solution.py:236
  267.3 9.0 %shard_map.118.q_ref = bf16[1024,256]{1,0:T(8,128)(2,1)} custom-call(s32[4]{0:T(128)} %pad_add_fusion.off_ref, bf16[1024,1024]{1,0:T(8,128)(2,1)} %copy-done, bf16[1024,1024]{1,0:T(8,128)(2,1)} %collective-permute-done.27.refs_1_, bf16[512,1024]{1,0:T(8,128)(2,1)} %copy-done.1, bf16[512,1024]{1,0:T(8,128)(2,1)} %collective-permute-done.28.refs_3_, ...), custom_call_target="tpu_custom_call" | custom-call | flops 2147483648 | bytes 11534336 | tf_op jit(solution)/shard_map/pallas_call | solution.py:236
  276.4 9.8 %shard_map.119 = bf16[8,256,256]{2,1,0:T(8,128)(2,1)} custom-call(s32[8]{0:T(128)} %get-tuple-element.72.start_ref, s32[8]{0:T(128)} %get-tuple-element.71.len_ref, bf16[1024,256]{1,0:T(8,128)(2,1)} %shard_map.118.q_ref, bf16[8,256,256]{2,1,0:T(8,128)(2,1)} %shard_map.113.kv_ref), custom_call_target="tpu_custom_call" | custom-call | flops 939524096 | bytes 2621440 | tf_op jit(solution)/shard_map/pallas_call | solution.py:337
  286.2 6.6 %all-to-all-start.1 = ((bf16[8,256,256]{2,1,0:T(8,128)(2,1)}), bf16[8,256,256]{2,1,0:T(8,128)(2,1)S(1)}, u32[]{:S(2)}, u32[]{:S(2)}) async-start(bf16[8,256,256]{2,1,0:T(8,128)(2,1)} %shard_map.119), calls=%async_computation.1 | async-start | bytes 2097152 | tf_op jit(solution)/shard_map/all_to_all | solution.py:519
  301.5 12.6 %collective-permute-done.49.refs_10_.refs_8_ = bf16[1024,128]{1,0:T(8,128)(2,1)S(1)} collective-permute-done((bf16[1024,128]{1,0:T(8,128)(2,1)S(1)}, bf16[1024,128]{1,0:T(8,128)(2,1)S(1)}, u32[]{:S(2)}, u32[]{:S(2)}) %collective-permute-start.49) | collective-permute-done | bytes 262176 | tf_op jit(solution)/shard_map/ppermute | solution.py:427
  317.0 4.9 %collective-permute-done.48.refs_14_.refs_12_ = bf16[1024,128]{1,0:T(8,128)(2,1)S(1)} collective-permute-done((bf16[1024,128]{1,0:T(8,128)(2,1)}, bf16[1024,128]{1,0:T(8,128)(2,1)S(1)}, u32[]{:S(2)}, u32[]{:S(2)}) %collective-permute-start.48) | collective-permute-done | bytes 262176 | tf_op jit(solution)/shard_map/ppermute | solution.py:430
  322.6 8.0 %shard_map.121 = f32[1024,128]{1,0:T(8,128)} custom-call(s32[4]{0:T(128)} %pad_add_fusion.off_ref, bf16[512,1024]{1,0:T(8,128)(2,1)} %collective-permute-done.2.refs_0_, bf16[512,1024]{1,0:T(8,128)(2,1)} %collective-permute-done.5.refs_0_.refs_1_, bf16[512,1024]{1,0:T(8,128)(2,1)} %collective-permute-done.8.refs_1_.refs_2_, ...), custom_call_target="tpu_custom_call" | custom-call | flops 1073741824 | bytes 9961472 | tf_op jit(solution)/shard_map/pallas_call | solution.py:236
  334.6 9.1 %shard_map.122.q_ref = bf16[1024,256]{1,0:T(8,128)(2,1)} custom-call(s32[4]{0:T(128)} %pad_add_fusion.off_ref, bf16[1024,1024]{1,0:T(8,128)(2,1)} %copy-done, bf16[1024,1024]{1,0:T(8,128)(2,1)} %collective-permute-done.27.refs_1_, bf16[512,1024]{1,0:T(8,128)(2,1)} %copy-done.1, bf16[512,1024]{1,0:T(8,128)(2,1)} %collective-permute-done.28.refs_3_, ...), custom_call_target="tpu_custom_call" | custom-call | flops 2147483648 | bytes 11534336 | tf_op jit(solution)/shard_map/pallas_call | solution.py:236
  343.7 9.7 %shard_map.123 = bf16[8,256,256]{2,1,0:T(8,128)(2,1)} custom-call(s32[8]{0:T(128)} %get-tuple-element.72.start_ref, s32[8]{0:T(128)} %get-tuple-element.71.len_ref, bf16[1024,256]{1,0:T(8,128)(2,1)} %shard_map.122.q_ref, bf16[8,256,256]{2,1,0:T(8,128)(2,1)} %shard_map.113.kv_ref), custom_call_target="tpu_custom_call" | custom-call | flops 939524096 | bytes 2621440 | tf_op jit(solution)/shard_map/pallas_call | solution.py:337
  354.8 8.0 %shard_map.125 = f32[1024,128]{1,0:T(8,128)} custom-call(s32[4]{0:T(128)} %pad_add_fusion.off_ref, bf16[512,1024]{1,0:T(8,128)(2,1)} %collective-permute-done.2.refs_0_, bf16[512,1024]{1,0:T(8,128)(2,1)} %collective-permute-done.5.refs_0_.refs_1_, bf16[512,1024]{1,0:T(8,128)(2,1)} %collective-permute-done.8.refs_1_.refs_2_, ...), custom_call_target="tpu_custom_call" | custom-call | flops 1073741824 | bytes 9961472 | tf_op jit(solution)/shard_map/pallas_call | solution.py:236
  363.6 8.4 %shard_map.126.q_ref = bf16[1024,128]{1,0:T(8,128)(2,1)} custom-call(s32[4]{0:T(128)} %pad_add_fusion.off_ref, bf16[1024,1024]{1,0:T(8,128)(2,1)} %copy-done, bf16[1024,1024]{1,0:T(8,128)(2,1)} %collective-permute-done.27.refs_1_, bf16[512,1024]{1,0:T(8,128)(2,1)} %copy-done.1, bf16[512,1024]{1,0:T(8,128)(2,1)} %collective-permute-done.28.refs_3_, ...), custom_call_target="tpu_custom_call" | custom-call | flops 1073741824 | bytes 9961472 | tf_op jit(solution)/shard_map/pallas_call | solution.py:236
  372.0 7.0 %shard_map.127 = bf16[8,256,128]{2,1,0:T(8,128)(2,1)} custom-call(s32[8]{0:T(128)} %get-tuple-element.72.start_ref, s32[8]{0:T(128)} %get-tuple-element.71.len_ref, bf16[1024,128]{1,0:T(8,128)(2,1)} %shard_map.126.q_ref, bf16[8,256,256]{2,1,0:T(8,128)(2,1)} %shard_map.113.kv_ref), custom_call_target="tpu_custom_call" | custom-call | flops 469762048 | bytes 1310720 | tf_op jit(solution)/shard_map/pallas_call | solution.py:337
  379.0 23.6 %all_to_all.25 = bf16[8,256,128]{2,1,0:T(8,128)(2,1)} all-to-all(bf16[8,256,128]{2,1,0:T(8,128)(2,1)} %shard_map.127), channel_id=1, replica_groups=mesh['dp'=8,'tensor'=4] {'dp'}, dimensions={0} | all-to-all | bytes 1048576 | tf_op jit(solution)/shard_map/all_to_all | solution.py:519
  411.3 18.8 %collective-permute-done.57.refs_13_ = f32[1024,128]{1,0:T(8,128)S(1)} collective-permute-done((f32[1024,128]{1,0:T(8,128)S(1)}, f32[1024,128]{1,0:T(8,128)S(1)}, u32[]{:S(2)}, u32[]{:S(2)}) %collective-permute-start.57) | collective-permute-done | bytes 524320 | tf_op jit(solution)/shard_map/ppermute | solution.py:418
  430.9 8.4 %shard_map.129.q_ref = bf16[1024,128]{1,0:T(8,128)(2,1)} custom-call(s32[4]{0:T(128)} %pad_add_fusion.off_ref, bf16[1024,1024]{1,0:T(8,128)(2,1)} %copy-done, bf16[1024,1024]{1,0:T(8,128)(2,1)} %collective-permute-done.27.refs_1_, bf16[512,1024]{1,0:T(8,128)(2,1)} %copy-done.1, bf16[512,1024]{1,0:T(8,128)(2,1)} %collective-permute-done.28.refs_3_, ...), custom_call_target="tpu_custom_call" | custom-call | flops 1073741824 | bytes 9961472 | tf_op jit(solution)/shard_map/pallas_call | solution.py:236
  439.3 7.0 %shard_map.130 = bf16[8,256,128]{2,1,0:T(8,128)(2,1)} custom-call(s32[8]{0:T(128)} %get-tuple-element.72.start_ref, s32[8]{0:T(128)} %get-tuple-element.71.len_ref, bf16[1024,128]{1,0:T(8,128)(2,1)} %shard_map.129.q_ref, bf16[8,256,256]{2,1,0:T(8,128)(2,1)} %shard_map.113.kv_ref), custom_call_target="tpu_custom_call" | custom-call | flops 469762048 | bytes 1310720 | tf_op jit(solution)/shard_map/pallas_call | solution.py:337
  (286 shorter events, 168.8 us)
Async XLA Ops:
  16.3 24.5 %collective-permute-start.2 = (bf16[512,1024]{1,0:T(8,128)(2,1)S(1)}, bf16[512,1024]{1,0:T(8,128)(2,1)}, u32[]{:S(2)}, u32[]{:S(2)}) collective-permute-start(bf16[512,1024]{1,0:T(8,128)(2,1)S(1)} %get-tuple-element.83), channel_id=1, source_target_pairs={{0,4},{4,0},{8,12},{12,8},{16,20},{20,16},{24,28},{28,24},{1,5},{5... | collective-permute-start | bytes 3145736 | tf_op jit(solution)/shard_map/ppermute | solution.py:418
  19.5 23.8 %collective-permute-start.9 = (bf16[512,1024]{1,0:T(8,128)(2,1)S(1)}, bf16[512,1024]{1,0:T(8,128)(2,1)S(1)}, u32[]{:S(2)}, u32[]{:S(2)}) collective-permute-start(bf16[512,1024]{1,0:T(8,128)(2,1)S(1)} %get-tuple-element.81), channel_id=1, source_target_pairs={{0,2},{1,3},{2,0},{3,1},{4,6},{5,7},{6,4},{7,5},{8,10},{9,11},{10,... | collective-permute-start | bytes 3145736 | tf_op jit(solution)/shard_map/ppermute | solution.py:421
  25.8 20.2 %collective-permute-start.19 = (bf16[1024,256]{1,0:T(8,128)(2,1)S(1)}, bf16[1024,256]{1,0:T(8,128)(2,1)S(1)}, u32[]{:S(2)}, u32[]{:S(2)}) collective-permute-start(bf16[1024,256]{1,0:T(8,128)(2,1)S(1)} %copy-done.14), channel_id=1, source_target_pairs={{0,8},{4,12},{8,16},{12,20},{16,24},{20,28},{1,9},{5,13},{9,17},{1... | collective-permute-start | bytes 1572872 | tf_op jit(solution)/shard_map/ppermute | solution.py:427
  43.3 23.4 %collective-permute-start.10 = (bf16[512,1024]{1,0:T(8,128)(2,1)}, bf16[512,1024]{1,0:T(8,128)(2,1)S(1)}, u32[]{:S(2)}, u32[]{:S(2)}) collective-permute-start(bf16[512,1024]{1,0:T(8,128)(2,1)} %collective-permute-done.2.refs_0_), channel_id=1, source_target_pairs={{0,2},{1,3},{2,0},{3,1},{4,6},{5,7},{6,4},{7,5},{8,10},{9,11},{10,... | collective-permute-start | bytes 3145736 | tf_op jit(solution)/shard_map/ppermute | solution.py:421
  44.8 22.7 %collective-permute-start.5 = (bf16[512,1024]{1,0:T(8,128)(2,1)S(1)}, bf16[512,1024]{1,0:T(8,128)(2,1)}, u32[]{:S(2)}, u32[]{:S(2)}) collective-permute-start(bf16[512,1024]{1,0:T(8,128)(2,1)S(1)} %get-tuple-element.38), channel_id=1, source_target_pairs={{0,4},{4,0},{8,12},{12,8},{16,20},{20,16},{24,28},{28,24},{1,5},{5... | collective-permute-start | bytes 3145736 | tf_op jit(solution)/shard_map/ppermute | solution.py:418
  50.6 26.0 %collective-permute-start.23 = (bf16[1024,256]{1,0:T(8,128)(2,1)S(1)}, bf16[1024,256]{1,0:T(8,128)(2,1)S(1)}, u32[]{:S(2)}, u32[]{:S(2)}) collective-permute-start(bf16[1024,256]{1,0:T(8,128)(2,1)S(1)} %collective-permute-done.22.refs_12_.refs_10_), channel_id=1, source_target_pairs={{8,0},{12,4},{16,8},{20,12},{9,1},{13,5},{17,9},{21,13},{10,2},{14... | collective-permute-start | bytes 1572872 | tf_op jit(solution)/shard_map/ppermute | solution.py:430
  65.4 20.9 %collective-permute-start.13 = (bf16[1024,256]{1,0:T(8,128)(2,1)S(1)}, bf16[1024,256]{1,0:T(8,128)(2,1)S(1)}, u32[]{:S(2)}, u32[]{:S(2)}) collective-permute-start(bf16[1024,256]{1,0:T(8,128)(2,1)S(1)} %collective-permute-done.7.refs_9_.refs_11_), channel_id=1, source_target_pairs={{8,0},{12,4},{9,1},{13,5},{10,2},{14,6},{11,3},{15,7}} | collective-permute-start | bytes 1572872 | tf_op jit(solution)/shard_map/ppermute | solution.py:430
  67.5 32.6 %collective-permute-start.17 = (bf16[512,1024]{1,0:T(8,128)(2,1)}, bf16[512,1024]{1,0:T(8,128)(2,1)}, u32[]{:S(2)}, u32[]{:S(2)}) collective-permute-start(bf16[512,1024]{1,0:T(8,128)(2,1)} %collective-permute-done.5.refs_0_.refs_1_), channel_id=1, source_target_pairs={{0,2},{1,3},{2,0},{3,1},{4,6},{5,7},{6,4},{7,5},{8,10},{9,11},{10,... | collective-permute-start | bytes 3145736 | tf_op jit(solution)/shard_map/ppermute | solution.py:421
  76.6 24.1 %collective-permute-start.11 = (bf16[512,1024]{1,0:T(8,128)(2,1)S(1)}, bf16[512,1024]{1,0:T(8,128)(2,1)S(1)}, u32[]{:S(2)}, u32[]{:S(2)}) collective-permute-start(bf16[512,1024]{1,0:T(8,128)(2,1)S(1)} %collective-permute-done.10.refs_2_.refs_4_), channel_id=1, source_target_pairs={{0,1},{1,0},{2,3},{3,2},{4,5},{5,4},{6,7},{7,6},{8,9},{9,8},{10,11... | collective-permute-start | bytes 3145736 | tf_op jit(solution)/shard_map/ppermute | solution.py:424
  95.2 62.0 %collective-permute-start.27 = (bf16[1024,1024]{1,0:T(8,128)(2,1)S(1)}, bf16[1024,1024]{1,0:T(8,128)(2,1)}, u32[]{:S(2)}, u32[]{:S(2)}) collective-permute-start(bf16[1024,1024]{1,0:T(8,128)(2,1)S(1)} %get-tuple-element.73.refs_0_), channel_id=1, source_target_pairs={{0,1},{1,0},{2,3},{3,2},{4,5},{5,4},{6,7},{7,6},{8,9},{9,8},{10,11... | collective-permute-start | bytes 6291464 | tf_op jit(solution)/shard_map/ppermute | solution.py:424
  100.1 22.3 %collective-permute-start.16 = (bf16[512,1024]{1,0:T(8,128)(2,1)}, bf16[512,1024]{1,0:T(8,128)(2,1)}, u32[]{:S(2)}, u32[]{:S(2)}) collective-permute-start(bf16[512,1024]{1,0:T(8,128)(2,1)} %collective-permute-done.5.refs_0_.refs_1_), channel_id=1, source_target_pairs={{0,1},{1,0},{2,3},{3,2},{4,5},{5,4},{6,7},{7,6},{8,9},{9,8},{10,11... | collective-permute-start | bytes 3145736 | tf_op jit(solution)/shard_map/ppermute | solution.py:424
  100.1 26.9 %collective-permute-start.18 = (bf16[512,1024]{1,0:T(8,128)(2,1)}, bf16[512,1024]{1,0:T(8,128)(2,1)}, u32[]{:S(2)}, u32[]{:S(2)}) collective-permute-start(bf16[512,1024]{1,0:T(8,128)(2,1)} %collective-permute-done.17.refs_2_.refs_5_), channel_id=1, source_target_pairs={{0,1},{1,0},{2,3},{3,2},{4,5},{5,4},{6,7},{7,6},{8,9},{9,8},{10,11... | collective-permute-start | bytes 3145736 | tf_op jit(solution)/shard_map/ppermute | solution.py:424
  103.3 34.0 %collective-permute-start.28 = (bf16[512,1024]{1,0:T(8,128)(2,1)}, bf16[512,1024]{1,0:T(8,128)(2,1)}, u32[]{:S(2)}, u32[]{:S(2)}) collective-permute-start(bf16[512,1024]{1,0:T(8,128)(2,1)} %get-tuple-element.46), channel_id=1, source_target_pairs={{0,2},{1,3},{2,0},{3,1},{4,6},{5,7},{6,4},{7,5},{8,10},{9,11},{10,... | collective-permute-start | bytes 3145736 | tf_op jit(solution)/shard_map/ppermute | solution.py:421
  137.3 28.6 %collective-permute-start.29 = (bf16[512,1024]{1,0:T(8,128)(2,1)S(1)}, bf16[512,1024]{1,0:T(8,128)(2,1)S(1)}, u32[]{:S(2)}, u32[]{:S(2)}) collective-permute-start(bf16[512,1024]{1,0:T(8,128)(2,1)S(1)} %collective-permute-done.9.refs_2_), channel_id=1, source_target_pairs={{0,1},{1,0},{2,3},{3,2},{4,5},{5,4},{6,7},{7,6},{8,9},{9,8},{10,11... | collective-permute-start | bytes 3145736 | tf_op jit(solution)/shard_map/ppermute | solution.py:424
  137.3 29.3 %collective-permute-start.30 = (bf16[512,1024]{1,0:T(8,128)(2,1)}, bf16[512,1024]{1,0:T(8,128)(2,1)S(1)}, u32[]{:S(2)}, u32[]{:S(2)}) collective-permute-start(bf16[512,1024]{1,0:T(8,128)(2,1)} %collective-permute-done.28.refs_3_), channel_id=1, source_target_pairs={{0,1},{1,0},{2,3},{3,2},{4,5},{5,4},{6,7},{7,6},{8,9},{9,8},{10,11... | collective-permute-start | bytes 3145736 | tf_op jit(solution)/shard_map/ppermute | solution.py:424
  157.2 33.6 %collective-permute-start.39 = (f32[1024,256]{1,0:T(8,128)}, f32[1024,256]{1,0:T(8,128)S(1)}, u32[]{:S(2)}, u32[]{:S(2)}) collective-permute-start(f32[1024,256]{1,0:T(8,128)} %shard_map.111), channel_id=1, source_target_pairs={{0,4},{4,0},{8,12},{12,8},{16,20},{20,16},{24,28},{28,24},{1,5},{5... | collective-permute-start | bytes 3145736 | tf_op jit(solution)/shard_map/ppermute | solution.py:418
  165.8 25.0 %collective-permute-start.36 = (bf16[1024,256]{1,0:T(8,128)(2,1)S(1)}, bf16[1024,256]{1,0:T(8,128)(2,1)S(1)}, u32[]{:S(2)}, u32[]{:S(2)}) collective-permute-start(bf16[1024,256]{1,0:T(8,128)(2,1)S(1)} %collective-permute-done.35.refs_10_.refs_8_), channel_id=1, source_target_pairs={{8,16},{12,20},{16,24},{20,28},{9,17},{13,21},{17,25},{21,29},{10,... | collective-permute-start | bytes 1572872 | tf_op jit(solution)/shard_map/ppermute | solution.py:427
  166.6 24.3 %collective-permute-start.38 = (bf16[1024,256]{1,0:T(8,128)(2,1)S(1)}, bf16[1024,256]{1,0:T(8,128)(2,1)S(1)}, u32[]{:S(2)}, u32[]{:S(2)}) collective-permute-start(bf16[1024,256]{1,0:T(8,128)(2,1)S(1)} %collective-permute-done.37.refs_12_.refs_10_), channel_id=1, source_target_pairs={{8,0},{12,4},{16,8},{20,12},{9,1},{13,5},{17,9},{21,13},{10,2},{14... | collective-permute-start | bytes 1572872 | tf_op jit(solution)/shard_map/ppermute | solution.py:430
  210.8 75.4 %all-to-all-start = ((bf16[8,256,256]{2,1,0:T(8,128)(2,1)}), bf16[8,256,256]{2,1,0:T(8,128)(2,1)S(1)}, u32[]{:S(2)}, u32[]{:S(2)}) async-start(bf16[8,256,256]{2,1,0:T(8,128)(2,1)} %shard_map.116), calls=%async_computation | async-start | bytes 2097152 | tf_op jit(solution)/shard_map/all_to_all | solution.py:519
  221.3 45.0 %collective-permute-start.46 = (f32[1024,256]{1,0:T(8,128)S(1)}, f32[1024,256]{1,0:T(8,128)S(1)}, u32[]{:S(2)}, u32[]{:S(2)}) collective-permute-start(f32[1024,256]{1,0:T(8,128)S(1)} %copy-done.41), channel_id=1, source_target_pairs={{0,4},{4,0},{8,12},{12,8},{16,20},{20,16},{24,28},{28,24},{1,5},{5... | collective-permute-start | bytes 3145736 | tf_op jit(solution)/shard_map/ppermute | solution.py:418
  223.3 32.6 %collective-permute-start.40 = (bf16[1024,256]{1,0:T(8,128)(2,1)S(1)}, bf16[1024,256]{1,0:T(8,128)(2,1)S(1)}, u32[]{:S(2)}, u32[]{:S(2)}) collective-permute-start(bf16[1024,256]{1,0:T(8,128)(2,1)S(1)} %collective-permute-done.36.refs_9_.refs_7_), channel_id=1, source_target_pairs={{16,24},{20,28},{17,25},{21,29},{18,26},{22,30},{19,27},{23,31}} | collective-permute-start | bytes 1572872 | tf_op jit(solution)/shard_map/ppermute | solution.py:427
  224.0 31.9 %collective-permute-start.41 = (bf16[1024,256]{1,0:T(8,128)(2,1)S(1)}, bf16[1024,256]{1,0:T(8,128)(2,1)S(1)}, u32[]{:S(2)}, u32[]{:S(2)}) collective-permute-start(bf16[1024,256]{1,0:T(8,128)(2,1)S(1)} %collective-permute-done.38.refs_13_.refs_11_), channel_id=1, source_target_pairs={{8,0},{12,4},{9,1},{13,5},{10,2},{14,6},{11,3},{15,7}} | collective-permute-start | bytes 1572872 | tf_op jit(solution)/shard_map/ppermute | solution.py:430
  231.0 23.6 %collective-permute-start.44 = (bf16[1024,128]{1,0:T(8,128)(2,1)S(1)}, bf16[1024,128]{1,0:T(8,128)(2,1)S(1)}, u32[]{:S(2)}, u32[]{:S(2)}) collective-permute-start(bf16[1024,128]{1,0:T(8,128)(2,1)S(1)} %get-tuple-element.54.refs_11_.refs_9_), channel_id=1, source_target_pairs={{8,0},{12,4},{16,8},{20,12},{24,16},{28,20},{9,1},{13,5},{17,9},{2... | collective-permute-start | bytes 786440 | tf_op jit(solution)/shard_map/ppermute | solution.py:430
  241.1 25.2 %collective-permute-start.43 = (bf16[1024,128]{1,0:T(8,128)(2,1)S(1)}, bf16[1024,128]{1,0:T(8,128)(2,1)S(1)}, u32[]{:S(2)}, u32[]{:S(2)}) collective-permute-start(bf16[1024,128]{1,0:T(8,128)(2,1)S(1)} %collective-permute-done.42.refs_10_.refs_8_), channel_id=1, source_target_pairs={{8,16},{12,20},{16,24},{20,28},{9,17},{13,21},{17,25},{21,29},{10,... | collective-permute-start | bytes 786440 | tf_op jit(solution)/shard_map/ppermute | solution.py:427
  286.2 92.8 %all-to-all-start.1 = ((bf16[8,256,256]{2,1,0:T(8,128)(2,1)}), bf16[8,256,256]{2,1,0:T(8,128)(2,1)S(1)}, u32[]{:S(2)}, u32[]{:S(2)}) async-start(bf16[8,256,256]{2,1,0:T(8,128)(2,1)} %shard_map.119), calls=%async_computation.1 | async-start | bytes 2097152 | tf_op jit(solution)/shard_map/all_to_all | solution.py:519
  292.8 37.8 %collective-permute-start.53 = (f32[1024,256]{1,0:T(8,128)S(1)}, f32[1024,256]{1,0:T(8,128)S(1)}, u32[]{:S(2)}, u32[]{:S(2)}) collective-permute-start(f32[1024,256]{1,0:T(8,128)S(1)} %copy-done.42), channel_id=1, source_target_pairs={{0,4},{4,0},{8,12},{12,8},{16,20},{20,16},{24,28},{28,24},{1,5},{5... | collective-permute-start | bytes 3145736 | tf_op jit(solution)/shard_map/ppermute | solution.py:418
  300.2 21.7 %collective-permute-start.48 = (bf16[1024,128]{1,0:T(8,128)(2,1)}, bf16[1024,128]{1,0:T(8,128)(2,1)S(1)}, u32[]{:S(2)}, u32[]{:S(2)}) collective-permute-start(bf16[1024,128]{1,0:T(8,128)(2,1)} %copy-done.48), channel_id=1, source_target_pairs={{8,0},{12,4},{9,1},{13,5},{10,2},{14,6},{11,3},{15,7}} | collective-permute-start | bytes 786440 | tf_op jit(solution)/shard_map/ppermute | solution.py:430
  330.6 32.2 %collective-permute-start.56 = (f32[1024,128]{1,0:T(8,128)}, f32[1024,128]{1,0:T(8,128)S(1)}, u32[]{:S(2)}, u32[]{:S(2)}) collective-permute-start(f32[1024,128]{1,0:T(8,128)} %shard_map.121), channel_id=1, source_target_pairs={{0,4},{4,0},{8,12},{12,8},{16,20},{20,16},{24,28},{28,24},{1,5},{5... | collective-permute-start | bytes 1572872 | tf_op jit(solution)/shard_map/ppermute | solution.py:418
  332.4 21.0 %collective-permute-start.54 = (bf16[1024,128]{1,0:T(8,128)(2,1)S(1)}, bf16[1024,128]{1,0:T(8,128)(2,1)S(1)}, u32[]{:S(2)}, u32[]{:S(2)}) collective-permute-start(bf16[1024,128]{1,0:T(8,128)(2,1)S(1)} %collective-permute-done.50.refs_9_.refs_7_), channel_id=1, source_target_pairs={{16,24},{20,28},{17,25},{21,29},{18,26},{22,30},{19,27},{23,31}} | collective-permute-start | bytes 786440 | tf_op jit(solution)/shard_map/ppermute | solution.py:427
  333.1 20.4 %collective-permute-start.55 = (bf16[1024,128]{1,0:T(8,128)(2,1)S(1)}, bf16[1024,128]{1,0:T(8,128)(2,1)S(1)}, u32[]{:S(2)}, u32[]{:S(2)}) collective-permute-start(bf16[1024,128]{1,0:T(8,128)(2,1)S(1)} %collective-permute-done.52.refs_13_.refs_11_), channel_id=1, source_target_pairs={{8,0},{12,4},{9,1},{13,5},{10,2},{14,6},{11,3},{15,7}} | collective-permute-start | bytes 786440 | tf_op jit(solution)/shard_map/ppermute | solution.py:430
  402.5 43.7 %all-to-all-start.2 = ((bf16[8,256,256]{2,1,0:T(8,128)(2,1)}), bf16[8,256,256]{2,1,0:T(8,128)(2,1)S(1)}, u32[]{:S(2)}, u32[]{:S(2)}) async-start(bf16[8,256,256]{2,1,0:T(8,128)(2,1)} %shard_map.123), calls=%async_computation.2 | async-start | bytes 2097152 | tf_op jit(solution)/shard_map/all_to_all | solution.py:519
  406.1 24.0 %collective-permute-start.57 = (f32[1024,128]{1,0:T(8,128)S(1)}, f32[1024,128]{1,0:T(8,128)S(1)}, u32[]{:S(2)}, u32[]{:S(2)}) collective-permute-start(f32[1024,128]{1,0:T(8,128)S(1)} %copy-done.61), channel_id=1, source_target_pairs={{0,4},{4,0},{8,12},{12,8},{16,20},{20,16},{24,28},{28,24},{1,5},{5... | collective-permute-start | bytes 1572872 | tf_op jit(solution)/shard_map/ppermute | solution.py:418
  (98 other events, 1895.1 us)
